TPU v7x, 128 devices: a whole 4x4x4 slice. The times are simulated.
128 devices in a mesh: seq: 32 (over y, x, core), song: 4 (over z).
Axes of the slice: x: 4, y: 4, z: 4, core: 2. Of those that a mesh axis runs over, the one named last changes fastest.
Arguments:
- spectrum: bfloat16 [4, 2048, 8196], P('song', 'seq'), may hold values from -6 to 6
- widths: int32 [32], replicated, may hold values from 4 to 257, as said below
- lengths: int32 [4], P('song'), may hold values from 1024 to 2048, as said below
- bin_gain: float32 [8196], replicated, may hold values from 0.5 to 2
- embed_weight: bfloat16 [8196, 384], replicated, may hold values from -0.375 to 0.375
- embed_bias: float32 [32, 384], replicated, may hold values from -3 to 3
- time_gain: float32 [384], replicated, may hold values from 0.5 to 2
- time_qkv: bfloat16 [384, 1536], replicated
- time_out: bfloat16 [512, 384], replicated, may hold values from -2 to 2
- band_gain: float32 [384], replicated, may hold values from 0.5 to 2
- band_qkv: bfloat16 [384, 1536], replicated
- band_out: bfloat16 [512, 384], replicated, may hold values from -1 to 1
- cotangent: bfloat16 [4, 2048, 32, 384], P('song', 'seq'), may hold values from -0.125 to 0.125
Outputs:
- features_out: bfloat16 [4, 2048, 32, 384], P('song', 'seq')
- out_grad: float32 [512, 384], replicated
Inputs may be any that keep to these rules, and one draw needn't show every extreme that they name: The widths sum to 2049, each is at least 4, one is exactly 257. Frames from lengths[s] on are padding; at least one song fills all 2048 frames.
All inputs are finite; a program needn't handle non-finite values.
Results may differ from a plain program's by a relative error of at most 0.024.
The roundings to bfloat16 on the way count: a program that leaves them out, or rounds other values in their place, can miss the bound.
Values may be sent and summed in bfloat16 or wider, within the bound.
A program may use at most 192 MiB of HBM per device.

v0:
```python
import jax
import jax.numpy as jnp
from jax import lax
from jax.sharding import PartitionSpec as P

WMAX = 257
HEADS = 8


FLOOR = 0.25
EPSILON = 1e-05


def rotate(values, position):
    half_dim = values.shape[-1] // 2
    frequency = jnp.exp(
        -(2.0 * jnp.arange(half_dim, dtype=jnp.float32) / values.shape[-1]) * jnp.log(10000.0)
    )
    angles = position[..., None, None] * frequency
    cosine = jnp.cos(angles)
    sines = jnp.sin(angles)
    leading = values[..., :half_dim]
    second = values[..., half_dim:]
    return jnp.concatenate(
        [leading * cosine - second * sines, second * cosine + leading * sines], axis=-1
    )


def norm_rows(inputs, gain):
    floats = inputs.astype(jnp.float32)
    square = jnp.mean(floats * floats, axis=-1, keepdims=True)
    return (floats * lax.rsqrt(square + EPSILON) * gain).astype(jnp.bfloat16)


def softmax_rows(scores):
    maximum = jnp.max(scores, axis=-1, keepdims=True)
    powers = jnp.exp(scores - maximum)
    return (powers / jnp.sum(powers, axis=-1, keepdims=True)).astype(jnp.bfloat16)


def per_device(
    spectrum,
    widths,
    lengths,
    bin_gain,
    embed_weight,
    embed_bias,
    time_gain,
    time_qkv,
    time_out,
    band_gain,
    band_qkv,
    band_out,
    cotangent,
):
    seq_count = lax.axis_size("seq")
    my_index = lax.axis_index("seq")
    local_frames = spectrum.shape[1]
    feature_count = spectrum.shape[2]
    bin_count = feature_count // 4
    band_count = widths.shape[0]
    model_width = embed_weight.shape[1]
    inner_width = time_out.shape[0]
    head_size = inner_width // HEADS
    attn_scale = head_size ** (-0.5)
    slice_width = WMAX * 4
    bands_each = -(-band_count // seq_count)
    slot_count = bands_each * seq_count
    extra_slots = slot_count - band_count
    frame_count = local_frames * seq_count
    starts = jnp.cumsum(widths) - widths
    slot_starts = jnp.concatenate([starts, jnp.full((extra_slots,), bin_count, jnp.int32)])
    slot_widths = jnp.concatenate([widths, jnp.zeros((extra_slots,), jnp.int32)])
    slot_bias = jnp.concatenate(
        [embed_bias, jnp.zeros((extra_slots, model_width), jnp.float32)], axis=0
    )
    weight_pad = jnp.concatenate(
        [embed_weight, jnp.zeros((slice_width, model_width), jnp.bfloat16)], axis=0
    )
    gain_pad = jnp.concatenate([bin_gain, jnp.zeros((slice_width,), jnp.float32)])
    column = jnp.arange(slice_width, dtype=jnp.int32)
    length = lengths[0]
    local_spec = spectrum[0]

    def embed_piece(source, offset, slot_id):
        band_piece = lax.dynamic_slice_in_dim(source, offset, slice_width, 1).astype(jnp.float32)
        entry_count = slot_widths[slot_id] * 4
        band_piece = jnp.where((column < entry_count)[None, :], band_piece, 0.0)
        mean_square = jnp.sum(band_piece * band_piece, axis=1, keepdims=True) / jnp.maximum(
            entry_count, 1
        ).astype(jnp.float32)
        band_scale = 1.0 / jnp.sqrt(jnp.maximum(mean_square, FLOOR))
        gain_slice = lax.dynamic_slice_in_dim(gain_pad, slot_starts[slot_id] * 4, slice_width, 0)
        normed = (band_piece * band_scale * gain_slice).astype(jnp.bfloat16)
        weight_rows = lax.dynamic_slice_in_dim(weight_pad, slot_starts[slot_id] * 4, slice_width, 0)
        summed = (
            jnp.dot(normed, weight_rows, preferred_element_type=jnp.float32) + slot_bias[slot_id]
        )
        return summed.astype(jnp.bfloat16)

    padded = jnp.concatenate(
        [local_spec, jnp.zeros((local_frames, slice_width), jnp.bfloat16)], axis=1
    )

    def local_band(slot_id):
        return embed_piece(padded, slot_starts[slot_id] * 4, slot_id)

    computed = lax.map(local_band, jnp.arange(band_count, dtype=jnp.int32))
    computed = jnp.concatenate(
        [computed, jnp.zeros((extra_slots, local_frames, model_width), jnp.bfloat16)], axis=0
    )
    owned = lax.all_to_all(computed, "seq", split_axis=0, concat_axis=1, tiled=True)
    block_rows = min(512, frame_count)
    block_count = frame_count // block_rows
    frame_pos = jnp.arange(frame_count, dtype=jnp.float32)
    key_live = jnp.arange(frame_count, dtype=jnp.int32) < length

    def time_pass(sequence):
        normal_rows = norm_rows(sequence, time_gain)
        project = jnp.dot(normal_rows, time_qkv, preferred_element_type=jnp.float32)
        queries = rotate(
            project[:, :inner_width].reshape(frame_count, HEADS, head_size), frame_pos
        ).astype(jnp.bfloat16)
        key_rows = rotate(
            project[:, inner_width : 2 * inner_width].reshape(frame_count, HEADS, head_size),
            frame_pos,
        ).astype(jnp.bfloat16)
        values_v = (
            project[:, 2 * inner_width :]
            .reshape(frame_count, HEADS, head_size)
            .astype(jnp.bfloat16)
        )

        def query_block(block_id):
            rows_q = lax.dynamic_slice_in_dim(queries, block_id * block_rows, block_rows, 0)
            scores = (
                jnp.einsum("qhd,khd->hqk", rows_q, key_rows, preferred_element_type=jnp.float32)
                * attn_scale
            )
            scores = jnp.where(key_live[None, None, :], scores, -1e30)
            weights = softmax_rows(scores)
            return jnp.einsum(
                "hqk,khd->qhd", weights, values_v, preferred_element_type=jnp.float32
            ).astype(jnp.bfloat16)

        head_out = lax.map(query_block, jnp.arange(block_count, dtype=jnp.int32)).reshape(
            frame_count, inner_width
        )
        mixed = sequence.astype(jnp.float32) + jnp.dot(
            head_out, time_out, preferred_element_type=jnp.float32
        )
        return mixed.astype(jnp.bfloat16)

    timed = lax.map(time_pass, owned)
    returned = lax.all_to_all(timed, "seq", split_axis=1, concat_axis=0, tiled=True)
    band_pos = jnp.arange(band_count, dtype=jnp.float32)[:, None]
    normal_rows = norm_rows(returned, band_gain)
    project = jnp.dot(
        normal_rows.reshape(-1, model_width), band_qkv, preferred_element_type=jnp.float32
    )
    project = project.reshape(band_count, local_frames, 3 * inner_width)
    queries = rotate(
        project[..., :inner_width].reshape(band_count, local_frames, HEADS, head_size), band_pos
    ).astype(jnp.bfloat16)
    key_rows = rotate(
        project[..., inner_width : 2 * inner_width].reshape(
            band_count, local_frames, HEADS, head_size
        ),
        band_pos,
    ).astype(jnp.bfloat16)
    values_v = (
        project[..., 2 * inner_width :]
        .reshape(band_count, local_frames, HEADS, head_size)
        .astype(jnp.bfloat16)
    )
    scores = (
        jnp.einsum("bthd,cthd->thbc", queries, key_rows, preferred_element_type=jnp.float32)
        * attn_scale
    )
    weights = softmax_rows(scores)
    head_out = jnp.einsum("thbc,cthd->bthd", weights, values_v, preferred_element_type=jnp.float32)
    head_out = head_out.astype(jnp.bfloat16).reshape(band_count, local_frames, inner_width)
    projected = jnp.dot(
        head_out.reshape(-1, inner_width), band_out, preferred_element_type=jnp.float32
    )
    output = (
        returned.astype(jnp.float32) + projected.reshape(band_count, local_frames, model_width)
    ).astype(jnp.bfloat16)
    live_frame = my_index * local_frames + jnp.arange(local_frames, dtype=jnp.int32) < length
    masked = jnp.where(live_frame[None, :, None], head_out, jnp.zeros_like(head_out))
    partial_grad = jnp.einsum(
        "bti,tbd->id", masked, cotangent[0], preferred_element_type=jnp.float32
    )
    gradient = lax.psum(partial_grad, ("seq", "song"))
    return (output.transpose(1, 0, 2)[None], gradient)


def solution(mesh):
    return jax.shard_map(
        per_device,
        mesh=mesh,
        in_specs=(
            P("song", "seq", None),
            P(),
            P("song"),
            P(),
            P(),
            P(),
            P(),
            P(),
            P(),
            P(),
            P(),
            P(),
            P("song", "seq", None, None),
        ),
        out_specs=(P("song", "seq", None, None), P()),
        check_vma=False,
    )
```

profile of v0, /device:TPU:1, one launch (start us, length us, event | category | flops | bytes accessed | tf_op | source)
XLA Modules:
  0.0 906.7 jit_solution(5389484238710741893)
XLA Ops:
  10.2 7.8 concatenate.29
  18.1 258.7 %while.29 = (s32[]{:T(128)}, bf16[32,64,384]{2,1,0:T(8,128)(2,1)}, s32[32]{0:T(128)S(1)}, s32[32]{0:T(128)S(1)}, s32[32]{0:T(128)S(1)}, /*index=5*/bf16[64,9224]...) while((s32[]{:T(128)}, bf16[32,64,384]{2,1,0:T(8,128)(2,1)}, ...), condition=%wide.region_3.4_spmd.clone, body=%wide.region_1.3_spmd.clone.sunk | while | flops 51170640 | bytes 1149533 | solution.py:108
  32.1 2.2 fusion.111
  40.2 2.2 fusion.111
  56.3 2.2 fusion.111
  64.4 2.2 fusion.111
  72.5 2.2 fusion.111
  80.6 2.2 fusion.111
  88.7 2.2 fusion.111
  96.7 2.2 fusion.111
  104.8 2.2 fusion.111
  112.9 2.2 fusion.111
  121.0 2.2 fusion.111
  129.1 2.2 fusion.111
  137.2 2.2 fusion.111
  153.3 2.2 fusion.111
  161.4 2.2 fusion.111
  169.5 2.2 fusion.111
  177.6 2.2 fusion.111
  193.8 2.2 fusion.111
  201.8 2.2 fusion.111
  209.9 2.2 fusion.111
  234.2 2.2 fusion.111
  242.3 2.2 fusion.111
  250.3 2.2 fusion.111
  258.4 2.2 fusion.111
  266.5 2.2 fusion.111
  276.8 8.7 all-to-all-start
  287.8 19.9 %all-to-all-done = bf16[32,64,384]{2,1,0:T(8,128)(2,1)S(1)} async-done(((bf16[32,64,384]{2,1,0:T(8,128)(2,1)}), bf16[32,64,384]{2,1,0:T(8,128)(2,1)S(1)}, u32[]{:S(2)}, u32[]{:S(2)}) %all-to-all-start) | async-done | bytes 1572896 | tf_op jit(solution)/shard_map/all_to_all | solution.py:112
  308.6 4.9 fusion.94
  316.3 2.5 subtract_convert_fusion.2
  318.7 2.5 pad_maximum_fusion
  321.3 134.1 %while.30 = (s32[]{:T(128)}, bf16[4,512,8,64]{1,3,2,0:T(8,128)(2,1)}, s32[4]{0:T(128)S(1)}, bf16[2048,8,64]{0,2,1:T(8,128)(2,1)}, bf16[2048,8,64]{0,2,1:T(8,128)...) while((s32[]{:T(128)}, ...), condition=%wide.region_8.9_spmd.clone, body=%wide.region_5.8_spmd.clone.sunk | while | flops 2198081536 | bytes 72388800 | solution.py:146
  323.3 16.9 %fusion.115 = (f32[8,512]{1,0:T(8,128)S(1)}, f32[8,512,2048]{2,1,0:T(8,128)}) fusion(pred[2048]{0:T(1024)(128)(4,1)S(1)} %iota_compare_fusion.5, bf16[2048,8,64]{0,2,1:T(8,128)(2,1)} %get-tuple-element.392, bf16[2048,8,64]{0,2,1:T(8,128)(2,1)} %get-tuple-element.391, s32[]{:T(128)S(6)} %select_n.64), kind=kOutput, calls=%fused_computation.106.clone.1 | convolution fusion | flops 1107298304 | bytes 36194308 | tf_op jit(solution)/shard_map/while/body/eval_jaxpr/while/body/eval_jaxpr/sub | solution.py:37
  340.2 14.7 %fusion.116 = bf16[4,512,8,64]{1,3,2,0:T(8,128)(2,1)} fusion(bf16[4,512,8,64]{1,3,2,0:T(8,128)(2,1)} %get-tuple-element.378, s32[]{:T(128)S(6)} %copy.82, bf16[2048,8,64]{0,2,1:T(8,128)(2,1)} %get-tuple-element.393, f32[8,512,2048]{2,1,0:T(8,128)} %get-tuple-element.322, f32[8,512]{1,0:T(8,128)S(1)} %get-tuple-element.323), kind=kOutput, calls=%fused_computation.14.clone.1 | convolution fusion | flops 1090781184 | bytes 36192260 | tf_op jit(solution)/shard_map/while/body/eval_jaxpr/while/body/eval_jaxpr/hqk,khd->qhd/dot_general | solution.py:142
  356.8 16.9 %fusion.115 = (f32[8,512]{1,0:T(8,128)S(1)}, f32[8,512,2048]{2,1,0:T(8,128)}) fusion(pred[2048]{0:T(1024)(128)(4,1)S(1)} %iota_compare_fusion.5, bf16[2048,8,64]{0,2,1:T(8,128)(2,1)} %get-tuple-element.392, bf16[2048,8,64]{0,2,1:T(8,128)(2,1)} %get-tuple-element.391, s32[]{:T(128)S(6)} %select_n.64), kind=kOutput, calls=%fused_computation.106.clone.1 | convolution fusion | flops 1107298304 | bytes 36194308 | tf_op jit(solution)/shard_map/while/body/eval_jaxpr/while/body/eval_jaxpr/sub | solution.py:37
  373.7 14.7 %fusion.116 = bf16[4,512,8,64]{1,3,2,0:T(8,128)(2,1)} fusion(bf16[4,512,8,64]{1,3,2,0:T(8,128)(2,1)} %get-tuple-element.378, s32[]{:T(128)S(6)} %copy.82, bf16[2048,8,64]{0,2,1:T(8,128)(2,1)} %get-tuple-element.393, f32[8,512,2048]{2,1,0:T(8,128)} %get-tuple-element.322, f32[8,512]{1,0:T(8,128)S(1)} %get-tuple-element.323), kind=kOutput, calls=%fused_computation.14.clone.1 | convolution fusion | flops 1090781184 | bytes 36192260 | tf_op jit(solution)/shard_map/while/body/eval_jaxpr/while/body/eval_jaxpr/hqk,khd->qhd/dot_general | solution.py:142
  390.3 16.9 %fusion.115 = (f32[8,512]{1,0:T(8,128)S(1)}, f32[8,512,2048]{2,1,0:T(8,128)}) fusion(pred[2048]{0:T(1024)(128)(4,1)S(1)} %iota_compare_fusion.5, bf16[2048,8,64]{0,2,1:T(8,128)(2,1)} %get-tuple-element.392, bf16[2048,8,64]{0,2,1:T(8,128)(2,1)} %get-tuple-element.391, s32[]{:T(128)S(6)} %select_n.64), kind=kOutput, calls=%fused_computation.106.clone.1 | convolution fusion | flops 1107298304 | bytes 36194308 | tf_op jit(solution)/shard_map/while/body/eval_jaxpr/while/body/eval_jaxpr/sub | solution.py:37
  407.2 14.7 %fusion.116 = bf16[4,512,8,64]{1,3,2,0:T(8,128)(2,1)} fusion(bf16[4,512,8,64]{1,3,2,0:T(8,128)(2,1)} %get-tuple-element.378, s32[]{:T(128)S(6)} %copy.82, bf16[2048,8,64]{0,2,1:T(8,128)(2,1)} %get-tuple-element.393, f32[8,512,2048]{2,1,0:T(8,128)} %get-tuple-element.322, f32[8,512]{1,0:T(8,128)S(1)} %get-tuple-element.323), kind=kOutput, calls=%fused_computation.14.clone.1 | convolution fusion | flops 1090781184 | bytes 36192260 | tf_op jit(solution)/shard_map/while/body/eval_jaxpr/while/body/eval_jaxpr/hqk,khd->qhd/dot_general | solution.py:142
  423.8 16.9 %fusion.115 = (f32[8,512]{1,0:T(8,128)S(1)}, f32[8,512,2048]{2,1,0:T(8,128)}) fusion(pred[2048]{0:T(1024)(128)(4,1)S(1)} %iota_compare_fusion.5, bf16[2048,8,64]{0,2,1:T(8,128)(2,1)} %get-tuple-element.392, bf16[2048,8,64]{0,2,1:T(8,128)(2,1)} %get-tuple-element.391, s32[]{:T(128)S(6)} %select_n.64), kind=kOutput, calls=%fused_computation.106.clone.1 | convolution fusion | flops 1107298304 | bytes 36194308 | tf_op jit(solution)/shard_map/while/body/eval_jaxpr/while/body/eval_jaxpr/sub | solution.py:37
  440.7 14.7 %fusion.116 = bf16[4,512,8,64]{1,3,2,0:T(8,128)(2,1)} fusion(bf16[4,512,8,64]{1,3,2,0:T(8,128)(2,1)} %get-tuple-element.378, s32[]{:T(128)S(6)} %copy.82, bf16[2048,8,64]{0,2,1:T(8,128)(2,1)} %get-tuple-element.393, f32[8,512,2048]{2,1,0:T(8,128)} %get-tuple-element.322, f32[8,512]{1,0:T(8,128)S(1)} %get-tuple-element.323), kind=kOutput, calls=%fused_computation.14.clone.1 | convolution fusion | flops 1090781184 | bytes 36192260 | tf_op jit(solution)/shard_map/while/body/eval_jaxpr/while/body/eval_jaxpr/hqk,khd->qhd/dot_general | solution.py:142
  455.4 3.4 copy.36
  460.7 28.8 %copy.71 = bf16[1,2048,384]{2,0,1:T(2,128)(2,1)} copy(bf16[1,2048,384]{2,1,0:T(8,128)(2,1)S(1)} %fusion.60) | data formatting | bytes 3145728 | tf_op jit(solution)/shard_map/while/body/jit(dynamic_update_index_in_dim)/broadcast_in_dim | solution.py:154
  490.0 34.3 %reduce.8 = bf16[2048,384]{1,0:T(8,128)(2,1)S(1)} reduce(bf16[2048,1,384]{2,1,0:T(2,128)(2,1)} %bitcast.92, bf16[]{:T(256)} %broadcast.188), dimensions={1}, to_apply=%bitcast.68.reduce_sub_computation | reduce | bytes 3145730
  525.7 5.6 all-to-all-start.1
  532.1 21.5 %all-to-all-done.1 = bf16[32,2,12288]{2,1,0:T(2,128)(2,1)S(1)} async-done(((bf16[32,2,12288]{2,1,0:T(2,128)(2,1)}), bf16[32,2,12288]{2,1,0:T(2,128)(2,1)S(1)}, u32[]{:S(2)}, u32[]{:S(2)}) %all-to-all-start.1) | async-done | bytes 1572896 | tf_op jit(solution)/shard_map/all_to_all | solution.py:155
  553.6 4.1 reshape.266
  557.7 46.8 %multiply_reduce_fusion.2 = f32[2048]{0:T(1024)S(1)} fusion(bf16[2048,1,384]{2,1,0:T(2,128)(2,1)} %reshape.266), kind=kLoop, calls=%fused_computation.73 | loop fusion | flops 2357248 | bytes 1581056 | tf_op jit(solution)/shard_map/reduce_sum | solution.py:31
  606.8 3.5 fusion.64
  611.9 4.2 fusion.89
  616.2 6.2 convert_element_type.95
  622.4 7.0 reshape.257
  629.4 7.0 reshape.256
  636.4 13.0 %fusion.92 = (f32[32,64,8,32]{3,2,1,0:T(8,128)}, f32[32,64,8,32]{3,2,1,0:T(8,128)}) fusion(f32[32,64,8,64]{3,2,1,0:T(8,128)} %reshape.256), kind=kLoop, calls=%fused_computation.110 | loop fusion | bytes 8388608 | tf_op jit(solution)/shard_map/slice | solution.py:22
  649.4 7.3 fusion.91
  656.7 44.4 %subtract_convert_fusion = (bf16[32,64,8,32]{3,0,2,1:T(8,128)(2,1)}, bf16[32,64,8,32]{3,0,2,1:T(8,128)(2,1)}, bf16[32,64,8,32]{3,0,2,1:T(8,128)(2,1)}, bf16[32,64,8,32]{3,0,2,1:T(8,128)(2,1)}) fusion(f32[32,64,8,32]{3,2,1,0:T(8,128)} %get-tuple-element.203, f32[32,64,8,32]{3,2,1,0:T(8,128)} %get-tuple-element.202, f32[32,32]{1,0:T(8,128)S(1)} %get-tuple-element.215, ...), kind=kLoop, calls=%fused_computation.45 | loop fusion | flops 8388608 | bytes 12591104 | tf_op jit(solution)/shard_map/convert.2
  701.1 13.5 %fusion.44 = f32[64,8,32,32]{2,3,1,0:T(8,128)} fusion(bf16[32,64,8,32]{3,0,2,1:T(8,128)(2,1)} %get-tuple-element.212, bf16[32,64,8,32]{3,0,2,1:T(8,128)(2,1)} %get-tuple-element.213, bf16[32,64,8,32]{3,0,2,1:T(8,128)(2,1)} %get-tuple-element.195, bf16[32,64,8,32]{3,0,2,1:T(8,128)(2,1)} %get-tuple-element.194), kind=kOutput, calls=%fused_computation.53 | convolution fusion | flops 75497472 | bytes 6291456 | tf_op jit(solution)/shard_map/bthd,cthd->thbc/dot_general | solution.py:177
  714.6 11.7 %fusion.93 = (f32[64,8,32]{2,1,0:T(8,128)S(1)}, f32[64,8,32,32]{2,3,1,0:T(8,128)}) fusion(f32[64,8,32,32]{2,3,1,0:T(8,128)} %fusion.44), kind=kOutput, calls=%fused_computation.111 | output fusion | flops 2097183 | bytes 4259840 | tf_op jit(solution)/shard_map/sub | solution.py:37
  726.3 9.1 %convert_bitcast_fusion = bf16[32,64,8,64]{3,0,2,1:T(8,128)(2,1)} fusion(f32[64,8,32,32]{2,3,1,0:T(8,128)} %get-tuple-element.219, f32[64,8,32]{2,1,0:T(8,128)S(1)} %get-tuple-element.218, bf16[32,64,8,64]{3,2,1,0:T(8,128)(2,1)S(1)} %copy-done.5), kind=kOutput, calls=%fused_computation.61 | convolution fusion | flops 69206016 | bytes 6356992 | tf_op jit(solution)/shard_map/thbc,cthd->bthd/dot_general | solution.py:181
  735.4 6.0 copy.44
  741.4 6.5 dot_general.39
  747.8 4.0 fusion.69
  751.8 3.8 fusion.68
  757.7 139.9 %all-reduce.5.cloned.1.call-done = f32[512,384]{1,0:T(8,128)} async-done(((f32[512,384]{1,0:T(8,128)}), f32[512,384]{1,0:T(8,128)}) %all-reduce.5.cloned.1.call-update) | async-done | bytes 786448 | tf_op jit(solution)/shard_map/psum | solution.py:194
  (333 shorter events, 132.8 us)
Async XLA Ops:
  7.2 740.6 %copy-start = (bf16[1,64,32,384]{3,2,1,0:T(8,128)(2,1)S(1)}, bf16[1,64,32,384]{3,2,1,0:T(8,128)(2,1)}, u32[]{:S(2)}) copy-start(bf16[1,64,32,384]{3,2,1,0:T(8,128)(2,1)} %param.29) | copy-start | bytes 4718596
  10.2 7.8 copy-start.8
  10.2 7.9 copy-start.13
  276.8 31.4 %copy-start.12 = (f32[384]{0:T(512)S(1)}, f32[384]{0:T(512)}, u32[]{:S(2)}) copy-start(f32[384]{0:T(512)} %param.23) | copy-start | bytes 4612
  276.8 30.9 %all-to-all-start = ((bf16[32,64,384]{2,1,0:T(8,128)(2,1)}), bf16[32,64,384]{2,1,0:T(8,128)(2,1)S(1)}, u32[]{:S(2)}, u32[]{:S(2)}) async-start(bf16[32,64,384]{2,1,0:T(8,128)(2,1)} %get-tuple-element.115), calls=%async_computation | async-start | bytes 3145728 | tf_op jit(solution)/shard_map/all_to_all | solution.py:112
  285.5 0.5 copy-start.10
  307.7 5.8 copy-start.3
  455.4 4.0 copy-start.4
  455.4 4.0 copy-start.14
  524.4 7.7 copy-start.11
  525.7 27.9 %all-to-all-start.1 = ((bf16[32,2,12288]{2,1,0:T(2,128)(2,1)}), bf16[32,2,12288]{2,1,0:T(2,128)(2,1)S(1)}, u32[]{:S(2)}, u32[]{:S(2)}) async-start(bf16[32,2,12288]{2,1,0:T(2,128)(2,1)} %reshape.265), calls=%async_computation.1 | async-start | bytes 3145728 | tf_op jit(solution)/shard_map/all_to_all | solution.py:155
  531.3 366.3 %all-reduce.5.cloned.1.call-start = ((), (), s32[]{:S(2)}) async-start(), calls=%async_computation.2 | async-start | bytes 1572864 | tf_op jit(solution)/shard_map/psum | solution.py:194
  557.7 49.0 %copy-start.6 = (bf16[384,1536]{1,0:T(8,128)(2,1)S(1)}, bf16[384,1536]{1,0:T(8,128)(2,1)}, u32[]{:S(2)}) copy-start(bf16[384,1536]{1,0:T(8,128)(2,1)} %param.27) | copy-start | bytes 3538948
  557.7 49.0 %copy-start.9 = (f32[384]{0:T(512)S(1)}, f32[384]{0:T(512)}, u32[]{:S(2)}) copy-start(f32[384]{0:T(512)} %param.26) | copy-start | bytes 4612
  606.7 3.5 copy-start.2
  636.4 13.0 %copy-start.1 = (f32[32,64,8,64]{3,2,1,0:T(8,128)S(1)}, f32[32,64,8,64]{3,2,1,0:T(8,128)}, u32[]{:S(2)}) copy-start(f32[32,64,8,64]{3,2,1,0:T(8,128)} %reshape.257) | copy-start | bytes 12582916
  714.6 11.7 %copy-start.5 = (bf16[32,64,8,64]{3,2,1,0:T(8,128)(2,1)S(1)}, bf16[32,64,8,64]{3,2,1,0:T(8,128)(2,1)}, u32[]{:S(2)}) copy-start(bf16[32,64,8,64]{3,2,1,0:T(8,128)(2,1)} %convert_element_type.95) | copy-start | bytes 6291460
  747.8 4.0 copy-start.7
Sparse Core Ops, SparseCore 0:
  751.9 145.6 all-reduce.4
where the time goes:
time: 919 us; the launch traced here: 907 us
  matrix products  236 us (26%)
  local copies, waits for them, and re-layouts  204 us (22%)
  waiting for transfers between devices  181 us (20%)
  other arithmetic  156 us (17%)
  loops' own time  100 us (11%)
  between operations  15.2 us (2%)
  starting transfers between devices  14.4 us (2%)
    psum x1, waiting for transfers between devices, per_device(): gradient = lax.psum(partial_grad, ('seq', 'song'))  140 us
    another operation x1, loops' own time, per_device(): computed = lax.map(local_band, jnp.arange(band_count, dtype=jnp.int32))  97.5 us
    dot_general x32, matrix products, embed_piece(): jnp.dot(normed, weight_rows, preferred_element_type=jnp.float32)  69.5 us
    sub x4, matrix products, softmax_rows(): powers = jnp.exp(scores - maximum)  67.6 us
    dot_general x4, matrix products, query_block(): jnp.einsum('hqk,khd->qhd', weights, values_v, preferred_element_type=jnp....  58.8 us
    reduce_sum x2, other arithmetic, norm_rows(): square = jnp.mean(floats * floats, axis=-1, keepdims=True)  47.2 us
    another operation x5, other arithmetic  47 us
    unnamed x1, other arithmetic  34.3 us
  transfers between devices with their start and end apart: 3, of which 3 were waited for; matrix products, arithmetic and copies ran while one was open for 1% of the time, Pallas kernels for 0%

commit v1 on v0

v1 whole, which is shorter than its diff:
```python
import functools

import jax
import jax.numpy as jnp
import numpy as np
from jax import lax
from jax.experimental import pallas as pl
from jax.experimental.pallas import tpu as pltpu
from jax.sharding import PartitionSpec as P

HEADS = 8
DH = 64
HALF = DH // 2
GROUP = 4 * DH
FLOOR = 0.25
EPSILON = 1e-05
LOG2E = 1.4426950408889634
WINDOW = 1152
NT = (((1,), (1,)), ((), ()))
TN = (((0,), (0,)), ((), ()))
MESH = pl.DeviceIdType.MESH
BF = jnp.bfloat16
F32 = jnp.float32
SAFE = 60.0
VSAFE = 2.0**40
VMEM = pltpu.VMEM
LIMIT = 56 * 2**20


def whole():
    return pl.BlockSpec(memory_space=pltpu.VMEM)


def smem():
    return pl.BlockSpec(memory_space=pltpu.SMEM)


def rotary_tables(positions, repeat):
    frequency = np.exp(-(2.0 * np.arange(HALF, dtype=np.float64) / DH) * np.log(10000.0))
    angles = positions.astype(np.float64)[:, None] * frequency
    cosine = np.tile(np.cos(angles), (1, repeat)).astype(np.float32)
    sines = np.tile(np.sin(angles), (1, repeat)).astype(np.float32)
    return cosine, sines


def split_halves(weights):
    row = lax.broadcasted_iota(jnp.int32, (GROUP, GROUP), 0)
    col = lax.broadcasted_iota(jnp.int32, (GROUP, GROUP), 1)
    source = (col % 128) // HALF * DH + col // 128 * HALF + col % HALF
    one_hot = (row == source).astype(F32).astype(BF)
    return jnp.dot(weights, one_hot, preferred_element_type=F32).astype(BF)


def rms_norm(rows, gain):
    square = jnp.mean(rows * rows, axis=-1, keepdims=True)
    return (rows * lax.rsqrt(square + EPSILON) * gain).astype(BF)


def rope(values, cosine, sines):
    leading = values[:, :128]
    second = values[:, 128:]
    return leading * cosine - second * sines, second * cosine + leading * sines


def embed_kernel(bands, limit, meta_ref, x_ref, gain_ref, w_ref, xt_ref, gt_ref, wt_ref, bias_ref, out_ref):
    lane = lax.broadcasted_iota(jnp.int32, (1, WINDOW), 1)

    def band(k, last):
        first = meta_ref[0, k]
        end = meta_ref[1, k]
        begin = pl.multiple_of(meta_ref[2, k] * 128, 128)
        window = pl.ds(begin, WINDOW)
        entry = lane + begin
        piece = x_ref[:, window].astype(F32)
        piece = jnp.where((entry >= first) & (entry < end), piece, 0.0)
        total = jnp.sum(piece * piece, axis=1, keepdims=True)
        if last:
            tail = xt_ref[...].astype(F32)
            total = total + jnp.sum(tail * tail, axis=1, keepdims=True)
        mean = total / (end - first + (limit - first - (end - first) if last else 0)).astype(F32)
        scale = 1.0 / jnp.sqrt(jnp.maximum(mean, FLOOR))
        normed = (piece * scale * gain_ref[:, window]).astype(BF)
        summed = jnp.dot(normed, w_ref[window, :], preferred_element_type=F32)
        if last:
            normed = (tail * scale * gt_ref[...]).astype(BF)
            summed = summed + jnp.dot(normed, wt_ref[...], preferred_element_type=F32)
        out_ref[k] = (summed + bias_ref[pl.ds(k, 1), :]).astype(BF)

    def step(i, carry):
        for j in range(4):
            band(i * 4 + j, False)
        return carry

    lax.fori_loop(0, bands // 4 - 1, step, 0)
    for k in range(bands - 4, bands - 1):
        band(k, False)
    band(bands - 1, True)


def embed(spectrum, widths, bin_gain, embed_weight, embed_bias):
    frames, feature_count = spectrum.shape
    bands, width = embed_bias.shape
    main = feature_count // 128 * 128
    tail = feature_count - main
    starts = (jnp.cumsum(widths) - widths) * 4
    ends = jnp.minimum(starts + widths * 4, main)
    begins = jnp.minimum(starts // 128, (main - WINDOW) // 128)
    meta = jnp.stack([starts, ends, begins]).astype(jnp.int32)
    x_tail = jnp.pad(spectrum[:, main:], ((0, 0), (0, 128 - tail)))
    gain_tail = jnp.pad(bin_gain[main:], (0, 128 - tail))[None]
    w_tail = jnp.pad(embed_weight[main:], ((0, 128 - tail), (0, 0)))
    return pl.pallas_call(
        functools.partial(embed_kernel, bands, feature_count),
        out_shape=jax.ShapeDtypeStruct((bands, frames, width), BF),
        in_specs=[smem()] + [whole()] * 7,
        out_specs=whole(),
        compiler_params=pltpu.CompilerParams(vmem_limit_bytes=LIMIT),
        cost_estimate=pl.CostEstimate(flops=2 * 10**9, bytes_accessed=9 * 10**6, transcendentals=0),
    )(meta, spectrum, bin_gain[None], embed_weight, x_tail, gain_tail, w_tail, embed_bias)


VROWS = 80


def time_kernel(columns, length_ref, x_ref, gain_ref, wqkv_ref, wout_ref, cos_ref, sin_ref, out_ref, q_ref, k_ref, v_ref, heads_ref):
    frames, width = x_ref.shape
    inner = HEADS * DH
    length = length_ref[0]
    rows_each = 512
    lane = lax.broadcasted_iota(jnp.int32, (1, GROUP), 1)
    wq = [split_halves(wqkv_ref[:, g * GROUP : (g + 1) * GROUP]) for g in range(2)]
    wk = [split_halves(wqkv_ref[:, inner + g * GROUP : inner + (g + 1) * GROUP]) for g in range(2)]
    wv = wqkv_ref[:, 2 * inner :]
    bound = jnp.zeros((1, 1), F32)
    vmost = jnp.zeros((1, 1), F32)
    first_key = [None, None]
    qmost = [jnp.zeros((1, 1), F32)] * HEADS
    kmost = [jnp.zeros((1, 1), F32)] * HEADS
    for b in range(frames // rows_each):
        rows = slice(b * rows_each, (b + 1) * rows_each)
        normed = rms_norm(x_ref[rows, :].astype(F32), gain_ref[...])
        cosine = cos_ref[rows, :]
        sines = sin_ref[rows, :]
        alive_row = (lax.broadcasted_iota(jnp.int32, (rows_each, 1), 0) + b * rows_each) < length
        alive_col = (lax.broadcasted_iota(jnp.int32, (1, rows_each), 1) + b * rows_each) < length
        for g in range(2):
            qa, qb = rope(jnp.dot(normed, wq[g], preferred_element_type=F32), cosine, sines)
            scaled = jnp.concatenate([qa, qb], axis=1) * (LOG2E * DH**-0.5)
            q_ref[g, rows, :] = scaled.astype(BF)
            ka, kb = rope(jnp.dot(normed, wk[g], preferred_element_type=F32), cosine, sines)
            keys = jnp.concatenate([ka, kb], axis=1)
            if b == 0:
                first_key[g] = keys[:1]
            keys = jnp.where(alive_row, keys, first_key[g])
            k_ref[g, rows, :] = keys.astype(BF)
            qq = scaled * scaled
            kk = keys * keys
            for h in range(4):
                mine = (lane % 128) // HALF == h
                qn = jnp.max(jnp.sum(jnp.where(mine, qq, 0.0), axis=1, keepdims=True), axis=0, keepdims=True)
                kn = jnp.max(jnp.sum(jnp.where(mine, kk, 0.0), axis=1, keepdims=True), axis=0, keepdims=True)
                qmost[4 * g + h] = jnp.maximum(qmost[4 * g + h], qn)
                kmost[4 * g + h] = jnp.maximum(kmost[4 * g + h], kn)
        values = lax.dot_general(wv, normed, (((0,), (1,)), ((), ())), preferred_element_type=F32)
        values = jnp.where(alive_col, values, 0.0)
        vmost = jnp.maximum(vmost, jnp.max(jnp.max(jnp.abs(values), axis=0, keepdims=True), axis=1, keepdims=True))
        values = values.astype(BF)
        ones = jnp.broadcast_to(jnp.where(alive_col, 1.0, 0.0), (VROWS - DH, rows_each)).astype(BF)
        for h in range(HEADS):
            v_ref[h, :DH, rows] = values[h * DH : (h + 1) * DH]
            v_ref[h, DH:, rows] = ones
    for h in range(HEADS):
        bound = jnp.maximum(bound, qmost[h] * kmost[h])
    fits = (jnp.max(bound) * 1.05 < SAFE * SAFE) & (jnp.max(vmost) < VSAFE)

    def attend(shift):
        def block(qb, carry):
            rows = pl.ds(pl.multiple_of(qb * columns, columns), columns)

            def head(h, inner_carry):
                g = h // 4
                mine = (lane % 128) // HALF == h % 4
                queries = jnp.where(mine, q_ref[g, rows, :], jnp.zeros((), BF))
                scores = lax.dot_general(k_ref[g], queries, NT, preferred_element_type=F32)
                if shift:
                    scores = scores - jnp.max(scores, axis=0, keepdims=True)
                powers = jnp.exp2(scores).astype(BF)
                mixed = jnp.dot(v_ref[h], powers, preferred_element_type=F32)
                mixed = mixed[:DH] / mixed[DH : DH + 1]
                heads_ref[pl.ds(pl.multiple_of(h * DH, DH), DH), :] = mixed.astype(BF)
                return inner_carry

            lax.fori_loop(0, HEADS, head, 0)
            projected = lax.dot_general(heads_ref[...], wout_ref[...], TN, preferred_element_type=F32)
            out_ref[rows, :] = (x_ref[rows, :].astype(F32) + projected).astype(BF)
            return carry

        lax.fori_loop(0, frames // columns, block, 0)

    @pl.when(fits)
    def _():
        attend(False)

    @pl.when(jnp.logical_not(fits))
    def _():
        attend(True)


def time_attention(sequence, lengths, gain, wqkv, wout):
    frames, width = sequence.shape
    columns = min(1024, frames)
    cosine, sines = rotary_tables(np.arange(frames), 4)
    return pl.pallas_call(
        functools.partial(time_kernel, columns),
        out_shape=jax.ShapeDtypeStruct((frames, width), BF),
        in_specs=[smem()] + [whole()] * 6,
        out_specs=whole(),
        scratch_shapes=[
            VMEM((2, frames, GROUP), BF),
            VMEM((2, frames, GROUP), BF),
            VMEM((HEADS, VROWS, frames), BF),
            VMEM((HEADS * DH, columns), BF),
        ],
        compiler_params=pltpu.CompilerParams(vmem_limit_bytes=LIMIT),
        cost_estimate=pl.CostEstimate(flops=4 * 10**10, bytes_accessed=6 * 10**6, transcendentals=0),
    )(lengths, sequence, gain[None], wqkv, wout, jnp.asarray(cosine), jnp.asarray(sines))


FRAMES_EACH = 16


def band_kernel(place_ref, x_ref, gain_ref, wqkv_ref, wout_ref, cot_ref, cos_ref, sin_ref, out_ref, grad_ref, heads_ref):
    bands, frames, width = x_ref.shape
    inner = HEADS * DH
    rows = bands * FRAMES_EACH
    half = 256
    lane = lax.broadcasted_iota(jnp.int32, (1, GROUP), 1)
    lane128 = lax.broadcasted_iota(jnp.int32, (1, 128), 1)
    wq = [split_halves(wqkv_ref[:, g * GROUP : (g + 1) * GROUP]) for g in range(2)]
    wk = [split_halves(wqkv_ref[:, inner + g * GROUP : inner + (g + 1) * GROUP]) for g in range(2)]
    wv = wqkv_ref[:, 2 * inner :]
    length = place_ref[0]
    base = place_ref[1]
    to = lax.broadcasted_iota(jnp.int32, (rows, rows), 0)
    src = lax.broadcasted_iota(jnp.int32, (rows, rows), 1)
    order = (src == to % bands * FRAMES_EACH + to // bands).astype(F32).astype(BF)
    same = lax.broadcasted_iota(jnp.int32, (half, half), 0) // bands == lax.broadcasted_iota(jnp.int32, (half, half), 1) // bands
    grad_ref[...] = jnp.zeros_like(grad_ref)

    def block(i, carry):
        piece = x_ref[:, pl.ds(pl.multiple_of(i * FRAMES_EACH, FRAMES_EACH), FRAMES_EACH), :].reshape(rows, width)
        x = jnp.dot(order, piece, preferred_element_type=F32)
        normed = rms_norm(x, gain_ref[...])
        cosine = cos_ref[...]
        sines = sin_ref[...]
        values = jnp.dot(normed, wv, preferred_element_type=F32)
        for g in range(2):
            qa, qb = rope(jnp.dot(normed, wq[g], preferred_element_type=F32), cosine, sines)
            queries = (jnp.concatenate([qa, qb], axis=1) * (LOG2E * DH**-0.5)).astype(BF)
            ka, kb = rope(jnp.dot(normed, wk[g], preferred_element_type=F32), cosine, sines)
            keys = jnp.concatenate([ka, kb], axis=1).astype(BF)
            for s in range(rows // half):
                part = slice(s * half, (s + 1) * half)
                for pair in range(2):
                    column = (2 * g + pair) * 128
                    v = values[part, column : column + 128]
                    outs = []
                    for odd in range(2):
                        mine = (lane % 128) // HALF == 2 * pair + odd
                        masked = jnp.where(mine, queries[part], jnp.zeros((), BF))
                        scores = lax.dot_general(masked, keys[part], NT, preferred_element_type=F32)
                        scores = jnp.where(same, scores, -1e30)
                        powers = jnp.exp2(scores - jnp.max(scores, axis=1, keepdims=True)).astype(BF)
                        own = (lane128 < DH) if odd == 0 else (lane128 >= DH)
                        extended = jnp.where(own, v, 1.0).astype(BF)
                        mixed = jnp.dot(powers, extended, preferred_element_type=F32)
                        outs.append(mixed / pltpu.roll(mixed, DH, 1))
                    joined = jnp.where(lane128 < DH, outs[0], outs[1])
                    heads_ref[part, column : column + 128] = joined.astype(BF)
        heads = heads_ref[...]
        projected = jnp.dot(heads, wout_ref[...], preferred_element_type=F32)
        here = pl.ds(pl.multiple_of(i * rows, rows), rows)
        out_ref[here, :] = (x + projected).astype(BF)
        frame = base + i * FRAMES_EACH + lax.broadcasted_iota(jnp.int32, (rows, 1), 0) // bands
        tangent = jnp.where(frame < length, cot_ref[here, :].astype(F32), 0.0).astype(BF)
        grad_ref[...] += lax.dot_general(heads, tangent, TN, preferred_element_type=F32)
        return carry

    lax.fori_loop(0, frames // FRAMES_EACH, block, 0)


def band_attention(returned, place, gain, wqkv, wout, cotangent):
    bands, frames, width = returned.shape
    inner = HEADS * DH
    rows = bands * FRAMES_EACH
    cosine, sines = rotary_tables(np.tile(np.arange(bands), FRAMES_EACH), 4)
    return pl.pallas_call(
        band_kernel,
        out_shape=(
            jax.ShapeDtypeStruct((frames * bands, width), BF),
            jax.ShapeDtypeStruct((inner, width), F32),
        ),
        in_specs=[smem()] + [whole()] * 7,
        out_specs=(whole(), whole()),
        scratch_shapes=[VMEM((rows, inner), BF)],
        compiler_params=pltpu.CompilerParams(vmem_limit_bytes=LIMIT),
        cost_estimate=pl.CostEstimate(flops=10**10, bytes_accessed=7 * 10**6, transcendentals=0),
    )(place, returned, gain[None], wqkv, wout, cotangent.reshape(frames * bands, width), jnp.asarray(cosine), jnp.asarray(sines))


def sum_kernel(seq, songs, part_ref, out_ref, small, got, mid, full, send1, recv1, send2, recv2, send3, recv3):
    me = lax.axis_index("seq")
    song = lax.axis_index("song")
    rows = small.shape[1]
    barrier = pltpu.get_barrier_semaphore()

    def greet(d, carry):
        pl.semaphore_signal(barrier, inc=1, device_id=(lax.rem(me + d, seq), song), device_id_type=MESH)
        return carry

    lax.fori_loop(1, seq, greet, 0)
    for d in range(1, songs):
        pl.semaphore_signal(barrier, inc=1, device_id=(me, lax.rem(song + d, songs)), device_id_type=MESH)
    for r in range(seq):
        small[r] = part_ref[r * rows : (r + 1) * rows, :].astype(BF)
    pl.semaphore_wait(barrier, seq - 1 + songs - 1)

    def first(d):
        peer = lax.rem(me + d, seq)
        return pltpu.make_async_remote_copy(
            src_ref=small.at[peer], dst_ref=got.at[d], send_sem=send1.at[d], recv_sem=recv1.at[d],
            device_id=(peer, song), device_id_type=MESH)

    def start1(d, carry):
        first(d).start()
        return carry

    def wait1(d, carry):
        first(d).wait()
        return carry

    lax.fori_loop(1, seq, start1, 0)
    got[0] = small[me]
    lax.fori_loop(1, seq, wait1, 0)
    total = got[0].astype(F32)
    for d in range(1, seq):
        total = total + got[d].astype(F32)
    mid[song] = total
    copies = []
    for d in range(1, songs):
        copies.append(pltpu.make_async_remote_copy(
            src_ref=mid.at[song], dst_ref=mid.at[song], send_sem=send2.at[d], recv_sem=recv2.at[d],
            device_id=(me, lax.rem(song + d, songs)), device_id_type=MESH))
    for c in copies:
        c.start()
    for c in copies:
        c.wait()
    total = mid[0]
    for s in range(1, songs):
        total = total + mid[s]
    full[me] = total.astype(BF)

    def third(d):
        return pltpu.make_async_remote_copy(
            src_ref=full.at[me], dst_ref=full.at[me], send_sem=send3.at[d], recv_sem=recv3.at[d],
            device_id=(lax.rem(me + d, seq), song), device_id_type=MESH)

    def start3(d, carry):
        third(d).start()
        return carry

    def wait3(d, carry):
        third(d).wait()
        return carry

    lax.fori_loop(1, seq, start3, 0)
    lax.fori_loop(1, seq, wait3, 0)
    for r in range(seq):
        out_ref[r * rows : (r + 1) * rows, :] = full[r].astype(F32)


def gradient_sum(partial):
    seq = lax.axis_size("seq")
    songs = lax.axis_size("song")
    inner, width = partial.shape
    rows = inner // seq
    dma = pltpu.SemaphoreType.DMA
    return pl.pallas_call(
        functools.partial(sum_kernel, seq, songs),
        out_shape=jax.ShapeDtypeStruct((inner, width), F32),
        in_specs=[whole()],
        out_specs=whole(),
        scratch_shapes=[
            VMEM((seq, rows, width), BF),
            VMEM((seq, rows, width), BF),
            VMEM((songs, rows, width), F32),
            VMEM((seq, rows, width), BF),
            dma((seq,)), dma((seq,)), dma((songs,)), dma((songs,)), dma((seq,)), dma((seq,)),
        ],
        compiler_params=pltpu.CompilerParams(collective_id=0, has_side_effects=True, vmem_limit_bytes=LIMIT),
        cost_estimate=pl.CostEstimate(flops=10**7, bytes_accessed=4 * 10**6, transcendentals=0),
    )(partial)


def per_device(spectrum, widths, lengths, bin_gain, embed_weight, embed_bias, time_gain, time_qkv, time_out, band_gain, band_qkv, band_out, cotangent):
    local_frames = spectrum.shape[1]
    bands, width = embed_bias.shape
    computed = embed(spectrum[0], widths, bin_gain, embed_weight, embed_bias)
    owned = lax.all_to_all(computed, "seq", split_axis=0, concat_axis=1, tiled=True)
    timed = time_attention(owned[0], lengths, time_gain, time_qkv, time_out)
    returned = lax.all_to_all(timed.reshape(-1, local_frames, width), "seq", split_axis=0, concat_axis=0, tiled=True)
    place = jnp.stack([lengths[0], lax.axis_index("seq") * local_frames]).astype(jnp.int32)
    output, partial = band_attention(returned, place, band_gain, band_qkv, band_out, cotangent[0])
    gradient = gradient_sum(partial)
    return output.reshape(1, local_frames, bands, width), gradient


def solution(mesh):
    return jax.shard_map(
        per_device,
        mesh=mesh,
        in_specs=(P("song", "seq", None), P(), P("song"), P(), P(), P(), P(), P(), P(), P(), P(), P(), P("song", "seq", None, None)),
        out_specs=(P("song", "seq", None, None), P()),
        check_vma=False,
    )
```

time: 919 us -> 190 us (0.21); the launches traced: 907 us -> 190 us
  matrix products: 236 us -> 0 us
  local copies, waits for them, and re-layouts: 204 us -> 11.6 us
  other arithmetic: 156 us -> 2.05 us
  waiting for transfers between devices: 181 us -> 42 us
  Pallas kernels: 0 us -> 118 us
  loops' own time: 100 us -> 0 us
  between operations: 15.2 us -> 1.33 us
    dot_general x43 -> x0, matrix products: 168 us -> none  [the longest x32 69.5 us: embed_piece(): jnp.dot(normed, weight_rows, preferred_element_type=jnp.float32)]
    psum x1 -> x0, waiting for transfers between devices: 140 us -> none  [per_device(): gradient = lax.psum(partial_grad, ('seq', 'song'))]
    pallas_call x0 -> x4, Pallas kernels: none -> 118 us  [the longest x1 60.6 us: time_attention(): pl.pallas_call(functools.partial(time_kernel, columns), out_shape=jax.Sha...]
    another operation x2 -> x0, loops' own time: 100 us -> none  [the longest x1 97.5 us: per_device(): computed = lax.map(local_band, jnp.arange(band_count, dtype=jnp.int32))]
    dynamic_slice x164 -> x0, local copies, waits for them, and re-layouts: 86.7 us -> none  [the longest x32 23.6 us: embed_piece(): slot_bias[slot_id]]
    sub x4 -> x0, matrix products: 67.6 us -> none  [softmax_rows(): powers = jnp.exp(scores - maximum)]
    reduce_sum x34 -> x0, other arithmetic: 54 us -> none  [the longest x2 47.2 us: norm_rows(): square = jnp.mean(floats * floats, axis=-1, keepdims=True)]
    another operation x5, other arithmetic: 47 us -> 2.05 us  [the longest x2 1.27 us: embed(): meta = jnp.stack([starts, ends, begins]).astype(jnp.int32)]
  transfers between devices with their start and end apart: 3 -> 2, of which waited for: 3 -> 2; matrix products, arithmetic and copies ran while one was open for 1% -> 1% of each run, Pallas kernels for 0% -> 0%
where the time goes in v1:
time: 190 us
  Pallas kernels  118 us (62%)
  waiting for transfers between devices  42 us (22%)
  starting transfers between devices  14.5 us (8%)
  local copies, waits for them, and re-layouts  11.6 us (6%)
  other arithmetic  2.05 us (1%)
    pallas_call x1, Pallas kernels, time_attention(): pl.pallas_call(functools.partial(time_kernel, columns), out_shape=jax.Sha...  60.6 us
    pallas_call x1, Pallas kernels, gradient_sum(): pl.pallas_call(functools.partial(sum_kernel, seq, songs), out_shape=jax.S...  27.6 us
    all_to_all x1, waiting for transfers between devices, per_device(): lax.all_to_all(timed.reshape(-1, local_frames, width), 'seq', split_axis=...  21.1 us
    all_to_all x1, waiting for transfers between devices, per_device(): lax.all_to_all(computed, 'seq', split_axis=0, concat_axis=1, tiled=True)  21 us
    pallas_call x1, Pallas kernels, band_attention(): pl.pallas_call(band_kernel, out_shape=(jax.ShapeDtypeStruct((frames * ban...  18.8 us
    pallas_call x1, Pallas kernels, embed(): pl.pallas_call(functools.partial(embed_kernel, bands, feature_count), out...  11.2 us
    all_to_all x1, starting transfers between devices, per_device(): lax.all_to_all(computed, 'seq', split_axis=0, concat_axis=1, tiled=True)  8.72 us
    all_to_all x1, starting transfers between devices, per_device(): lax.all_to_all(timed.reshape(-1, local_frames, width), 'seq', split_axis=...  5.73 us
  transfers between devices with their start and end apart: 2, of which 2 were waited for; matrix products, arithmetic and copies ran while one was open for 1% of the time, Pallas kernels for 0%

profile of v1, /device:TPU:1, one launch (start us, length us, event | category | flops | bytes accessed | tf_op | source)
XLA Modules:
  0.0 189.6 jit_solution(4190650912251417866)
XLA Ops:
  0.6 0.7 slice.10
  1.3 1.4 broadcast_in_dim.12.gain_ref
  2.7 0.6 pad_bitcast_fusion.gt_ref
  3.3 0.7 slice.11
  4.0 0.7 slice.12
  4.7 0.7 copy.20
  5.4 0.1 reduce-window.9
  5.5 0.1 reduce
  5.6 0.7 fusion
  6.3 0.6 pad.12.xt_ref
  6.9 0.7 pad.14.wt_ref
  7.5 0.6 pad_add_fusion.meta_ref
  8.1 11.2 %shard_map.176 = bf16[32,64,384]{2,1,0:T(8,128)(2,1)} custom-call(s32[3,32]{1,0:T(4,128)} %pad_add_fusion.meta_ref, bf16[64,8196]{1,0:T(8,128)(2,1)} %bitcast.18, f32[1,8196]{1,0:T(1,128)} %broadcast_in_dim.12.gain_ref, bf16[8196,384]{1,0:T(8,128)(2,1)} %w_ref.1, bf16[64,128]{1,0:T(8,128)(2,1)} %pad.12.xt_ref, f32[1,128]{1,0:T(1,128)} %pad_bitcast_fusion.gt_ref, ...), custom_call_target="tpu_custom_call" | custom-call | flops 2000000000 | bytes 9000000 | tf_op jit(solution)/shard_map/pallas_call | solution.py:112
  19.3 0.0 copy-start.2
  19.3 8.7 %all-to-all-start = ((bf16[32,64,384]{2,1,0:T(8,128)(2,1)}), bf16[32,64,384]{2,1,0:T(8,128)(2,1)S(1)}, u32[]{:S(2)}, u32[]{:S(2)}) async-start(bf16[32,64,384]{2,1,0:T(8,128)(2,1)} %shard_map.176), calls=%async_computation | async-start | bytes 3145728 | tf_op jit(solution)/shard_map/all_to_all | solution.py:409
  28.7 0.0 copy-done.2
  28.7 0.6 broadcast_in_dim.14.gain_ref
  29.2 21.0 %all-to-all-done = bf16[32,64,384]{2,1,0:T(8,128)(2,1)S(1)} async-done(((bf16[32,64,384]{2,1,0:T(8,128)(2,1)}), bf16[32,64,384]{2,1,0:T(8,128)(2,1)S(1)}, u32[]{:S(2)}, u32[]{:S(2)}) %all-to-all-start) | async-done | bytes 1572896 | tf_op jit(solution)/shard_map/all_to_all | solution.py:409
  50.2 0.0 copy-start.1
  50.2 1.1 copy-done.1
  51.3 60.6 %shard_map.177 = bf16[2048,384]{1,0:T(8,128)(2,1)} custom-call(s32[1]{0:T(128)S(6)} %copy.22.length_ref, bf16[2048,384]{1,0:T(8,128)(2,1)} %bitcast.16, f32[1,384]{1,0:T(1,128)} %broadcast_in_dim.14.gain_ref, bf16[384,1536]{1,0:T(8,128)(2,1)} %wqkv_ref.2, bf16[512,384]{1,0:T(8,128)(2,1)} %wout_ref.2, f32[2048,128]{1,0:T(8,128)} %constant.46.clone.cos_ref, ...), custom_call_target="tpu_custom_call" | custom-call | flops 40000000000 | bytes 6000000 | tf_op jit(solution)/shard_map/pallas_call | solution.py:213
  111.9 0.0 copy-start.3
  111.9 5.7 %all-to-all-start.1 = ((bf16[32,64,384]{2,1,0:T(8,128)(2,1)}), bf16[32,64,384]{2,1,0:T(8,128)(2,1)S(1)}, u32[]{:S(2)}, u32[]{:S(2)}) async-start(bf16[32,64,384]{2,1,0:T(8,128)(2,1)} %bitcast.15), calls=%async_computation.1 | async-start | bytes 3145728 | tf_op jit(solution)/shard_map/all_to_all | solution.py:411
  117.7 0.0 copy-done.3
  117.7 0.6 broadcast_in_dim.15.gain_ref
  118.3 0.6 pad_add_fusion.1.place_ref
  118.9 21.1 %all-to-all-done.1.x_ref = bf16[32,64,384]{2,1,0:T(8,128)(2,1)S(1)} async-done(((bf16[32,64,384]{2,1,0:T(8,128)(2,1)}), bf16[32,64,384]{2,1,0:T(8,128)(2,1)S(1)}, u32[]{:S(2)}, u32[]{:S(2)}) %all-to-all-start.1) | async-done | bytes 1572896 | tf_op jit(solution)/shard_map/all_to_all | solution.py:411
  139.9 0.0 copy-start
  139.9 1.2 copy-done
  141.1 18.8 %shard_map.178 = (bf16[2048,384]{1,0:T(8,128)(2,1)}, f32[512,384]{1,0:T(8,128)}) custom-call(s32[2]{0:T(128)} %pad_add_fusion.1.place_ref, bf16[32,64,384]{2,1,0:T(8,128)(2,1)} %copy-done, f32[1,384]{1,0:T(1,128)} %broadcast_in_dim.15.gain_ref, bf16[384,1536]{1,0:T(8,128)(2,1)} %wqkv_ref.3, bf16[512,384]{1,0:T(8,128)(2,1)} %wout_ref.3, ...), custom_call_target="tpu_custom_call" | custom-call | flops 10000000000 | bytes 7000000 | tf_op jit(solution)/shard_map/pallas_call | solution.py:297
  159.9 27.6 %shard_map.179 = f32[512,384]{1,0:T(8,128)} custom-call(f32[512,384]{1,0:T(8,128)} %get-tuple-element.5.part_ref), custom_call_target="tpu_custom_call" | custom-call | flops 10000000 | bytes 4000000 | tf_op jit(solution)/shard_map/pallas_call | solution.py:388
  187.5 2.1 %copy.23 = f32[512,384]{1,0:T(8,128)} copy(f32[512,384]{1,0:T(8,128)} %shard_map.179) | data formatting | bytes 1572864
Async XLA Ops:
  19.3 9.4 %copy-start.2 = (f32[384]{0:T(512)S(1)}, f32[384]{0:T(512)}, u32[]{:S(2)}) copy-start(f32[384]{0:T(512)} %param.23) | copy-start | bytes 4612
  19.3 30.9 %all-to-all-start = ((bf16[32,64,384]{2,1,0:T(8,128)(2,1)}), bf16[32,64,384]{2,1,0:T(8,128)(2,1)S(1)}, u32[]{:S(2)}, u32[]{:S(2)}) async-start(bf16[32,64,384]{2,1,0:T(8,128)(2,1)} %shard_map.176), calls=%async_computation | async-start | bytes 3145728 | tf_op jit(solution)/shard_map/all_to_all | solution.py:409
  50.2 1.1 copy-start.1
  111.9 5.7 %copy-start.3 = (f32[384]{0:T(512)S(1)}, f32[384]{0:T(512)}, u32[]{:S(2)}) copy-start(f32[384]{0:T(512)} %param.26) | copy-start | bytes 4612
  111.9 28.0 %all-to-all-start.1 = ((bf16[32,64,384]{2,1,0:T(8,128)(2,1)}), bf16[32,64,384]{2,1,0:T(8,128)(2,1)S(1)}, u32[]{:S(2)}, u32[]{:S(2)}) async-start(bf16[32,64,384]{2,1,0:T(8,128)(2,1)} %bitcast.15), calls=%async_computation.1 | async-start | bytes 3145728 | tf_op jit(solution)/shard_map/all_to_all | solution.py:411
  139.9 1.2 copy-start

commit v2 on v1

--- a/solution.py
+++ b/solution.py
@@ -21,8 +21,8 @@
 MESH = pl.DeviceIdType.MESH
 BF = jnp.bfloat16
 F32 = jnp.float32
-SAFE = 60.0
-VSAFE = 2.0**40
+SAFE = 100.0
+VSAFE = 2.0**12
 VMEM = pltpu.VMEM
 LIMIT = 56 * 2**20
 
@@ -62,140 +62,235 @@
     return leading * cosine - second * sines, second * cosine + leading * sines
 
 
-def embed_kernel(bands, limit, meta_ref, x_ref, gain_ref, w_ref, xt_ref, gt_ref, wt_ref, bias_ref, out_ref):
-    lane = lax.broadcasted_iota(jnp.int32, (1, WINDOW), 1)
-
-    def band(k, last):
+NARROW = 640
+
+
+def embed_kernel(bands, meta_ref, x_ref, gain_ref, w_ref, bias_ref, out_ref):
+    limit = x_ref.shape[1]
+    main = limit // 128 * 128
+
+    def band(k, size):
         first = meta_ref[0, k]
-        end = meta_ref[1, k]
-        begin = pl.multiple_of(meta_ref[2, k] * 128, 128)
-        window = pl.ds(begin, WINDOW)
-        entry = lane + begin
+        count = meta_ref[1, k]
+        begin = pl.multiple_of(jnp.minimum(meta_ref[2, k], (main - size) // 128) * 128, 128)
+        window = pl.ds(begin, size)
+        entry = lax.broadcasted_iota(jnp.int32, (1, size), 1) + begin
         piece = x_ref[:, window].astype(F32)
-        piece = jnp.where((entry >= first) & (entry < end), piece, 0.0)
-        total = jnp.sum(piece * piece, axis=1, keepdims=True)
-        if last:
-            tail = xt_ref[...].astype(F32)
-            total = total + jnp.sum(tail * tail, axis=1, keepdims=True)
-        mean = total / (end - first + (limit - first - (end - first) if last else 0)).astype(F32)
-        scale = 1.0 / jnp.sqrt(jnp.maximum(mean, FLOOR))
+        piece = jnp.where((entry >= first) & (entry < first + count), piece, 0.0)
+        tail = jnp.where(k == bands - 1, x_ref[:, main:].astype(F32), 0.0)
+        square = jnp.sum(piece * piece, axis=1, keepdims=True) + jnp.sum(tail * tail, axis=1, keepdims=True)
+        scale = 1.0 / jnp.sqrt(jnp.maximum(square / count.astype(F32), FLOOR))
         normed = (piece * scale * gain_ref[:, window]).astype(BF)
-        summed = jnp.dot(normed, w_ref[window, :], preferred_element_type=F32)
-        if last:
-            normed = (tail * scale * gt_ref[...]).astype(BF)
-            summed = summed + jnp.dot(normed, wt_ref[...], preferred_element_type=F32)
-        out_ref[k] = (summed + bias_ref[pl.ds(k, 1), :]).astype(BF)
+        summed = jnp.dot(normed, w_ref[window, :], preferred_element_type=F32) + bias_ref[pl.ds(k, 1), :]
+        normed = (tail * scale * gain_ref[:, main:]).astype(BF).astype(F32)
+        rows = w_ref[main:, :].astype(F32)
+        for e in range(limit - main):
+            summed = summed + normed[:, e : e + 1] * rows[e : e + 1, :]
+        out_ref[k] = summed.astype(BF)
 
     def step(i, carry):
-        for j in range(4):
-            band(i * 4 + j, False)
-        return carry
-
-    lax.fori_loop(0, bands // 4 - 1, step, 0)
-    for k in range(bands - 4, bands - 1):
-        band(k, False)
-    band(bands - 1, True)
+        narrow = meta_ref[1, 4 * i] <= NARROW - 124
+        for j in range(1, 4):
+            narrow = narrow & (meta_ref[1, 4 * i + j] <= NARROW - 124)
+
+        @pl.when(narrow)
+        def _():
+            for j in range(4):
+                band(4 * i + j, NARROW)
+
+        @pl.when(jnp.logical_not(narrow))
+        def _():
+            for j in range(4):
+                band(4 * i + j, WINDOW)
+
+        return carry
+
+    lax.fori_loop(0, bands // 4, step, 0)
 
 
 def embed(spectrum, widths, bin_gain, embed_weight, embed_bias):
     frames, feature_count = spectrum.shape
     bands, width = embed_bias.shape
-    main = feature_count // 128 * 128
-    tail = feature_count - main
     starts = (jnp.cumsum(widths) - widths) * 4
-    ends = jnp.minimum(starts + widths * 4, main)
-    begins = jnp.minimum(starts // 128, (main - WINDOW) // 128)
-    meta = jnp.stack([starts, ends, begins]).astype(jnp.int32)
-    x_tail = jnp.pad(spectrum[:, main:], ((0, 0), (0, 128 - tail)))
-    gain_tail = jnp.pad(bin_gain[main:], (0, 128 - tail))[None]
-    w_tail = jnp.pad(embed_weight[main:], ((0, 128 - tail), (0, 0)))
+    meta = jnp.stack([starts, widths * 4, starts // 128]).astype(jnp.int32)
     return pl.pallas_call(
-        functools.partial(embed_kernel, bands, feature_count),
+        functools.partial(embed_kernel, bands),
         out_shape=jax.ShapeDtypeStruct((bands, frames, width), BF),
-        in_specs=[smem()] + [whole()] * 7,
+        in_specs=[smem()] + [whole()] * 4,
         out_specs=whole(),
-        compiler_params=pltpu.CompilerParams(vmem_limit_bytes=LIMIT),
+        compiler_params=pltpu.CompilerParams(vmem_limit_bytes=32 * 2**20),
         cost_estimate=pl.CostEstimate(flops=2 * 10**9, bytes_accessed=9 * 10**6, transcendentals=0),
-    )(meta, spectrum, bin_gain[None], embed_weight, x_tail, gain_tail, w_tail, embed_bias)
+    )(meta, spectrum, bin_gain[None], embed_weight, embed_bias)
 
 
 VROWS = 80
 
 
-def time_kernel(columns, length_ref, x_ref, gain_ref, wqkv_ref, wout_ref, cos_ref, sin_ref, out_ref, q_ref, k_ref, v_ref, heads_ref):
-    frames, width = x_ref.shape
+def exchange_kernel(
+    seq, length_ref, bands_ref, gain_ref, wqkv_ref, cos_ref, sin_ref,
+    x_ref, qa_ref, qb_ref, k_ref, v_ref, most_ref, got, send_sem, recv_sem,
+):
+    frames, width = got.shape[1:]
+    half = frames // 2
     inner = HEADS * DH
-    length = length_ref[0]
-    rows_each = 512
+    me = lax.axis_index("seq")
+    song = lax.axis_index("song")
+    y, x, core = me // 8, me // 2 % 4, me % 2
+
+    def other(i, sign):
+        return (y + sign * (i // 8) + 4) % 4 * 8 + (x + sign * (i // 2 % 4) + 4) % 4 * 2 + (core + i % 2) % 2
+
+    barrier = pltpu.get_barrier_semaphore()
+
+    def greet(i, carry):
+        pl.semaphore_signal(barrier, inc=1, device_id=(other(i, 1), song), device_id_type=MESH)
+        return carry
+
+    lax.fori_loop(1, seq, greet, 0)
     lane = lax.broadcasted_iota(jnp.int32, (1, GROUP), 1)
     wq = [split_halves(wqkv_ref[:, g * GROUP : (g + 1) * GROUP]) for g in range(2)]
     wk = [split_halves(wqkv_ref[:, inner + g * GROUP : inner + (g + 1) * GROUP]) for g in range(2)]
     wv = wqkv_ref[:, 2 * inner :]
-    bound = jnp.zeros((1, 1), F32)
-    vmost = jnp.zeros((1, 1), F32)
-    first_key = [None, None]
-    qmost = [jnp.zeros((1, 1), F32)] * HEADS
-    kmost = [jnp.zeros((1, 1), F32)] * HEADS
-    for b in range(frames // rows_each):
-        rows = slice(b * rows_each, (b + 1) * rows_each)
-        normed = rms_norm(x_ref[rows, :].astype(F32), gain_ref[...])
+    pl.semaphore_wait(barrier, seq - 1)
+
+    def copy(i):
+        k = other(i, 1)
+        return pltpu.make_async_remote_copy(
+            src_ref=bands_ref.at[k], dst_ref=got.at[me], send_sem=send_sem.at[i], recv_sem=recv_sem.at[i],
+            device_id=(k, song), device_id_type=MESH)
+
+    def start(j, carry):
+        copy(8 * (1 + 2 * (j % 2)) + j // 2).start()
+        return carry
+
+    def start_rest(j, carry):
+        copy(16 + j).start()
+        copy(j).start()
+        return carry
+
+    lax.fori_loop(0, 16, start, 0)
+    copy(16).start()
+    lax.fori_loop(1, 8, start_rest, 0)
+    got[me] = bands_ref[me]
+    length = length_ref[0]
+
+    heads_of = lax.broadcasted_iota(jnp.int32, (GROUP, 128), 0) % 128 // HALF
+    per_head = (heads_of == lax.broadcasted_iota(jnp.int32, (GROUP, 128), 1)).astype(F32).astype(BF)
+
+    def longest(rows):
+        squares = jnp.dot((rows * rows).astype(BF), per_head, preferred_element_type=F32)
+        return jnp.max(squares, axis=0, keepdims=True)
+
+    def project(dy, stats):
+        row = (y - dy + 4) % 4
+
+        def wait(i, carry):
+            copy(8 * dy + i).wait_recv()
+            return carry
+
+        lax.fori_loop(1 if dy == 0 else 0, 8, wait, 0)
+        owners = pl.ds(pl.multiple_of(row * 8, 8), 8)
+        count = 8 * frames
+        base = pl.multiple_of(row * count, count)
+        rows = pl.ds(base, count)
+        received = got[owners]
+        x_ref[owners] = received
+        normed = rms_norm(received.reshape(count, width).astype(F32), gain_ref[...])
         cosine = cos_ref[rows, :]
         sines = sin_ref[rows, :]
-        alive_row = (lax.broadcasted_iota(jnp.int32, (rows_each, 1), 0) + b * rows_each) < length
-        alive_col = (lax.broadcasted_iota(jnp.int32, (1, rows_each), 1) + b * rows_each) < length
+        alive_row = (lax.broadcasted_iota(jnp.int32, (count, 1), 0) + base) < length
+        alive_col = (lax.broadcasted_iota(jnp.int32, (1, count), 1) + base) < length
+        here = pl.ds(pl.multiple_of(row * 8 * half, 8 * half), 8 * half)
+        kinds = []
         for g in range(2):
             qa, qb = rope(jnp.dot(normed, wq[g], preferred_element_type=F32), cosine, sines)
             scaled = jnp.concatenate([qa, qb], axis=1) * (LOG2E * DH**-0.5)
-            q_ref[g, rows, :] = scaled.astype(BF)
+            parts = scaled.reshape(8, frames, GROUP)
+            qa_ref[g, here, :] = parts[:, :half].reshape(8 * half, GROUP).astype(BF)
+            qb_ref[g, here, :] = parts[:, half:].reshape(8 * half, GROUP).astype(BF)
             ka, kb = rope(jnp.dot(normed, wk[g], preferred_element_type=F32), cosine, sines)
             keys = jnp.concatenate([ka, kb], axis=1)
-            if b == 0:
-                first_key[g] = keys[:1]
-            keys = jnp.where(alive_row, keys, first_key[g])
+            keys = jnp.where(alive_row, keys, 0.0)
             k_ref[g, rows, :] = keys.astype(BF)
-            qq = scaled * scaled
-            kk = keys * keys
-            for h in range(4):
-                mine = (lane % 128) // HALF == h
-                qn = jnp.max(jnp.sum(jnp.where(mine, qq, 0.0), axis=1, keepdims=True), axis=0, keepdims=True)
-                kn = jnp.max(jnp.sum(jnp.where(mine, kk, 0.0), axis=1, keepdims=True), axis=0, keepdims=True)
-                qmost[4 * g + h] = jnp.maximum(qmost[4 * g + h], qn)
-                kmost[4 * g + h] = jnp.maximum(kmost[4 * g + h], kn)
+            kinds.append(longest(scaled))
+            kinds.append(longest(keys))
         values = lax.dot_general(wv, normed, (((0,), (1,)), ((), ())), preferred_element_type=F32)
         values = jnp.where(alive_col, values, 0.0)
-        vmost = jnp.maximum(vmost, jnp.max(jnp.max(jnp.abs(values), axis=0, keepdims=True), axis=1, keepdims=True))
+        vmost = jnp.max(jnp.max(jnp.abs(values), axis=0, keepdims=True), axis=1, keepdims=True)
+        kinds.append(jnp.broadcast_to(vmost, (1, 128)))
         values = values.astype(BF)
-        ones = jnp.broadcast_to(jnp.where(alive_col, 1.0, 0.0), (VROWS - DH, rows_each)).astype(BF)
+        ones = jnp.broadcast_to(jnp.where(alive_col, 1.0, 0.0), (VROWS - DH, count)).astype(BF)
         for h in range(HEADS):
             v_ref[h, :DH, rows] = values[h * DH : (h + 1) * DH]
             v_ref[h, DH:, rows] = ones
-    for h in range(HEADS):
-        bound = jnp.maximum(bound, qmost[h] * kmost[h])
-    fits = (jnp.max(bound) * 1.05 < SAFE * SAFE) & (jnp.max(vmost) < VSAFE)
+        if stats is None:
+            return kinds
+        return [jnp.maximum(p, n) for p, n in zip(stats, kinds)]
+
+    stats = None
+    for dy in (1, 3, 0, 2):
+        stats = project(dy, stats)
+    for n, row in enumerate(stats):
+        most_ref[n : n + 1, :] = row
+
+    def finish(i, carry):
+        copy(i).wait_send()
+        return carry
+
+    lax.fori_loop(1, seq, finish, 0)
+
+
+def exchange(computed, lengths, gain, wqkv):
+    seq = lax.axis_size("seq")
+    bands, frames, width = computed.shape
+    count = seq * frames
+    cosine, sines = rotary_tables(np.arange(count), 4)
+    dma = pltpu.SemaphoreType.DMA
+    return pl.pallas_call(
+        functools.partial(exchange_kernel, seq),
+        out_shape=(
+            jax.ShapeDtypeStruct((seq, frames, width), BF),
+            jax.ShapeDtypeStruct((2, count // 2, GROUP), BF),
+            jax.ShapeDtypeStruct((2, count // 2, GROUP), BF),
+            jax.ShapeDtypeStruct((2, count, GROUP), BF),
+            jax.ShapeDtypeStruct((HEADS, VROWS, count), BF),
+            jax.ShapeDtypeStruct((5, 128), F32),
+        ),
+        in_specs=[smem()] + [whole()] * 5,
+        out_specs=[whole()] * 6,
+        scratch_shapes=[VMEM((seq, frames, width), BF), dma((seq,)), dma((seq,))],
+        compiler_params=pltpu.CompilerParams(collective_id=1, has_side_effects=True, vmem_limit_bytes=TIME_LIMIT),
+        cost_estimate=pl.CostEstimate(flops=4 * 10**9, bytes_accessed=10 * 10**6, transcendentals=0),
+    )(lengths, computed, gain[None], wqkv, jnp.asarray(cosine), jnp.asarray(sines))
+
+
+TIME_LIMIT = 36 * 2**20
+
+
+def time_kernel(chunk, length_ref, most_ref, x_ref, wout_ref, q_ref, k_ref, v_ref, out_ref, heads_ref):
+    owners, frames, width = x_ref.shape
+    half = frames // 2
+    lane = lax.broadcasted_iota(jnp.int32, (1, GROUP), 1)
+    bound = jnp.maximum(most_ref[0:1, :] * most_ref[1:2, :], most_ref[2:3, :] * most_ref[3:4, :])
+    fits = (jnp.max(bound) * 1.05 < SAFE * SAFE) & (jnp.max(most_ref[4:5, :]) < VSAFE)
 
     def attend(shift):
-        def block(qb, carry):
-            rows = pl.ds(pl.multiple_of(qb * columns, columns), columns)
-
-            def head(h, inner_carry):
-                g = h // 4
-                mine = (lane % 128) // HALF == h % 4
-                queries = jnp.where(mine, q_ref[g, rows, :], jnp.zeros((), BF))
-                scores = lax.dot_general(k_ref[g], queries, NT, preferred_element_type=F32)
-                if shift:
-                    scores = scores - jnp.max(scores, axis=0, keepdims=True)
-                powers = jnp.exp2(scores).astype(BF)
-                mixed = jnp.dot(v_ref[h], powers, preferred_element_type=F32)
-                mixed = mixed[:DH] / mixed[DH : DH + 1]
-                heads_ref[pl.ds(pl.multiple_of(h * DH, DH), DH), :] = mixed.astype(BF)
-                return inner_carry
-
-            lax.fori_loop(0, HEADS, head, 0)
-            projected = lax.dot_general(heads_ref[...], wout_ref[...], TN, preferred_element_type=F32)
-            out_ref[rows, :] = (x_ref[rows, :].astype(F32) + projected).astype(BF)
+        def head(h, carry):
+            g = h // 4
+            mine = (lane % 128) // HALF == h % 4
+            queries = jnp.where(mine, q_ref[g], jnp.zeros((), BF))
+            scores = lax.dot_general(k_ref[g], queries, NT, preferred_element_type=F32)
+            if shift:
+                alive = lax.broadcasted_iota(jnp.int32, (owners * frames, 1), 0) < length_ref[0]
+                scores = jnp.where(alive, scores, -1e30)
+                scores = scores - jnp.max(scores, axis=0, keepdims=True)
+            powers = jnp.exp2(scores).astype(BF)
+            mixed = jnp.dot(v_ref[h], powers, preferred_element_type=F32)
+            mixed = mixed[:DH] / mixed[DH : DH + 1]
+            heads_ref[pl.ds(pl.multiple_of(h * DH, DH), DH), :] = mixed.astype(BF)
             return carry
 
-        lax.fori_loop(0, frames // columns, block, 0)
+        lax.fori_loop(0, HEADS, head, 0)
 
     @pl.when(fits)
     def _():
@@ -205,31 +300,34 @@
     def _():
         attend(True)
 
-
-def time_attention(sequence, lengths, gain, wqkv, wout):
-    frames, width = sequence.shape
-    columns = min(1024, frames)
-    cosine, sines = rotary_tables(np.arange(frames), 4)
+    projected = lax.dot_general(heads_ref[...], wout_ref[...], TN, preferred_element_type=F32)
+    before = x_ref[:, chunk * half : (chunk + 1) * half, :].astype(F32)
+    out_ref[...] = (before + projected.reshape(owners, half, width)).astype(BF)
+
+
+def time_attention(chunk, lengths, most, sequence, wout, q, k, v):
+    owners, frames, width = sequence.shape
     return pl.pallas_call(
-        functools.partial(time_kernel, columns),
-        out_shape=jax.ShapeDtypeStruct((frames, width), BF),
+        functools.partial(time_kernel, chunk),
+        out_shape=jax.ShapeDtypeStruct((owners, frames // 2, width), BF),
         in_specs=[smem()] + [whole()] * 6,
         out_specs=whole(),
-        scratch_shapes=[
-            VMEM((2, frames, GROUP), BF),
-            VMEM((2, frames, GROUP), BF),
-            VMEM((HEADS, VROWS, frames), BF),
-            VMEM((HEADS * DH, columns), BF),
-        ],
-        compiler_params=pltpu.CompilerParams(vmem_limit_bytes=LIMIT),
-        cost_estimate=pl.CostEstimate(flops=4 * 10**10, bytes_accessed=6 * 10**6, transcendentals=0),
-    )(lengths, sequence, gain[None], wqkv, wout, jnp.asarray(cosine), jnp.asarray(sines))
+        scratch_shapes=[VMEM((HEADS * DH, owners * frames // 2), BF)],
+        compiler_params=pltpu.CompilerParams(vmem_limit_bytes=TIME_LIMIT),
+        cost_estimate=pl.CostEstimate(flops=2 * 10**10, bytes_accessed=8 * 10**6, transcendentals=0),
+    )(lengths, most, sequence, wout, q, k, v)
 
 
 FRAMES_EACH = 16
 
 
-def band_kernel(place_ref, x_ref, gain_ref, wqkv_ref, wout_ref, cot_ref, cos_ref, sin_ref, out_ref, grad_ref, heads_ref):
+def band_kernel(chunk, chunks, place_ref, x_ref, gain_ref, wqkv_ref, wout_ref, cot_ref, cos_ref, sin_ref, *rest):
+    if chunk:
+        before_ref, _, out_ref, grad_ref, heads_ref = rest
+        grad_ref[...] = before_ref[...]
+    else:
+        out_ref, grad_ref, heads_ref = rest
+        grad_ref[...] = jnp.zeros_like(grad_ref)
     bands, frames, width = x_ref.shape
     inner = HEADS * DH
     rows = bands * FRAMES_EACH
@@ -240,12 +338,11 @@
     wk = [split_halves(wqkv_ref[:, inner + g * GROUP : inner + (g + 1) * GROUP]) for g in range(2)]
     wv = wqkv_ref[:, 2 * inner :]
     length = place_ref[0]
-    base = place_ref[1]
+    base = place_ref[1] + chunk * frames
     to = lax.broadcasted_iota(jnp.int32, (rows, rows), 0)
     src = lax.broadcasted_iota(jnp.int32, (rows, rows), 1)
     order = (src == to % bands * FRAMES_EACH + to // bands).astype(F32).astype(BF)
     same = lax.broadcasted_iota(jnp.int32, (half, half), 0) // bands == lax.broadcasted_iota(jnp.int32, (half, half), 1) // bands
-    grad_ref[...] = jnp.zeros_like(grad_ref)
 
     def block(i, carry):
         piece = x_ref[:, pl.ds(pl.multiple_of(i * FRAMES_EACH, FRAMES_EACH), FRAMES_EACH), :].reshape(rows, width)
@@ -289,23 +386,37 @@
     lax.fori_loop(0, frames // FRAMES_EACH, block, 0)
 
 
-def band_attention(returned, place, gain, wqkv, wout, cotangent):
+def band_attention(chunk, chunks, returned, place, gain, wqkv, wout, cotangent, output=None, grad=None):
     bands, frames, width = returned.shape
     inner = HEADS * DH
     rows = bands * FRAMES_EACH
     cosine, sines = rotary_tables(np.tile(np.arange(bands), FRAMES_EACH), 4)
+    part = pl.BlockSpec((frames * bands, width), lambda i: (chunk, 0))
+
+    def full(*shape):
+        return pl.BlockSpec(shape, lambda i: (0,) * len(shape))
+
+    operands = [place, returned, gain[None], wqkv, wout, cotangent, jnp.asarray(cosine), jnp.asarray(sines)]
+    specs = [smem(), full(*returned.shape), full(1, width), full(*wqkv.shape), full(*wout.shape), part, full(*cosine.shape), full(*sines.shape)]
+    aliases = {}
+    if chunk:
+        operands += [grad, output]
+        specs += [full(inner, width), pl.BlockSpec(memory_space=pl.ANY)]
+        aliases = {len(operands) - 1: 0}
     return pl.pallas_call(
-        band_kernel,
+        functools.partial(band_kernel, chunk, chunks),
+        grid=(1,),
         out_shape=(
-            jax.ShapeDtypeStruct((frames * bands, width), BF),
+            jax.ShapeDtypeStruct((frames * chunks * bands, width), BF),
             jax.ShapeDtypeStruct((inner, width), F32),
         ),
-        in_specs=[smem()] + [whole()] * 7,
-        out_specs=(whole(), whole()),
+        in_specs=specs,
+        out_specs=(part, full(inner, width)),
         scratch_shapes=[VMEM((rows, inner), BF)],
-        compiler_params=pltpu.CompilerParams(vmem_limit_bytes=LIMIT),
-        cost_estimate=pl.CostEstimate(flops=10**10, bytes_accessed=7 * 10**6, transcendentals=0),
-    )(place, returned, gain[None], wqkv, wout, cotangent.reshape(frames * bands, width), jnp.asarray(cosine), jnp.asarray(sines))
+        input_output_aliases=aliases,
+        compiler_params=pltpu.CompilerParams(vmem_limit_bytes=TIME_LIMIT),
+        cost_estimate=pl.CostEstimate(flops=10**10, bytes_accessed=5 * 10**6, transcendentals=0),
+    )(*operands)
 
 
 def sum_kernel(seq, songs, part_ref, out_ref, small, got, mid, full, send1, recv1, send2, recv2, send3, recv3):
@@ -406,11 +517,15 @@
     local_frames = spectrum.shape[1]
     bands, width = embed_bias.shape
     computed = embed(spectrum[0], widths, bin_gain, embed_weight, embed_bias)
-    owned = lax.all_to_all(computed, "seq", split_axis=0, concat_axis=1, tiled=True)
-    timed = time_attention(owned[0], lengths, time_gain, time_qkv, time_out)
-    returned = lax.all_to_all(timed.reshape(-1, local_frames, width), "seq", split_axis=0, concat_axis=0, tiled=True)
     place = jnp.stack([lengths[0], lax.axis_index("seq") * local_frames]).astype(jnp.int32)
-    output, partial = band_attention(returned, place, band_gain, band_qkv, band_out, cotangent[0])
+    tangent = cotangent.reshape(local_frames * bands, width)
+    owned, early, late, k, v, most = exchange(computed, lengths, time_gain, time_qkv)
+    first = time_attention(0, lengths, most, owned, time_out, early, k, v)
+    first = lax.all_to_all(first, "seq", split_axis=0, concat_axis=0, tiled=True)
+    second = time_attention(1, lengths, most, owned, time_out, late, k, v)
+    second = lax.all_to_all(second, "seq", split_axis=0, concat_axis=0, tiled=True)
+    output, partial = band_attention(0, 2, first, place, band_gain, band_qkv, band_out, tangent)
+    output, partial = band_attention(1, 2, second, place, band_gain, band_qkv, band_out, tangent, output, partial)
     gradient = gradient_sum(partial)
     return output.reshape(1, local_frames, bands, width), gradient
 

time: 190 us -> 180 us (0.947)
  waiting for transfers between devices: 42 us -> 1.03 us
  Pallas kernels: 118 us -> 136 us
  local copies, waits for them, and re-layouts: 11.6 us -> 26.7 us
  starting transfers between devices: 14.5 us -> 12.5 us
    all_to_all x2, waiting for transfers between devices: 42 us -> 1.03 us  [the longest x1 1.03 us: per_device(): lax.all_to_all(second, 'seq', split_axis=0, concat_axis=0, tiled=True)]
    unnamed x9 -> x51, local copies, waits for them, and re-layouts: 4.38 us -> 24.5 us
    pallas_call x3 -> x6, Pallas kernels: 90.6 us -> 108 us  [the longest x2 53.5 us: time_attention(): pl.pallas_call(functools.partial(time_kernel, chunk), out_shape=jax.Shape...]
    slice x3 -> x0, local copies, waits for them, and re-layouts: 2.1 us -> none  [the longest x1 0.72 us: embed(): x_tail = jnp.pad(spectrum[:, main:], ((0, 0), (0, 128 - tail)))]
    all_to_all x2, starting transfers between devices: 14.5 us -> 12.5 us  [the longest x1 7.52 us: per_device(): lax.all_to_all(second, 'seq', split_axis=0, concat_axis=0, tiled=True)]
  transfers between devices with their start and end apart: 2 -> 2, of which waited for: 2 -> 1; matrix products, arithmetic and copies ran while one was open for 1% -> 0% of each run, Pallas kernels for 0% -> 20%
where the time goes in v2:
time: 180 us; the launch traced here: 179 us
  Pallas kernels  136 us (76%)
  local copies, waits for them, and re-layouts  26.7 us (15%)
  starting transfers between devices  12.5 us (7%)
    pallas_call x2, Pallas kernels, time_attention(): pl.pallas_call(functools.partial(time_kernel, chunk), out_shape=jax.Shape...  53.5 us
    pallas_call x1, Pallas kernels, exchange(): pl.pallas_call(functools.partial(exchange_kernel, seq), out_shape=(jax.Sh...  30.4 us
    pallas_call x1, Pallas kernels, gradient_sum(): pl.pallas_call(functools.partial(sum_kernel, seq, songs), out_shape=jax.S...  27.9 us
    unnamed x51, local copies, waits for them, and re-layouts  24.5 us
    pallas_call x2, Pallas kernels, band_attention(): pl.pallas_call(functools.partial(band_kernel, chunk, chunks), grid=(1,),...  18.2 us
    all_to_all x1, starting transfers between devices, per_device(): lax.all_to_all(second, 'seq', split_axis=0, concat_axis=0, tiled=True)  7.52 us
    pallas_call x1, Pallas kernels, embed(): pl.pallas_call(functools.partial(embed_kernel, bands), out_shape=jax.Shap...  6.13 us
    all_to_all x1, starting transfers between devices, per_device(): lax.all_to_all(first, 'seq', split_axis=0, concat_axis=0, tiled=True)  4.96 us
  transfers between devices with their start and end apart: 2, of which 1 were waited for; matrix products, arithmetic and copies ran while one was open for 0% of the time, Pallas kernels for 20%

profile of v2, /device:TPU:1, one launch (start us, length us, event | category | flops | bytes accessed | tf_op | source)
XLA Modules:
  0.0 178.8 jit_solution(7077948295817479178)
XLA Ops:
  1.3 0.7 copy.23
  2.0 0.1 reduce-window.9
  2.1 0.1 reduce
  2.2 0.7 fusion.1
  2.9 0.8 broadcast_in_dim.10.gain_ref
  3.7 0.7 broadcast_in_dim.11.gain_ref
  4.3 0.0 copy-start
  4.4 2.8 %copy-done = bf16[8196,384]{1,0:T(8,128)(2,1)S(1)} copy-done((bf16[8196,384]{1,0:T(8,128)(2,1)S(1)}, bf16[8196,384]{1,0:T(8,128)(2,1)}, u32[]{:S(2)}) %copy-start) | copy-done | bytes 6294552
  7.1 0.0 copy-start.1
  7.1 1.2 copy-done.1
  8.4 0.0 copy-start.3
  8.4 0.8 copy-done.3
  9.2 0.0 copy-start.5
  9.2 0.0 copy-start.10
  9.2 0.0 copy-start.11
  9.2 6.1 %shard_map.194.bands_ref = bf16[32,64,384]{2,1,0:T(8,128)(2,1)S(1)} custom-call(s32[3,32]{1,0:T(4,128)S(1)} %pad_add_fusion.meta_ref, bf16[64,8196]{1,0:T(8,128)(2,1)S(1)} %bitcast.11, f32[1,8196]{1,0:T(1,128)S(1)} %broadcast_in_dim.10.gain_ref, bf16[8196,384]{1,0:T(8,128)(2,1)S(1)} %copy-done, f32[32,384]{1,0:T(8,128)S(1)} %copy-done.3), custom_call_target="tpu_custom_call" | custom-call | flops 2000000000 | bytes 9000000 | tf_op jit(solution)/shard_map/pallas_call | solution.py:116
  15.3 0.0 copy-done.5
  15.3 0.0 copy-done.10
  15.3 0.0 copy-done.11
  15.3 0.0 copy-start.8
  15.4 30.4 %shard_map.195 = (bf16[32,64,384]{2,1,0:T(8,128)(2,1)S(1)}, bf16[2,1024,256]{2,1,0:T(8,128)(2,1)S(1)}, bf16[2,1024,256]{2,1,0:T(8,128)(2,1)S(1)}, bf16[2,2048,25...) custom-call(s32[1]{0:T(128)S(6)} %copy.26.length_ref, ...), custom_call_target="tpu_custom_call" | custom-call | flops 4000000000 | bytes 10000000 | tf_op jit(solution)/shard_map/pallas_call | solution.py:249
  45.8 0.0 copy-start.20
  45.8 1.0 copy-done.20
  46.8 0.0 copy-done.8
  46.8 27.1 %shard_map.197 = bf16[32,32,384]{2,1,0:T(8,128)(2,1)} custom-call(s32[1]{0:T(128)S(6)} %copy.26.length_ref, f32[5,128]{1,0:T(8,128)S(1)} %get-tuple-element.12.most_ref, bf16[32,64,384]{2,1,0:T(8,128)(2,1)S(1)} %get-tuple-element.13.x_ref, bf16[512,384]{1,0:T(8,128)(2,1)S(1)} %copy-done.8, bf16[2,1024,256]{2,1,0:T(8,128)(2,1)S(1)} %get-tuple-element.17.q_ref, ...), custom_call_target="tpu_custom_call" | custom-call | flops 20000000000 | bytes 8000000 | tf_op jit(solution)/shard_map/pallas_call | solution.py:310
  73.9 0.0 copy-start.16
  73.9 1.5 copy-done.16
  75.4 1.4 copy-done.18
  76.7 5.0 %all-to-all-start.1 = ((bf16[32,32,384]{2,1,0:T(8,128)(2,1)}), bf16[32,32,384]{2,1,0:T(8,128)(2,1)S(1)}, u32[]{:S(2)}, u32[]{:S(2)}) async-start(bf16[32,32,384]{2,1,0:T(8,128)(2,1)} %shard_map.197), calls=%async_computation.1 | async-start | bytes 1572864 | tf_op jit(solution)/shard_map/all_to_all | solution.py:524
  81.7 0.0 copy-start.17
  81.7 1.7 copy-done.17
  83.5 0.0 copy-start.19
  83.5 1.6 copy-done.19
  85.0 1.2 copy-done.21
  86.3 0.0 copy-start.24
  86.3 0.0 copy-start.9
  86.3 26.4 %shard_map.196 = bf16[32,32,384]{2,1,0:T(8,128)(2,1)} custom-call(s32[1]{0:T(128)S(6)} %copy.26.length_ref, f32[5,128]{1,0:T(8,128)S(1)} %get-tuple-element.12.most_ref, bf16[32,64,384]{2,1,0:T(8,128)(2,1)S(1)} %get-tuple-element.13.x_ref, bf16[512,384]{1,0:T(8,128)(2,1)S(1)} %copy-done.8, bf16[2,1024,256]{2,1,0:T(8,128)(2,1)S(1)} %copy-done.21, ...), custom_call_target="tpu_custom_call" | custom-call | flops 20000000000 | bytes 8000000 | tf_op jit(solution)/shard_map/pallas_call | solution.py:310
  112.7 0.0 copy-start.4
  112.7 0.0 copy-done.24
  112.7 0.1 pad_add_fusion.1.place_ref
  112.8 0.0 all-to-all-done.1.x_ref
  112.8 7.5 %all-to-all-start = ((bf16[32,32,384]{2,1,0:T(8,128)(2,1)}), bf16[32,32,384]{2,1,0:T(8,128)(2,1)S(1)}, u32[]{:S(2)}, u32[]{:S(2)}) async-start(bf16[32,32,384]{2,1,0:T(8,128)(2,1)} %shard_map.196), calls=%async_computation | async-start | bytes 1572864 | tf_op jit(solution)/shard_map/all_to_all | solution.py:526
  120.3 0.0 copy-done.9
  120.3 0.0 copy-done.4
  120.3 0.0 copy-start.6
  120.3 1.3 copy-done.6
  121.6 0.0 copy-start.12
  121.6 0.9 copy-done.12
  122.5 0.9 copy-done.14
  123.5 9.1 %shard_map.198 = (bf16[2048,384]{1,0:T(8,128)(2,1)}, f32[512,384]{1,0:T(8,128)S(1)}) custom-call(s32[2]{0:T(128)S(1)} %pad_add_fusion.1.place_ref, bf16[32,32,384]{2,1,0:T(8,128)(2,1)S(1)} %all-to-all-done.1.x_ref, f32[1,384]{1,0:T(1,128)S(1)} %broadcast_in_dim.12.gain_ref, bf16[384,1536]{1,0:T(8,128)(2,1)S(1)} %copy-done.6, bf16[512,384]{1,0:T(8,128)(2,1)S(1)} %copy-done.9, ...), custom_call_target="tpu_custom_call" | custom-call | flops 10000000000 | bytes 5000000 | tf_op jit(solution)/shard_map/pallas_call | solution.py:406
  132.6 0.0 copy-start.22
  132.6 0.9 copy-done.22
  133.5 1.0 all-to-all-done.x_ref
  134.5 0.0 copy-start.7
  134.5 1.3 copy-done.7
  135.8 0.0 copy-start.13
  135.8 0.9 copy-done.13
  136.7 0.0 copy-start.15
  136.7 0.9 copy-done.15
  137.7 1.1 copy-done.23
  138.8 9.1 %shard_map.199 = (bf16[2048,384]{1,0:T(8,128)(2,1)}, f32[512,384]{1,0:T(8,128)S(1)}) custom-call(s32[2]{0:T(128)S(1)} %pad_add_fusion.1.place_ref, bf16[32,32,384]{2,1,0:T(8,128)(2,1)S(1)} %all-to-all-done.x_ref, f32[1,384]{1,0:T(1,128)S(1)} %broadcast_in_dim.12.gain_ref, bf16[384,1536]{1,0:T(8,128)(2,1)S(1)} %copy-done.7, ...), custom_call_target="tpu_custom_call", output_to_operand_aliasing={{0}: (9, {})} | custom-call | flops 10000000000 | bytes 5000000 | tf_op jit(solution)/shard_map/pallas_call | solution.py:406
  147.9 0.9 copy-done.2
  148.8 27.9 %shard_map.200 = f32[512,384]{1,0:T(8,128)} custom-call(f32[512,384]{1,0:T(8,128)} %copy-done.2), custom_call_target="tpu_custom_call" | custom-call | flops 10000000 | bytes 4000000 | tf_op jit(solution)/shard_map/pallas_call | solution.py:499
  176.7 2.1 %copy.27 = f32[512,384]{1,0:T(8,128)} copy(f32[512,384]{1,0:T(8,128)} %shard_map.200) | data formatting | bytes 1572864
  (7 shorter events, 0.0 us)
Async XLA Ops:
  4.3 2.8 %copy-start = (bf16[8196,384]{1,0:T(8,128)(2,1)S(1)}, bf16[8196,384]{1,0:T(8,128)(2,1)}, u32[]{:S(2)}) copy-start(bf16[8196,384]{1,0:T(8,128)(2,1)} %w_ref.1) | copy-start | bytes 18883588
  7.1 1.2 copy-start.1
  8.4 0.8 copy-start.3
  9.2 6.1 %copy-start.5 = (bf16[384,1536]{1,0:T(8,128)(2,1)S(1)}, bf16[384,1536]{1,0:T(8,128)(2,1)}, u32[]{:S(2)}) copy-start(bf16[384,1536]{1,0:T(8,128)(2,1)} %wqkv_ref.3) | copy-start | bytes 3538948
  9.2 6.2 %copy-start.10 = (f32[2048,128]{1,0:T(8,128)S(1)}, f32[2048,128]{1,0:T(8,128)}, u32[]{:S(2)}) copy-start(f32[2048,128]{1,0:T(8,128)} %constant.37.clone.cos_ref) | copy-start | bytes 3145732
  9.2 6.2 %copy-start.11 = (f32[2048,128]{1,0:T(8,128)S(1)}, f32[2048,128]{1,0:T(8,128)}, u32[]{:S(2)}) copy-start(f32[2048,128]{1,0:T(8,128)} %constant.38.clone.sin_ref) | copy-start | bytes 3145732
  15.3 31.4 %copy-start.8 = (bf16[512,384]{1,0:T(8,128)(2,1)S(1)}, bf16[512,384]{1,0:T(8,128)(2,1)}, u32[]{:S(2)}) copy-start(bf16[512,384]{1,0:T(8,128)(2,1)} %wout_ref.5) | copy-start | bytes 1179652
  45.8 1.0 copy-start.20
  73.9 1.5 copy-start.16
  75.4 1.4 copy-start.18
  76.7 36.0 %all-to-all-start.1 = ((bf16[32,32,384]{2,1,0:T(8,128)(2,1)}), bf16[32,32,384]{2,1,0:T(8,128)(2,1)S(1)}, u32[]{:S(2)}, u32[]{:S(2)}) async-start(bf16[32,32,384]{2,1,0:T(8,128)(2,1)} %shard_map.197), calls=%async_computation.1 | async-start | bytes 1572864 | tf_op jit(solution)/shard_map/all_to_all | solution.py:524
  81.7 1.7 copy-start.17
  83.5 1.6 copy-start.19
  85.0 1.2 copy-start.21
  86.3 26.4 %copy-start.24 = (f32[384]{0:T(512)S(1)}, f32[384]{0:T(512)}, u32[]{:S(2)}) copy-start(f32[384]{0:T(512)} %param.28) | copy-start | bytes 4612
  86.3 34.0 %copy-start.9 = (bf16[512,384]{1,0:T(8,128)(2,1)S(1)}, bf16[512,384]{1,0:T(8,128)(2,1)}, u32[]{:S(2)}) copy-start(bf16[512,384]{1,0:T(8,128)(2,1)} %wout_ref.7) | copy-start | bytes 1179652
  112.7 7.6 %copy-start.4 = (bf16[1,64,32,384]{3,2,1,0:T(8,128)(2,1)S(1)}, bf16[1,64,32,384]{3,2,1,0:T(8,128)(2,1)}, u32[]{:S(2)}) copy-start(bf16[1,64,32,384]{3,2,1,0:T(8,128)(2,1)} %param.31) | copy-start | bytes 4718596
  112.8 21.7 %all-to-all-start = ((bf16[32,32,384]{2,1,0:T(8,128)(2,1)}), bf16[32,32,384]{2,1,0:T(8,128)(2,1)S(1)}, u32[]{:S(2)}, u32[]{:S(2)}) async-start(bf16[32,32,384]{2,1,0:T(8,128)(2,1)} %shard_map.196), calls=%async_computation | async-start | bytes 1572864 | tf_op jit(solution)/shard_map/all_to_all | solution.py:526
  120.3 1.3 copy-start.6
  121.6 0.9 copy-start.12
  122.5 0.9 copy-start.14
  132.6 0.9 copy-start.22
  134.5 1.3 copy-start.7
  135.8 0.9 copy-start.13
  136.7 0.9 copy-start.15
  137.7 1.1 copy-start.23
  147.9 0.9 copy-start.2

commit v3 on v2

--- a/solution.py
+++ b/solution.py
@@ -65,14 +65,18 @@
 NARROW = 640
 
 
-def embed_kernel(bands, meta_ref, x_ref, gain_ref, w_ref, bias_ref, out_ref):
+def embed_kernel(bands, widths_ref, x_ref, gain_ref, w_ref, bias_ref, out_ref, starts_ref):
     limit = x_ref.shape[1]
     main = limit // 128 * 128
+    total = 0
+    for k in range(bands):
+        starts_ref[k] = total
+        total = total + widths_ref[k] * 4
 
     def band(k, size):
-        first = meta_ref[0, k]
-        count = meta_ref[1, k]
-        begin = pl.multiple_of(jnp.minimum(meta_ref[2, k], (main - size) // 128) * 128, 128)
+        first = starts_ref[k]
+        count = widths_ref[k] * 4
+        begin = pl.multiple_of(jnp.minimum(first // 128, (main - size) // 128) * 128, 128)
         window = pl.ds(begin, size)
         entry = lax.broadcasted_iota(jnp.int32, (1, size), 1) + begin
         piece = x_ref[:, window].astype(F32)
@@ -89,9 +93,9 @@
         out_ref[k] = summed.astype(BF)
 
     def step(i, carry):
-        narrow = meta_ref[1, 4 * i] <= NARROW - 124
+        narrow = widths_ref[4 * i] * 4 <= NARROW - 124
         for j in range(1, 4):
-            narrow = narrow & (meta_ref[1, 4 * i + j] <= NARROW - 124)
+            narrow = narrow & (widths_ref[4 * i + j] * 4 <= NARROW - 124)
 
         @pl.when(narrow)
         def _():
@@ -111,16 +115,15 @@
 def embed(spectrum, widths, bin_gain, embed_weight, embed_bias):
     frames, feature_count = spectrum.shape
     bands, width = embed_bias.shape
-    starts = (jnp.cumsum(widths) - widths) * 4
-    meta = jnp.stack([starts, widths * 4, starts // 128]).astype(jnp.int32)
     return pl.pallas_call(
         functools.partial(embed_kernel, bands),
         out_shape=jax.ShapeDtypeStruct((bands, frames, width), BF),
         in_specs=[smem()] + [whole()] * 4,
         out_specs=whole(),
+        scratch_shapes=[pltpu.SMEM((bands,), jnp.int32)],
         compiler_params=pltpu.CompilerParams(vmem_limit_bytes=32 * 2**20),
         cost_estimate=pl.CostEstimate(flops=2 * 10**9, bytes_accessed=9 * 10**6, transcendentals=0),
-    )(meta, spectrum, bin_gain[None], embed_weight, embed_bias)
+    )(widths, spectrum, bin_gain[None], embed_weight, embed_bias)
 
 
 VROWS = 80
@@ -264,7 +267,7 @@
     )(lengths, computed, gain[None], wqkv, jnp.asarray(cosine), jnp.asarray(sines))
 
 
-TIME_LIMIT = 36 * 2**20
+TIME_LIMIT = 28 * 2**20
 
 
 def time_kernel(chunk, length_ref, most_ref, x_ref, wout_ref, q_ref, k_ref, v_ref, out_ref, heads_ref):
@@ -321,213 +324,229 @@
 FRAMES_EACH = 16
 
 
-def band_kernel(chunk, chunks, place_ref, x_ref, gain_ref, wqkv_ref, wout_ref, cot_ref, cos_ref, sin_ref, *rest):
-    if chunk:
-        before_ref, _, out_ref, grad_ref, heads_ref = rest
-        grad_ref[...] = before_ref[...]
-    else:
-        out_ref, grad_ref, heads_ref = rest
-        grad_ref[...] = jnp.zeros_like(grad_ref)
-    bands, frames, width = x_ref.shape
+def finish_kernel(
+    seq, songs, length_ref, early_ref, later_ref, gain_ref, wqkv_ref, wout_ref, cot_hbm, cos_ref, sin_ref,
+    out_hbm, sum_ref, got, cot_ref, heads_ref, x_ref, feat_ref, grad_ref, halves, half_in, parts, parts_in, mid, full,
+    cot_sem, out_sem, send_sem, recv_sem, core_send, core_recv, plane_send, plane_recv, song_send, song_recv, back_send, back_recv, last_send, last_recv,
+):
+    bands, chunk, width = early_ref.shape
     inner = HEADS * DH
     rows = bands * FRAMES_EACH
+    blocks = chunk // FRAMES_EACH
     half = 256
+    me = lax.axis_index("seq")
+    song = lax.axis_index("song")
+    y, x, core = me // 8, me // 2 % 4, me % 2
+
+    def other(i):
+        return (y + i // 8) % 4 * 8 + (x + i // 2 % 4) % 4 * 2 + (core + i % 2) % 2
+
+    cot_copy = pltpu.make_async_copy(cot_hbm, cot_ref, cot_sem)
+    cot_copy.start()
+    barrier = pltpu.get_barrier_semaphore()
+
+    def greet(i, carry):
+        pl.semaphore_signal(barrier, inc=1, device_id=(other(i), song), device_id_type=MESH)
+        return carry
+
+    lax.fori_loop(1, seq, greet, 0)
+    for d in range(1, songs):
+        pl.semaphore_signal(barrier, inc=1, device_id=(me, (song + d) % songs), device_id_type=MESH)
+
     lane = lax.broadcasted_iota(jnp.int32, (1, GROUP), 1)
-    lane128 = lax.broadcasted_iota(jnp.int32, (1, 128), 1)
     wq = [split_halves(wqkv_ref[:, g * GROUP : (g + 1) * GROUP]) for g in range(2)]
     wk = [split_halves(wqkv_ref[:, inner + g * GROUP : inner + (g + 1) * GROUP]) for g in range(2)]
     wv = wqkv_ref[:, 2 * inner :]
-    length = place_ref[0]
-    base = place_ref[1] + chunk * frames
     to = lax.broadcasted_iota(jnp.int32, (rows, rows), 0)
     src = lax.broadcasted_iota(jnp.int32, (rows, rows), 1)
     order = (src == to % bands * FRAMES_EACH + to // bands).astype(F32).astype(BF)
-    same = lax.broadcasted_iota(jnp.int32, (half, half), 0) // bands == lax.broadcasted_iota(jnp.int32, (half, half), 1) // bands
-
-    def block(i, carry):
-        piece = x_ref[:, pl.ds(pl.multiple_of(i * FRAMES_EACH, FRAMES_EACH), FRAMES_EACH), :].reshape(rows, width)
-        x = jnp.dot(order, piece, preferred_element_type=F32)
-        normed = rms_norm(x, gain_ref[...])
-        cosine = cos_ref[...]
-        sines = sin_ref[...]
-        values = jnp.dot(normed, wv, preferred_element_type=F32)
-        for g in range(2):
-            qa, qb = rope(jnp.dot(normed, wq[g], preferred_element_type=F32), cosine, sines)
-            queries = (jnp.concatenate([qa, qb], axis=1) * (LOG2E * DH**-0.5)).astype(BF)
-            ka, kb = rope(jnp.dot(normed, wk[g], preferred_element_type=F32), cosine, sines)
-            keys = jnp.concatenate([ka, kb], axis=1).astype(BF)
-            for s in range(rows // half):
-                part = slice(s * half, (s + 1) * half)
-                for pair in range(2):
-                    column = (2 * g + pair) * 128
-                    v = values[part, column : column + 128]
-                    outs = []
-                    for odd in range(2):
-                        mine = (lane % 128) // HALF == 2 * pair + odd
-                        masked = jnp.where(mine, queries[part], jnp.zeros((), BF))
-                        scores = lax.dot_general(masked, keys[part], NT, preferred_element_type=F32)
-                        scores = jnp.where(same, scores, -1e30)
-                        powers = jnp.exp2(scores - jnp.max(scores, axis=1, keepdims=True)).astype(BF)
-                        own = (lane128 < DH) if odd == 0 else (lane128 >= DH)
-                        extended = jnp.where(own, v, 1.0).astype(BF)
-                        mixed = jnp.dot(powers, extended, preferred_element_type=F32)
-                        outs.append(mixed / pltpu.roll(mixed, DH, 1))
-                    joined = jnp.where(lane128 < DH, outs[0], outs[1])
-                    heads_ref[part, column : column + 128] = joined.astype(BF)
-        heads = heads_ref[...]
-        projected = jnp.dot(heads, wout_ref[...], preferred_element_type=F32)
-        here = pl.ds(pl.multiple_of(i * rows, rows), rows)
-        out_ref[here, :] = (x + projected).astype(BF)
-        frame = base + i * FRAMES_EACH + lax.broadcasted_iota(jnp.int32, (rows, 1), 0) // bands
-        tangent = jnp.where(frame < length, cot_ref[here, :].astype(F32), 0.0).astype(BF)
-        grad_ref[...] += lax.dot_general(heads, tangent, TN, preferred_element_type=F32)
-        return carry
-
-    lax.fori_loop(0, frames // FRAMES_EACH, block, 0)
-
-
-def band_attention(chunk, chunks, returned, place, gain, wqkv, wout, cotangent, output=None, grad=None):
-    bands, frames, width = returned.shape
+    same = (
+        lax.broadcasted_iota(jnp.int32, (4 * half, half), 0) % half // bands
+        == lax.broadcasted_iota(jnp.int32, (4 * half, half), 1) // bands
+    )
+    grad_ref[...] = jnp.zeros_like(grad_ref)
+    pl.semaphore_wait(barrier, seq - 1 + songs - 1)
+
+    def copy(i):
+        k = other(i)
+        return pltpu.make_async_remote_copy(
+            src_ref=later_ref.at[k], dst_ref=got.at[me], send_sem=send_sem.at[i], recv_sem=recv_sem.at[i],
+            device_id=(k, song), device_id_type=MESH)
+
+    def start(i, carry):
+        copy(seq - i).start()
+        return carry
+
+    def arrive(i, carry):
+        copy(seq - i).wait()
+        return carry
+
+    lax.fori_loop(1, seq, start, 0)
+    got[me] = later_ref[me]
+    length = length_ref[0]
+    cot_copy.wait()
+
+    def attend(source_ref, first):
+        def block(i, carry):
+            piece = source_ref[:, pl.ds(pl.multiple_of(i * FRAMES_EACH, FRAMES_EACH), FRAMES_EACH), :].reshape(rows, width)
+            values_x = jnp.dot(order, piece, preferred_element_type=F32)
+            here = pl.ds(pl.multiple_of((i + first) * rows, rows), rows)
+            x_ref[here, :] = values_x.astype(BF)
+            normed = rms_norm(values_x, gain_ref[...])
+            cosine = cos_ref[...]
+            sines = sin_ref[...]
+            values = jnp.dot(normed, wv, preferred_element_type=F32)
+            joined_groups = []
+            for g in range(2):
+                qa, qb = rope(jnp.dot(normed, wq[g], preferred_element_type=F32), cosine, sines)
+                queries = (jnp.concatenate([qa, qb], axis=1) * (LOG2E * DH**-0.5)).astype(BF)
+                ka, kb = rope(jnp.dot(normed, wk[g], preferred_element_type=F32), cosine, sines)
+                keys = jnp.concatenate([ka, kb], axis=1).astype(BF)
+                pieces = []
+                for s in range(rows // half):
+                    part = slice(s * half, (s + 1) * half)
+                    stacked = jnp.concatenate(
+                        [jnp.where((lane % 128) // HALF == h, queries[part], jnp.zeros((), BF)) for h in range(4)], axis=0)
+                    scores = lax.dot_general(stacked, keys[part], NT, preferred_element_type=F32)
+                    scores = jnp.where(same, scores, -1e30)
+                    powers = jnp.exp2(scores - jnp.max(scores, axis=1, keepdims=True))
+                    mixed = jnp.dot(
+                        powers.astype(BF), values[part, g * GROUP : (g + 1) * GROUP].astype(BF), preferred_element_type=F32)
+                    mixed = mixed / jnp.sum(powers, axis=1, keepdims=True)
+                    joined = mixed[:half]
+                    for h in range(1, 4):
+                        joined = jnp.where(lane // DH == h, mixed[h * half : (h + 1) * half], joined)
+                    pieces.append(joined.astype(BF))
+                joined_groups.append(jnp.concatenate(pieces, axis=0))
+            heads = jnp.concatenate(joined_groups, axis=1)
+            heads_ref[here, :] = heads
+            frame = me * (2 * chunk) + (i + first) * FRAMES_EACH + lax.broadcasted_iota(jnp.int32, (rows, 1), 0) // bands
+            tangent = jnp.where(frame < length, cot_ref[here, :].astype(F32), 0.0).astype(BF)
+            grad_ref[...] += lax.dot_general(heads, tangent, TN, preferred_element_type=F32)
+            return carry
+
+        lax.fori_loop(0, blocks, block, 0)
+
+    def out_copy(i):
+        here = slice(i * rows, (i + 1) * rows)
+        return pltpu.make_async_copy(feat_ref.at[here], out_hbm.at[here], out_sem.at[i])
+
+    def features(i):
+        here = slice(i * rows, (i + 1) * rows)
+        projected = jnp.dot(heads_ref[here, :], wout_ref[...], preferred_element_type=F32)
+        feat_ref[here, :] = (x_ref[here, :].astype(F32) + projected).astype(BF)
+        out_copy(i).start()
+
+    attend(early_ref, 0)
+    lax.fori_loop(1, seq, arrive, 0)
+    attend(got, blocks)
+
+    def remote(src_ref, dst_ref, send, recv, device):
+        return pltpu.make_async_remote_copy(
+            src_ref=src_ref, dst_ref=dst_ref, send_sem=send, recv_sem=recv, device_id=device, device_id_type=MESH)
+
+    twin = (me + 1 - 2 * core, song)
+    plane = [(dy, dx) for dy in range(4) for dx in range(4) if dy or dx]
+
+    def at(dy, dx):
+        return ((y + dy) % 4 * 8 + (x + dx) % 4 * 2 + core, song)
+
+    halves[...] = grad_ref[...].astype(BF).reshape(halves.shape)
+    exchange_half = remote(halves.at[1 - core], half_in, core_send, core_recv, twin)
+    exchange_half.start()
+    exchange_half.wait()
+    parts[...] = (halves[core].astype(F32) + half_in[...].astype(F32)).astype(BF).reshape(parts.shape)
+    copies = [
+        remote(parts.at[(x + dx) % 4 * 4 + (y + dy) % 4], parts_in.at[dx * 4 + dy], plane_send.at[dx * 4 + dy], plane_recv.at[dx * 4 + dy], at(dy, dx))
+        for dy, dx in plane
+    ]
+    for one in copies:
+        one.start()
+    parts_in[0] = parts[x * 4 + y]
+    features(0)
+    features(1)
+    for one in copies:
+        one.wait()
+    total = parts_in[0].astype(F32)
+    for n in range(1, 16):
+        total = total + parts_in[n].astype(F32)
+    mid[song] = total
+    copies = [
+        remote(mid.at[song], mid.at[song], song_send.at[d], song_recv.at[d], (me, (song + d) % songs)) for d in range(1, songs)
+    ]
+    for one in copies:
+        one.start()
+    features(2)
+    for one in copies:
+        one.wait()
+    total = mid[0]
+    for n in range(1, songs):
+        total = total + mid[n]
+    full[core, x * 4 + y] = total.astype(BF)
+    copies = [
+        remote(full.at[core, x * 4 + y], full.at[core, x * 4 + y], back_send.at[dx * 4 + dy], back_recv.at[dx * 4 + dy], at(dy, dx))
+        for dy, dx in plane
+    ]
+    for one in copies:
+        one.start()
+    features(3)
+    for one in copies:
+        one.wait()
+    exchange_half = remote(full.at[core], full.at[core], last_send, last_recv, twin)
+    exchange_half.start()
+    exchange_half.wait()
+    sum_ref[...] = full[...].reshape(inner, width)
+    for i in range(4):
+        out_copy(i).wait()
+
+
+def finish(lengths, early, later, gain, wqkv, wout, cotangent):
+    seq = lax.axis_size("seq")
+    songs = lax.axis_size("song")
+    bands, chunk, width = early.shape
     inner = HEADS * DH
     rows = bands * FRAMES_EACH
+    count = 2 * chunk * bands
     cosine, sines = rotary_tables(np.tile(np.arange(bands), FRAMES_EACH), 4)
-    part = pl.BlockSpec((frames * bands, width), lambda i: (chunk, 0))
-
-    def full(*shape):
-        return pl.BlockSpec(shape, lambda i: (0,) * len(shape))
-
-    operands = [place, returned, gain[None], wqkv, wout, cotangent, jnp.asarray(cosine), jnp.asarray(sines)]
-    specs = [smem(), full(*returned.shape), full(1, width), full(*wqkv.shape), full(*wout.shape), part, full(*cosine.shape), full(*sines.shape)]
-    aliases = {}
-    if chunk:
-        operands += [grad, output]
-        specs += [full(inner, width), pl.BlockSpec(memory_space=pl.ANY)]
-        aliases = {len(operands) - 1: 0}
+    dma = pltpu.SemaphoreType.DMA
+    anywhere = pl.BlockSpec(memory_space=pl.ANY)
     return pl.pallas_call(
-        functools.partial(band_kernel, chunk, chunks),
-        grid=(1,),
-        out_shape=(
-            jax.ShapeDtypeStruct((frames * chunks * bands, width), BF),
-            jax.ShapeDtypeStruct((inner, width), F32),
-        ),
-        in_specs=specs,
-        out_specs=(part, full(inner, width)),
-        scratch_shapes=[VMEM((rows, inner), BF)],
-        input_output_aliases=aliases,
-        compiler_params=pltpu.CompilerParams(vmem_limit_bytes=TIME_LIMIT),
-        cost_estimate=pl.CostEstimate(flops=10**10, bytes_accessed=5 * 10**6, transcendentals=0),
-    )(*operands)
-
-
-def sum_kernel(seq, songs, part_ref, out_ref, small, got, mid, full, send1, recv1, send2, recv2, send3, recv3):
-    me = lax.axis_index("seq")
-    song = lax.axis_index("song")
-    rows = small.shape[1]
-    barrier = pltpu.get_barrier_semaphore()
-
-    def greet(d, carry):
-        pl.semaphore_signal(barrier, inc=1, device_id=(lax.rem(me + d, seq), song), device_id_type=MESH)
-        return carry
-
-    lax.fori_loop(1, seq, greet, 0)
-    for d in range(1, songs):
-        pl.semaphore_signal(barrier, inc=1, device_id=(me, lax.rem(song + d, songs)), device_id_type=MESH)
-    for r in range(seq):
-        small[r] = part_ref[r * rows : (r + 1) * rows, :].astype(BF)
-    pl.semaphore_wait(barrier, seq - 1 + songs - 1)
-
-    def first(d):
-        peer = lax.rem(me + d, seq)
-        return pltpu.make_async_remote_copy(
-            src_ref=small.at[peer], dst_ref=got.at[d], send_sem=send1.at[d], recv_sem=recv1.at[d],
-            device_id=(peer, song), device_id_type=MESH)
-
-    def start1(d, carry):
-        first(d).start()
-        return carry
-
-    def wait1(d, carry):
-        first(d).wait()
-        return carry
-
-    lax.fori_loop(1, seq, start1, 0)
-    got[0] = small[me]
-    lax.fori_loop(1, seq, wait1, 0)
-    total = got[0].astype(F32)
-    for d in range(1, seq):
-        total = total + got[d].astype(F32)
-    mid[song] = total
-    copies = []
-    for d in range(1, songs):
-        copies.append(pltpu.make_async_remote_copy(
-            src_ref=mid.at[song], dst_ref=mid.at[song], send_sem=send2.at[d], recv_sem=recv2.at[d],
-            device_id=(me, lax.rem(song + d, songs)), device_id_type=MESH))
-    for c in copies:
-        c.start()
-    for c in copies:
-        c.wait()
-    total = mid[0]
-    for s in range(1, songs):
-        total = total + mid[s]
-    full[me] = total.astype(BF)
-
-    def third(d):
-        return pltpu.make_async_remote_copy(
-            src_ref=full.at[me], dst_ref=full.at[me], send_sem=send3.at[d], recv_sem=recv3.at[d],
-            device_id=(lax.rem(me + d, seq), song), device_id_type=MESH)
-
-    def start3(d, carry):
-        third(d).start()
-        return carry
-
-    def wait3(d, carry):
-        third(d).wait()
-        return carry
-
-    lax.fori_loop(1, seq, start3, 0)
-    lax.fori_loop(1, seq, wait3, 0)
-    for r in range(seq):
-        out_ref[r * rows : (r + 1) * rows, :] = full[r].astype(F32)
-
-
-def gradient_sum(partial):
-    seq = lax.axis_size("seq")
-    songs = lax.axis_size("song")
-    inner, width = partial.shape
-    rows = inner // seq
-    dma = pltpu.SemaphoreType.DMA
-    return pl.pallas_call(
-        functools.partial(sum_kernel, seq, songs),
-        out_shape=jax.ShapeDtypeStruct((inner, width), F32),
-        in_specs=[whole()],
-        out_specs=whole(),
+        functools.partial(finish_kernel, seq, songs),
+        out_shape=(jax.ShapeDtypeStruct((count, width), BF), jax.ShapeDtypeStruct((inner, width), BF)),
+        in_specs=[smem()] + [whole()] * 5 + [anywhere] + [whole()] * 2,
+        out_specs=(anywhere, whole()),
         scratch_shapes=[
-            VMEM((seq, rows, width), BF),
-            VMEM((seq, rows, width), BF),
-            VMEM((songs, rows, width), F32),
-            VMEM((seq, rows, width), BF),
-            dma((seq,)), dma((seq,)), dma((songs,)), dma((songs,)), dma((seq,)), dma((seq,)),
+            VMEM((bands, chunk, width), BF),
+            VMEM((count, width), BF),
+            VMEM((count, inner), BF),
+            VMEM((count, width), BF),
+            VMEM((count, width), BF),
+            VMEM((inner, width), F32),
+            VMEM((2, inner // 2, width), BF),
+            VMEM((inner // 2, width), BF),
+            VMEM((16, inner // 32, width), BF),
+            VMEM((16, inner // 32, width), BF),
+            VMEM((songs, inner // 32, width), F32),
+            VMEM((2, 16, inner // 32, width), BF),
+            dma, dma((4,)), dma((seq,)), dma((seq,)), dma, dma, dma((16,)), dma((16,)),
+            dma((songs,)), dma((songs,)), dma((16,)), dma((16,)), dma, dma,
         ],
-        compiler_params=pltpu.CompilerParams(collective_id=0, has_side_effects=True, vmem_limit_bytes=LIMIT),
-        cost_estimate=pl.CostEstimate(flops=10**7, bytes_accessed=4 * 10**6, transcendentals=0),
-    )(partial)
+        compiler_params=pltpu.CompilerParams(collective_id=2, has_side_effects=True, vmem_limit_bytes=36 * 2**20),
+        cost_estimate=pl.CostEstimate(flops=10**10, bytes_accessed=7 * 10**6, transcendentals=0),
+    )(lengths, early, later, gain, wqkv, wout, cotangent, jnp.asarray(cosine), jnp.asarray(sines))
 
 
 def per_device(spectrum, widths, lengths, bin_gain, embed_weight, embed_bias, time_gain, time_qkv, time_out, band_gain, band_qkv, band_out, cotangent):
     local_frames = spectrum.shape[1]
     bands, width = embed_bias.shape
     computed = embed(spectrum[0], widths, bin_gain, embed_weight, embed_bias)
-    place = jnp.stack([lengths[0], lax.axis_index("seq") * local_frames]).astype(jnp.int32)
     tangent = cotangent.reshape(local_frames * bands, width)
     owned, early, late, k, v, most = exchange(computed, lengths, time_gain, time_qkv)
     first = time_attention(0, lengths, most, owned, time_out, early, k, v)
     first = lax.all_to_all(first, "seq", split_axis=0, concat_axis=0, tiled=True)
     second = time_attention(1, lengths, most, owned, time_out, late, k, v)
-    second = lax.all_to_all(second, "seq", split_axis=0, concat_axis=0, tiled=True)
-    output, partial = band_attention(0, 2, first, place, band_gain, band_qkv, band_out, tangent)
-    output, partial = band_attention(1, 2, second, place, band_gain, band_qkv, band_out, tangent, output, partial)
-    gradient = gradient_sum(partial)
-    return output.reshape(1, local_frames, bands, width), gradient
+    output, gradient = finish(lengths, first, second, band_gain[None], band_qkv, band_out, tangent)
+    return output.reshape(1, local_frames, bands, width), gradient.astype(F32)
 
 
 def solution(mesh):

time: 180 us -> 169 us (0.939)
  starting transfers between devices: 12.5 us -> 4.97 us
    all_to_all x1 -> x0, starting transfers between devices: 7.52 us -> none  [per_device(): lax.all_to_all(second, 'seq', split_axis=0, concat_axis=0, tiled=True)]
    pallas_call x3 -> x1, Pallas kernels: 46.1 us -> 46.2 us  [finish(): pl.pallas_call(functools.partial(finish_kernel, seq, songs), out_shape=(j...]
  transfers between devices with their start and end apart: 2 -> 1, of which waited for: 1 -> 0; matrix products, arithmetic and copies ran while one was open for 0% -> 0% of each run, Pallas kernels for 20% -> 15%
where the time goes in v3:
time: 169 us; the launch traced here: 168 us
  Pallas kernels  136 us (80%)
  local copies, waits for them, and re-layouts  25 us (15%)
  starting transfers between devices  4.97 us (3%)
    pallas_call x2, Pallas kernels, time_attention(): pl.pallas_call(functools.partial(time_kernel, chunk), out_shape=jax.Shape...  52.8 us
    pallas_call x1, Pallas kernels, finish(): pl.pallas_call(functools.partial(finish_kernel, seq, songs), out_shape=(j...  46.2 us
    pallas_call x1, Pallas kernels, exchange(): pl.pallas_call(functools.partial(exchange_kernel, seq), out_shape=(jax.Sh...  30.4 us
    unnamed x51, local copies, waits for them, and re-layouts  23.5 us
    pallas_call x1, Pallas kernels, embed(): pl.pallas_call(functools.partial(embed_kernel, bands), out_shape=jax.Shap...  5.99 us
    all_to_all x1, starting transfers between devices, per_device(): lax.all_to_all(first, 'seq', split_axis=0, concat_axis=0, tiled=True)  4.97 us
  transfers between devices with their start and end apart: 1, of which 0 were waited for; matrix products, arithmetic and copies ran while one was open for 0% of the time, Pallas kernels for 15%

profile of v3, /device:TPU:1, one launch (start us, length us, event | category | flops | bytes accessed | tf_op | source)
XLA Modules:
  0.0 167.8 jit_solution(14073183066628508684)
XLA Ops:
  1.3 0.8 broadcast_in_dim.9.gain_ref
  2.1 0.7 broadcast_in_dim.10.gain_ref
  2.8 0.0 copy-start
  2.8 2.8 %copy-done = bf16[8196,384]{1,0:T(8,128)(2,1)S(1)} copy-done((bf16[8196,384]{1,0:T(8,128)(2,1)S(1)}, bf16[8196,384]{1,0:T(8,128)(2,1)}, u32[]{:S(2)}) %copy-start) | copy-done | bytes 6294552
  5.5 0.0 copy-start.1
  5.5 1.2 copy-done.1
  6.8 0.0 copy-start.2
  6.8 0.8 copy-done.2
  7.6 0.0 copy-start.3
  7.6 0.7 copy-done.3
  8.2 0.0 copy-start.5
  8.2 0.0 copy-start.10
  8.2 0.0 copy-start.11
  8.2 6.0 %shard_map.176.bands_ref = bf16[32,64,384]{2,1,0:T(8,128)(2,1)S(1)} custom-call(s32[32]{0:T(128)S(1)} %copy-done.3, bf16[64,8196]{1,0:T(8,128)(2,1)S(1)} %bitcast.4, f32[1,8196]{1,0:T(1,128)S(1)} %broadcast_in_dim.9.gain_ref, bf16[8196,384]{1,0:T(8,128)(2,1)S(1)} %copy-done, f32[32,384]{1,0:T(8,128)S(1)} %copy-done.2), custom_call_target="tpu_custom_call" | custom-call | flops 2000000000 | bytes 9000000 | tf_op jit(solution)/shard_map/pallas_call | solution.py:118
  14.2 0.0 copy-done.5
  14.2 0.0 copy-done.10
  14.3 0.0 copy-done.11
  14.3 0.0 copy-start.7
  14.3 30.4 %shard_map.177 = (bf16[32,64,384]{2,1,0:T(8,128)(2,1)S(1)}, bf16[2,1024,256]{2,1,0:T(8,128)(2,1)S(1)}, bf16[2,1024,256]{2,1,0:T(8,128)(2,1)S(1)}, bf16[2,2048,25...) custom-call(s32[1]{0:T(128)S(6)} %copy.20.length_ref, ...), custom_call_target="tpu_custom_call" | custom-call | flops 4000000000 | bytes 10000000 | tf_op jit(solution)/shard_map/pallas_call | solution.py:252
  44.7 0.0 copy-start.20
  44.7 1.0 copy-done.20
  45.7 0.0 copy-done.7
  45.8 27.1 %shard_map.178 = bf16[32,32,384]{2,1,0:T(8,128)(2,1)} custom-call(s32[1]{0:T(128)S(6)} %copy.20.length_ref, f32[5,128]{1,0:T(8,128)S(1)} %get-tuple-element.10.most_ref, bf16[32,64,384]{2,1,0:T(8,128)(2,1)S(1)} %get-tuple-element.11.x_ref, bf16[512,384]{1,0:T(8,128)(2,1)S(1)} %copy-done.7, bf16[2,1024,256]{2,1,0:T(8,128)(2,1)S(1)} %get-tuple-element.12.q_ref, ...), custom_call_target="tpu_custom_call" | custom-call | flops 20000000000 | bytes 8000000 | tf_op jit(solution)/shard_map/pallas_call | solution.py:313
  72.8 0.0 copy-start.14
  72.8 1.5 copy-done.14
  74.3 0.0 copy-start.16
  74.3 1.4 copy-done.16
  75.7 0.0 copy-start.18
  75.7 1.1 copy-done.18
  76.9 5.0 %all-to-all-start = ((bf16[32,32,384]{2,1,0:T(8,128)(2,1)}), bf16[32,32,384]{2,1,0:T(8,128)(2,1)S(1)}, u32[]{:S(2)}, u32[]{:S(2)}) async-start(bf16[32,32,384]{2,1,0:T(8,128)(2,1)} %shard_map.178), calls=%async_computation | async-start | bytes 1572864 | tf_op jit(solution)/shard_map/all_to_all | solution.py:546
  81.8 0.0 copy-start.8
  81.8 1.0 copy-done.8
  82.8 0.0 copy-start.15
  82.8 1.7 %copy-done.15 = bf16[8,80,2048]{2,1,0:T(8,128)(2,1)S(1)} copy-done((bf16[8,80,2048]{2,1,0:T(8,128)(2,1)S(1)}, bf16[8,80,2048]{2,1,0:T(8,128)(2,1)}, u32[]{:S(2)}) %copy-start.15) | copy-done | bytes 2621464
  84.6 0.0 copy-start.17
  84.6 1.6 copy-done.17
  86.2 0.0 copy-start.19
  86.2 1.4 copy-done.19
  87.6 0.0 copy-start.21
  87.6 1.2 copy-done.21
  88.8 0.0 copy-start.24
  88.8 0.0 copy-start.4
  88.8 0.0 copy-start.6
  88.8 25.8 %shard_map.179.later_ref = bf16[32,32,384]{2,1,0:T(8,128)(2,1)S(1)} custom-call(s32[1]{0:T(128)S(6)} %copy.20.length_ref, f32[5,128]{1,0:T(8,128)S(1)} %get-tuple-element.10.most_ref, bf16[32,64,384]{2,1,0:T(8,128)(2,1)S(1)} %copy-done.19, bf16[512,384]{1,0:T(8,128)(2,1)S(1)} %copy-done.8, bf16[2,1024,256]{2,1,0:T(8,128)(2,1)S(1)} %copy-done.21, ...), custom_call_target="tpu_custom_call" | custom-call | flops 20000000000 | bytes 8000000 | tf_op jit(solution)/shard_map/pallas_call | solution.py:313
  114.6 0.0 copy-start.22
  114.6 0.9 copy-done.22
  115.4 0.0 copy-done.24
  115.4 0.0 all-to-all-done.early_ref
  115.5 0.0 copy-done.4
  115.5 0.0 copy-done.6
  115.5 0.0 copy-start.9
  115.5 1.0 copy-done.9
  116.5 0.0 copy-start.12
  116.5 0.9 copy-done.12
  117.4 0.0 copy-start.13
  117.4 0.9 copy-done.13
  118.4 0.0 copy-start.23
  118.4 1.1 copy-done.23
  119.5 46.2 %shard_map.180 = (bf16[2048,384]{1,0:T(8,128)(2,1)S(1)}, bf16[512,384]{1,0:T(8,128)(2,1)S(1)}) custom-call(s32[1]{0:T(128)S(6)} %copy.20.length_ref, bf16[32,32,384]{2,1,0:T(8,128)(2,1)S(1)} %all-to-all-done.early_ref, bf16[32,32,384]{2,1,0:T(8,128)(2,1)S(1)} %copy-done.23, f32[1,384]{1,0:T(1,128)S(1)} %broadcast_in_dim.11.gain_ref, ...), custom_call_target="tpu_custom_call" | custom-call | flops 10000000000 | bytes 7000000 | tf_op jit(solution)/shard_map/pallas_call | solution.py:513
  165.8 0.9 convert_element_type.3
  166.7 1.1 copy.21
  (1 shorter events, 0.0 us)
Async XLA Ops:
  2.8 2.8 %copy-start = (bf16[8196,384]{1,0:T(8,128)(2,1)S(1)}, bf16[8196,384]{1,0:T(8,128)(2,1)}, u32[]{:S(2)}) copy-start(bf16[8196,384]{1,0:T(8,128)(2,1)} %w_ref.1) | copy-start | bytes 18883588
  5.5 1.2 copy-start.1
  6.8 0.8 copy-start.2
  7.6 0.7 copy-start.3
  8.2 6.0 %copy-start.5 = (bf16[384,1536]{1,0:T(8,128)(2,1)S(1)}, bf16[384,1536]{1,0:T(8,128)(2,1)}, u32[]{:S(2)}) copy-start(bf16[384,1536]{1,0:T(8,128)(2,1)} %wqkv_ref.2) | copy-start | bytes 3538948
  8.2 6.0 %copy-start.10 = (f32[2048,128]{1,0:T(8,128)S(1)}, f32[2048,128]{1,0:T(8,128)}, u32[]{:S(2)}) copy-start(f32[2048,128]{1,0:T(8,128)} %constant.8.clone.cos_ref) | copy-start | bytes 3145732
  8.2 6.0 %copy-start.11 = (f32[2048,128]{1,0:T(8,128)S(1)}, f32[2048,128]{1,0:T(8,128)}, u32[]{:S(2)}) copy-start(f32[2048,128]{1,0:T(8,128)} %constant.9.clone.sin_ref) | copy-start | bytes 3145732
  14.3 31.5 %copy-start.7 = (bf16[512,384]{1,0:T(8,128)(2,1)S(1)}, bf16[512,384]{1,0:T(8,128)(2,1)}, u32[]{:S(2)}) copy-start(bf16[512,384]{1,0:T(8,128)(2,1)} %wout_ref.4) | copy-start | bytes 1179652
  44.7 1.0 copy-start.20
  72.8 1.5 copy-start.14
  74.3 1.4 copy-start.16
  75.7 1.1 copy-start.18
  76.9 38.6 %all-to-all-start = ((bf16[32,32,384]{2,1,0:T(8,128)(2,1)}), bf16[32,32,384]{2,1,0:T(8,128)(2,1)S(1)}, u32[]{:S(2)}, u32[]{:S(2)}) async-start(bf16[32,32,384]{2,1,0:T(8,128)(2,1)} %shard_map.178), calls=%async_computation | async-start | bytes 1572864 | tf_op jit(solution)/shard_map/all_to_all | solution.py:546
  81.8 1.0 copy-start.8
  82.8 1.7 %copy-start.15 = (bf16[8,80,2048]{2,1,0:T(8,128)(2,1)S(1)}, bf16[8,80,2048]{2,1,0:T(8,128)(2,1)}, u32[]{:S(2)}) copy-start(bf16[8,80,2048]{2,1,0:T(8,128)(2,1)} %copy-done.14) | copy-start | bytes 7864324
  84.6 1.6 copy-start.17
  86.2 1.4 copy-start.19
  87.6 1.2 copy-start.21
  88.8 26.6 %copy-start.24 = (f32[384]{0:T(512)S(1)}, f32[384]{0:T(512)}, u32[]{:S(2)}) copy-start(f32[384]{0:T(512)} %param.26) | copy-start | bytes 4612
  88.8 26.7 %copy-start.4 = (bf16[1,64,32,384]{3,2,1,0:T(8,128)(2,1)S(1)}, bf16[1,64,32,384]{3,2,1,0:T(8,128)(2,1)}, u32[]{:S(2)}) copy-start(bf16[1,64,32,384]{3,2,1,0:T(8,128)(2,1)} %param.29) | copy-start | bytes 4718596
  88.8 26.7 %copy-start.6 = (bf16[384,1536]{1,0:T(8,128)(2,1)S(1)}, bf16[384,1536]{1,0:T(8,128)(2,1)}, u32[]{:S(2)}) copy-start(bf16[384,1536]{1,0:T(8,128)(2,1)} %wqkv_ref.3) | copy-start | bytes 3538948
  114.6 0.9 copy-start.22
  115.5 1.0 copy-start.9
  116.5 0.9 copy-start.12
  117.4 0.9 copy-start.13
  118.4 1.1 copy-start.23

commit v4 on v3

--- a/solution.py
+++ b/solution.py
@@ -131,7 +131,7 @@
 
 def exchange_kernel(
     seq, length_ref, bands_ref, gain_ref, wqkv_ref, cos_ref, sin_ref,
-    x_ref, qa_ref, qb_ref, k_ref, v_ref, most_ref, got, send_sem, recv_sem,
+    x_ref, q_ref, k_ref, v_ref, most_ref, got, send_sem, recv_sem,
 ):
     frames, width = got.shape[1:]
     half = frames // 2
@@ -197,8 +197,9 @@
         base = pl.multiple_of(row * count, count)
         rows = pl.ds(base, count)
         received = got[owners]
-        x_ref[owners] = received
-        normed = rms_norm(received.reshape(count, width).astype(F32), gain_ref[...])
+        x_ref[0, owners] = received[:, :half]
+        x_ref[1, owners] = received[:, half:]
+        normed = rms_norm(received.reshape(count, width).astype(F32), gain_ref[...].reshape(1, width))
         cosine = cos_ref[rows, :]
         sines = sin_ref[rows, :]
         alive_row = (lax.broadcasted_iota(jnp.int32, (count, 1), 0) + base) < length
@@ -209,8 +210,8 @@
             qa, qb = rope(jnp.dot(normed, wq[g], preferred_element_type=F32), cosine, sines)
             scaled = jnp.concatenate([qa, qb], axis=1) * (LOG2E * DH**-0.5)
             parts = scaled.reshape(8, frames, GROUP)
-            qa_ref[g, here, :] = parts[:, :half].reshape(8 * half, GROUP).astype(BF)
-            qb_ref[g, here, :] = parts[:, half:].reshape(8 * half, GROUP).astype(BF)
+            for n in range(2):
+                q_ref[n, g, here, :] = parts[:, n * half : (n + 1) * half].reshape(8 * half, GROUP).astype(BF)
             ka, kb = rope(jnp.dot(normed, wk[g], preferred_element_type=F32), cosine, sines)
             keys = jnp.concatenate([ka, kb], axis=1)
             keys = jnp.where(alive_row, keys, 0.0)
@@ -252,48 +253,48 @@
     return pl.pallas_call(
         functools.partial(exchange_kernel, seq),
         out_shape=(
-            jax.ShapeDtypeStruct((seq, frames, width), BF),
-            jax.ShapeDtypeStruct((2, count // 2, GROUP), BF),
-            jax.ShapeDtypeStruct((2, count // 2, GROUP), BF),
+            jax.ShapeDtypeStruct((2, seq, frames // 2, width), BF),
+            jax.ShapeDtypeStruct((2, 2, count // 2, GROUP), BF),
             jax.ShapeDtypeStruct((2, count, GROUP), BF),
             jax.ShapeDtypeStruct((HEADS, VROWS, count), BF),
             jax.ShapeDtypeStruct((5, 128), F32),
         ),
         in_specs=[smem()] + [whole()] * 5,
-        out_specs=[whole()] * 6,
+        out_specs=[whole()] * 5,
         scratch_shapes=[VMEM((seq, frames, width), BF), dma((seq,)), dma((seq,))],
         compiler_params=pltpu.CompilerParams(collective_id=1, has_side_effects=True, vmem_limit_bytes=TIME_LIMIT),
         cost_estimate=pl.CostEstimate(flops=4 * 10**9, bytes_accessed=10 * 10**6, transcendentals=0),
-    )(lengths, computed, gain[None], wqkv, jnp.asarray(cosine), jnp.asarray(sines))
+    )(lengths, computed, gain, wqkv, jnp.asarray(cosine), jnp.asarray(sines))
 
 
 TIME_LIMIT = 28 * 2**20
 
 
-def time_kernel(chunk, length_ref, most_ref, x_ref, wout_ref, q_ref, k_ref, v_ref, out_ref, heads_ref):
-    owners, frames, width = x_ref.shape
-    half = frames // 2
+def time_kernel(length_ref, most_ref, x_ref, wout_ref, q_ref, k_ref, v_ref, out_ref, heads_ref):
+    chunks, owners, half, width = x_ref.shape
     lane = lax.broadcasted_iota(jnp.int32, (1, GROUP), 1)
     bound = jnp.maximum(most_ref[0:1, :] * most_ref[1:2, :], most_ref[2:3, :] * most_ref[3:4, :])
     fits = (jnp.max(bound) * 1.05 < SAFE * SAFE) & (jnp.max(most_ref[4:5, :]) < VSAFE)
 
     def attend(shift):
-        def head(h, carry):
+        def head(n, carry):
+            chunk = n // HEADS
+            h = n % HEADS
             g = h // 4
             mine = (lane % 128) // HALF == h % 4
-            queries = jnp.where(mine, q_ref[g], jnp.zeros((), BF))
+            queries = jnp.where(mine, q_ref[chunk, g], jnp.zeros((), BF))
             scores = lax.dot_general(k_ref[g], queries, NT, preferred_element_type=F32)
             if shift:
-                alive = lax.broadcasted_iota(jnp.int32, (owners * frames, 1), 0) < length_ref[0]
+                alive = lax.broadcasted_iota(jnp.int32, (k_ref.shape[1], 1), 0) < length_ref[0]
                 scores = jnp.where(alive, scores, -1e30)
                 scores = scores - jnp.max(scores, axis=0, keepdims=True)
             powers = jnp.exp2(scores).astype(BF)
             mixed = jnp.dot(v_ref[h], powers, preferred_element_type=F32)
             mixed = mixed[:DH] / mixed[DH : DH + 1]
-            heads_ref[pl.ds(pl.multiple_of(h * DH, DH), DH), :] = mixed.astype(BF)
+            heads_ref[chunk, pl.ds(pl.multiple_of(h * DH, DH), DH), :] = mixed.astype(BF)
             return carry
 
-        lax.fori_loop(0, HEADS, head, 0)
+        lax.fori_loop(0, chunks * HEADS, head, 0)
 
     @pl.when(fits)
     def _():
@@ -303,21 +304,21 @@
     def _():
         attend(True)
 
-    projected = lax.dot_general(heads_ref[...], wout_ref[...], TN, preferred_element_type=F32)
-    before = x_ref[:, chunk * half : (chunk + 1) * half, :].astype(F32)
-    out_ref[...] = (before + projected.reshape(owners, half, width)).astype(BF)
-
-
-def time_attention(chunk, lengths, most, sequence, wout, q, k, v):
-    owners, frames, width = sequence.shape
+    for chunk in range(chunks):
+        projected = lax.dot_general(heads_ref[chunk], wout_ref[...], TN, preferred_element_type=F32)
+        out_ref[chunk] = (x_ref[chunk].astype(F32) + projected.reshape(owners, half, width)).astype(BF)
+
+
+def time_attention(lengths, most, sequence, wout, q, k, v):
+    chunks, owners, half, width = sequence.shape
     return pl.pallas_call(
-        functools.partial(time_kernel, chunk),
-        out_shape=jax.ShapeDtypeStruct((owners, frames // 2, width), BF),
+        time_kernel,
+        out_shape=jax.ShapeDtypeStruct(sequence.shape, BF),
         in_specs=[smem()] + [whole()] * 6,
         out_specs=whole(),
-        scratch_shapes=[VMEM((HEADS * DH, owners * frames // 2), BF)],
+        scratch_shapes=[VMEM((chunks, HEADS * DH, owners * half), BF)],
         compiler_params=pltpu.CompilerParams(vmem_limit_bytes=TIME_LIMIT),
-        cost_estimate=pl.CostEstimate(flops=2 * 10**10, bytes_accessed=8 * 10**6, transcendentals=0),
+        cost_estimate=pl.CostEstimate(flops=4 * 10**10, bytes_accessed=8 * 10**6, transcendentals=0),
     )(lengths, most, sequence, wout, q, k, v)
 
 
@@ -325,11 +326,11 @@
 
 
 def finish_kernel(
-    seq, songs, length_ref, early_ref, later_ref, gain_ref, wqkv_ref, wout_ref, cot_hbm, cos_ref, sin_ref,
+    seq, songs, length_ref, timed_ref, gain_ref, wqkv_ref, wout_ref, cot_hbm, cos_ref, sin_ref,
     out_hbm, sum_ref, got, cot_ref, heads_ref, x_ref, feat_ref, grad_ref, halves, half_in, parts, parts_in, mid, full,
     cot_sem, out_sem, send_sem, recv_sem, core_send, core_recv, plane_send, plane_recv, song_send, song_recv, back_send, back_recv, last_send, last_recv,
 ):
-    bands, chunk, width = early_ref.shape
+    _, bands, chunk, width = timed_ref.shape
     inner = HEADS * DH
     rows = bands * FRAMES_EACH
     blocks = chunk // FRAMES_EACH
@@ -367,32 +368,37 @@
     grad_ref[...] = jnp.zeros_like(grad_ref)
     pl.semaphore_wait(barrier, seq - 1 + songs - 1)
 
-    def copy(i):
+    def copy(n, i):
         k = other(i)
         return pltpu.make_async_remote_copy(
-            src_ref=later_ref.at[k], dst_ref=got.at[me], send_sem=send_sem.at[i], recv_sem=recv_sem.at[i],
+            src_ref=timed_ref.at[n, k], dst_ref=got.at[n, me], send_sem=send_sem.at[n, i], recv_sem=recv_sem.at[n, i],
             device_id=(k, song), device_id_type=MESH)
 
-    def start(i, carry):
-        copy(seq - i).start()
-        return carry
-
-    def arrive(i, carry):
-        copy(seq - i).wait()
-        return carry
-
-    lax.fori_loop(1, seq, start, 0)
-    got[me] = later_ref[me]
+    for n in range(2):
+
+        def start(i, carry):
+            copy(n, seq - i).start()
+            return carry
+
+        lax.fori_loop(1, seq, start, 0)
+    got[:, me] = timed_ref[:, me]
     length = length_ref[0]
     cot_copy.wait()
 
-    def attend(source_ref, first):
+    def attend(n):
+        def arrive(i, carry):
+            copy(n, seq - i).wait()
+            return carry
+
+        lax.fori_loop(1, seq, arrive, 0)
+        first = n * blocks
+
         def block(i, carry):
-            piece = source_ref[:, pl.ds(pl.multiple_of(i * FRAMES_EACH, FRAMES_EACH), FRAMES_EACH), :].reshape(rows, width)
+            piece = got[n, :, pl.ds(pl.multiple_of(i * FRAMES_EACH, FRAMES_EACH), FRAMES_EACH), :].reshape(rows, width)
             values_x = jnp.dot(order, piece, preferred_element_type=F32)
             here = pl.ds(pl.multiple_of((i + first) * rows, rows), rows)
             x_ref[here, :] = values_x.astype(BF)
-            normed = rms_norm(values_x, gain_ref[...])
+            normed = rms_norm(values_x, gain_ref[...].reshape(1, width))
             cosine = cos_ref[...]
             sines = sin_ref[...]
             values = jnp.dot(normed, wv, preferred_element_type=F32)
@@ -437,9 +443,8 @@
         feat_ref[here, :] = (x_ref[here, :].astype(F32) + projected).astype(BF)
         out_copy(i).start()
 
-    attend(early_ref, 0)
-    lax.fori_loop(1, seq, arrive, 0)
-    attend(got, blocks)
+    attend(0)
+    attend(1)
 
     def remote(src_ref, dst_ref, send, recv, device):
         return pltpu.make_async_remote_copy(
@@ -500,10 +505,10 @@
         out_copy(i).wait()
 
 
-def finish(lengths, early, later, gain, wqkv, wout, cotangent):
+def finish(lengths, timed, gain, wqkv, wout, cotangent):
     seq = lax.axis_size("seq")
     songs = lax.axis_size("song")
-    bands, chunk, width = early.shape
+    _, bands, chunk, width = timed.shape
     inner = HEADS * DH
     rows = bands * FRAMES_EACH
     count = 2 * chunk * bands
@@ -513,10 +518,10 @@
     return pl.pallas_call(
         functools.partial(finish_kernel, seq, songs),
         out_shape=(jax.ShapeDtypeStruct((count, width), BF), jax.ShapeDtypeStruct((inner, width), BF)),
-        in_specs=[smem()] + [whole()] * 5 + [anywhere] + [whole()] * 2,
+        in_specs=[smem()] + [whole()] * 4 + [anywhere] + [whole()] * 2,
         out_specs=(anywhere, whole()),
         scratch_shapes=[
-            VMEM((bands, chunk, width), BF),
+            VMEM((2, bands, chunk, width), BF),
             VMEM((count, width), BF),
             VMEM((count, inner), BF),
             VMEM((count, width), BF),
@@ -528,12 +533,12 @@
             VMEM((16, inner // 32, width), BF),
             VMEM((songs, inner // 32, width), F32),
             VMEM((2, 16, inner // 32, width), BF),
-            dma, dma((4,)), dma((seq,)), dma((seq,)), dma, dma, dma((16,)), dma((16,)),
+            dma, dma((4,)), dma((2, seq)), dma((2, seq)), dma, dma, dma((16,)), dma((16,)),
             dma((songs,)), dma((songs,)), dma((16,)), dma((16,)), dma, dma,
         ],
         compiler_params=pltpu.CompilerParams(collective_id=2, has_side_effects=True, vmem_limit_bytes=36 * 2**20),
         cost_estimate=pl.CostEstimate(flops=10**10, bytes_accessed=7 * 10**6, transcendentals=0),
-    )(lengths, early, later, gain, wqkv, wout, cotangent, jnp.asarray(cosine), jnp.asarray(sines))
+    )(lengths, timed, gain, wqkv, wout, cotangent, jnp.asarray(cosine), jnp.asarray(sines))
 
 
 def per_device(spectrum, widths, lengths, bin_gain, embed_weight, embed_bias, time_gain, time_qkv, time_out, band_gain, band_qkv, band_out, cotangent):
@@ -541,11 +546,9 @@
     bands, width = embed_bias.shape
     computed = embed(spectrum[0], widths, bin_gain, embed_weight, embed_bias)
     tangent = cotangent.reshape(local_frames * bands, width)
-    owned, early, late, k, v, most = exchange(computed, lengths, time_gain, time_qkv)
-    first = time_attention(0, lengths, most, owned, time_out, early, k, v)
-    first = lax.all_to_all(first, "seq", split_axis=0, concat_axis=0, tiled=True)
-    second = time_attention(1, lengths, most, owned, time_out, late, k, v)
-    output, gradient = finish(lengths, first, second, band_gain[None], band_qkv, band_out, tangent)
+    owned, q, k, v, most = exchange(computed, lengths, time_gain, time_qkv)
+    timed = time_attention(lengths, most, owned, time_out, q, k, v)
+    output, gradient = finish(lengths, timed, band_gain, band_qkv, band_out, tangent)
     return output.reshape(1, local_frames, bands, width), gradient.astype(F32)
 
 

time: 169 us -> 156 us (0.923)
  local copies, waits for them, and re-layouts: 25 us -> 7.46 us
  Pallas kernels: 136 us -> 146 us
  starting transfers between devices: 4.97 us -> 0 us
    unnamed x51 -> x31, local copies, waits for them, and re-layouts: 23.5 us -> 6.67 us
    pallas_call x1, Pallas kernels: 46.2 us -> 57.8 us  [finish(): pl.pallas_call(functools.partial(finish_kernel, seq, songs), out_shape=(j...]
    all_to_all x1 -> x0, starting transfers between devices: 4.97 us -> none  [per_device(): lax.all_to_all(first, 'seq', split_axis=0, concat_axis=0, tiled=True)]
    pallas_call x2 -> x1, Pallas kernels: 52.8 us -> 52 us  [time_attention(): pl.pallas_call(time_kernel, out_shape=jax.ShapeDtypeStruct(sequence.shape...]
  transfers between devices with their start and end apart: 1 -> 0, of which waited for: 0 -> 0; matrix products, arithmetic and copies ran while one was open for 0% -> 0% of each run, Pallas kernels for 15% -> 0%
where the time goes in v4:
time: 156 us
  Pallas kernels  146 us (94%)
  local copies, waits for them, and re-layouts  7.46 us (5%)
    pallas_call x1, Pallas kernels, finish(): pl.pallas_call(functools.partial(finish_kernel, seq, songs), out_shape=(j...  57.8 us
    pallas_call x1, Pallas kernels, time_attention(): pl.pallas_call(time_kernel, out_shape=jax.ShapeDtypeStruct(sequence.shape...  52 us
    pallas_call x1, Pallas kernels, exchange(): pl.pallas_call(functools.partial(exchange_kernel, seq), out_shape=(jax.Sh...  30.4 us
    unnamed x31, local copies, waits for them, and re-layouts  6.67 us
    pallas_call x1, Pallas kernels, embed(): pl.pallas_call(functools.partial(embed_kernel, bands), out_shape=jax.Shap...  5.99 us

profile of v4, /device:TPU:1, one launch (start us, length us, event | category | flops | bytes accessed | tf_op | source)
XLA Modules:
  0.0 156.1 jit_solution(12146183319241095115)
XLA Ops:
  1.3 0.8 broadcast_in_dim.3.gain_ref
  2.1 0.0 copy-start
  2.1 2.8 %copy-done = bf16[8196,384]{1,0:T(8,128)(2,1)S(1)} copy-done((bf16[8196,384]{1,0:T(8,128)(2,1)S(1)}, bf16[8196,384]{1,0:T(8,128)(2,1)}, u32[]{:S(2)}) %copy-start) | copy-done | bytes 6294552
  4.9 0.0 copy-start.1
  4.9 1.2 copy-done.1
  6.1 0.0 copy-start.2
  6.1 0.8 copy-done.2
  6.9 0.0 copy-start.3
  6.9 0.7 copy-done.3
  7.5 0.0 copy-start.5
  7.5 0.0 copy-start.9
  7.6 0.0 copy-start.11
  7.6 0.0 copy-start.12
  7.6 6.0 %shard_map.176.bands_ref = bf16[32,64,384]{2,1,0:T(8,128)(2,1)S(1)} custom-call(s32[32]{0:T(128)S(1)} %copy-done.3, bf16[64,8196]{1,0:T(8,128)(2,1)S(1)} %bitcast.4, f32[1,8196]{1,0:T(1,128)S(1)} %broadcast_in_dim.3.gain_ref, bf16[8196,384]{1,0:T(8,128)(2,1)S(1)} %copy-done, f32[32,384]{1,0:T(8,128)S(1)} %copy-done.2), custom_call_target="tpu_custom_call" | custom-call | flops 2000000000 | bytes 9000000 | tf_op jit(solution)/shard_map/pallas_call | solution.py:118
  13.6 0.0 copy-done.5
  13.6 0.0 copy-done.9
  13.6 0.0 copy-done.11
  13.6 0.0 copy-done.12
  13.6 0.0 copy-start.7
  13.6 30.4 %shard_map.177 = (bf16[2,32,32,384]{3,2,1,0:T(8,128)(2,1)S(1)}, bf16[2,2,1024,256]{3,2,1,0:T(8,128)(2,1)S(1)}, bf16[2,2048,256]{2,1,0:T(8,128)(2,1)S(1)}, bf16[8,80,2048]{2,1,0:T(8,128)(2,1)S(1)}, f32[5,128]{1,0:T(8,128)S(1)}) custom-call(s32[1]{0:T(128)S(6)} %copy.20.length_ref, bf16[32,64,384]{2,1,0:T(8,128)(2,1)S(1)} %shard_map.176.bands_ref, ...), custom_call_target="tpu_custom_call" | custom-call | flops 4000000000 | bytes 10000000 | tf_op jit(solution)/shard_map/pallas_call | solution.py:253
  44.1 0.0 copy-done.7
  44.1 0.0 copy-start.4
  44.1 0.0 copy-start.6
  44.1 0.0 copy-start.8
  44.1 0.0 copy-start.10
  44.1 0.0 copy-start.13
  44.1 0.0 copy-start.14
  44.1 52.0 %shard_map.178.timed_ref = bf16[2,32,32,384]{3,2,1,0:T(8,128)(2,1)S(1)} custom-call(s32[1]{0:T(128)S(6)} %copy.20.length_ref, f32[5,128]{1,0:T(8,128)S(1)} %get-tuple-element.9.most_ref, bf16[2,32,32,384]{3,2,1,0:T(8,128)(2,1)S(1)} %get-tuple-element.10.x_ref, bf16[512,384]{1,0:T(8,128)(2,1)S(1)} %copy-done.7, ...), custom_call_target="tpu_custom_call" | custom-call | flops 40000000000 | bytes 8000000 | tf_op jit(solution)/shard_map/pallas_call | solution.py:314
  96.2 0.0 copy-done.4
  96.2 0.0 copy-done.6
  96.2 0.0 copy-done.8
  96.2 0.0 copy-done.10
  96.2 0.0 copy-done.13
  96.2 0.0 copy-done.14
  96.2 57.8 %shard_map.179 = (bf16[2048,384]{1,0:T(8,128)(2,1)S(1)}, bf16[512,384]{1,0:T(8,128)(2,1)S(1)}) custom-call(s32[1]{0:T(128)S(6)} %copy.20.length_ref, bf16[2,32,32,384]{3,2,1,0:T(8,128)(2,1)S(1)} %shard_map.178.timed_ref, f32[384]{0:T(512)S(1)} %copy-done.10, bf16[384,1536]{1,0:T(8,128)(2,1)S(1)} %copy-done.6, bf16[512,384]{1,0:T(8,128)(2,1)S(1)} %copy-done.8, ...), custom_call_target="tpu_custom_call" | custom-call | flops 10000000000 | bytes 7000000 | tf_op jit(solution)/shard_map/pallas_call | solution.py:518
  154.0 0.9 convert_element_type.3
  154.9 1.1 copy.21
Async XLA Ops:
  2.1 2.8 %copy-start = (bf16[8196,384]{1,0:T(8,128)(2,1)S(1)}, bf16[8196,384]{1,0:T(8,128)(2,1)}, u32[]{:S(2)}) copy-start(bf16[8196,384]{1,0:T(8,128)(2,1)} %w_ref.1) | copy-start | bytes 18883588
  4.9 1.2 copy-start.1
  6.1 0.8 copy-start.2
  6.9 0.7 copy-start.3
  7.5 6.0 %copy-start.5 = (bf16[384,1536]{1,0:T(8,128)(2,1)S(1)}, bf16[384,1536]{1,0:T(8,128)(2,1)}, u32[]{:S(2)}) copy-start(bf16[384,1536]{1,0:T(8,128)(2,1)} %wqkv_ref.2) | copy-start | bytes 3538948
  7.5 6.0 %copy-start.9 = (f32[384]{0:T(512)S(1)}, f32[384]{0:T(512)}, u32[]{:S(2)}) copy-start(f32[384]{0:T(512)} %gain_ref.2) | copy-start | bytes 4612
  7.6 6.0 %copy-start.11 = (f32[2048,128]{1,0:T(8,128)S(1)}, f32[2048,128]{1,0:T(8,128)}, u32[]{:S(2)}) copy-start(f32[2048,128]{1,0:T(8,128)} %constant.9.clone.sin_ref) | copy-start | bytes 3145732
  7.6 6.0 %copy-start.12 = (f32[2048,128]{1,0:T(8,128)S(1)}, f32[2048,128]{1,0:T(8,128)}, u32[]{:S(2)}) copy-start(f32[2048,128]{1,0:T(8,128)} %constant.8.clone.cos_ref) | copy-start | bytes 3145732
  13.6 30.5 %copy-start.7 = (bf16[512,384]{1,0:T(8,128)(2,1)S(1)}, bf16[512,384]{1,0:T(8,128)(2,1)}, u32[]{:S(2)}) copy-start(bf16[512,384]{1,0:T(8,128)(2,1)} %wout_ref.2) | copy-start | bytes 1179652
  44.1 52.1 %copy-start.4 = (bf16[1,64,32,384]{3,2,1,0:T(8,128)(2,1)S(1)}, bf16[1,64,32,384]{3,2,1,0:T(8,128)(2,1)}, u32[]{:S(2)}) copy-start(bf16[1,64,32,384]{3,2,1,0:T(8,128)(2,1)} %param.29) | copy-start | bytes 4718596
  44.1 52.1 %copy-start.6 = (bf16[384,1536]{1,0:T(8,128)(2,1)S(1)}, bf16[384,1536]{1,0:T(8,128)(2,1)}, u32[]{:S(2)}) copy-start(bf16[384,1536]{1,0:T(8,128)(2,1)} %wqkv_ref.3) | copy-start | bytes 3538948
  44.1 52.1 %copy-start.8 = (bf16[512,384]{1,0:T(8,128)(2,1)S(1)}, bf16[512,384]{1,0:T(8,128)(2,1)}, u32[]{:S(2)}) copy-start(bf16[512,384]{1,0:T(8,128)(2,1)} %wout_ref.3) | copy-start | bytes 1179652
  44.1 52.1 %copy-start.10 = (f32[384]{0:T(512)S(1)}, f32[384]{0:T(512)}, u32[]{:S(2)}) copy-start(f32[384]{0:T(512)} %gain_ref.3) | copy-start | bytes 4612
  44.1 52.1 %copy-start.13 = (f32[512,128]{1,0:T(8,128)S(1)}, f32[512,128]{1,0:T(8,128)}, u32[]{:S(2)}) copy-start(f32[512,128]{1,0:T(8,128)} %constant.11.clone.sin_ref) | copy-start | bytes 786436
  44.1 52.1 %copy-start.14 = (f32[512,128]{1,0:T(8,128)S(1)}, f32[512,128]{1,0:T(8,128)}, u32[]{:S(2)}) copy-start(f32[512,128]{1,0:T(8,128)} %constant.10.clone.cos_ref) | copy-start | bytes 786436

commit v5 on v4

--- a/solution.py
+++ b/solution.py
@@ -65,34 +65,48 @@
 NARROW = 640
 
 
-def embed_kernel(bands, widths_ref, x_ref, gain_ref, w_ref, bias_ref, out_ref, starts_ref):
+def embed_kernel(bands, widths_ref, x_ref, gain_ref, w_hbm, last_ref, bias_ref, out_ref, starts_ref, w_ref, normed_ref, tail_ref, w_sem):
     limit = x_ref.shape[1]
     main = limit // 128 * 128
+    each = main // 4
+
+    def load(n):
+        here = pl.ds(n * each, each)
+        return pltpu.make_async_copy(w_hbm.at[here], w_ref.at[here], w_sem.at[n])
+
+    for n in range(4):
+        load(n).start()
     total = 0
     for k in range(bands):
         starts_ref[k] = total
         total = total + widths_ref[k] * 4
 
-    def band(k, size):
+    def window(k, size):
+        return pl.multiple_of(jnp.minimum(starts_ref[k] // 128, (main - size) // 128) * 128, 128)
+
+    def normalise(k, size):
         first = starts_ref[k]
         count = widths_ref[k] * 4
-        begin = pl.multiple_of(jnp.minimum(first // 128, (main - size) // 128) * 128, 128)
-        window = pl.ds(begin, size)
+        begin = window(k, size)
         entry = lax.broadcasted_iota(jnp.int32, (1, size), 1) + begin
-        piece = x_ref[:, window].astype(F32)
+        piece = x_ref[:, pl.ds(begin, size)].astype(F32)
         piece = jnp.where((entry >= first) & (entry < first + count), piece, 0.0)
         tail = jnp.where(k == bands - 1, x_ref[:, main:].astype(F32), 0.0)
         square = jnp.sum(piece * piece, axis=1, keepdims=True) + jnp.sum(tail * tail, axis=1, keepdims=True)
         scale = 1.0 / jnp.sqrt(jnp.maximum(square / count.astype(F32), FLOOR))
-        normed = (piece * scale * gain_ref[:, window]).astype(BF)
-        summed = jnp.dot(normed, w_ref[window, :], preferred_element_type=F32) + bias_ref[pl.ds(k, 1), :]
-        normed = (tail * scale * gain_ref[:, main:]).astype(BF).astype(F32)
-        rows = w_ref[main:, :].astype(F32)
+        normed_ref[k, :, :size] = (piece * scale * gain_ref[:, pl.ds(begin, size)]).astype(BF)
+        tail_ref[k] = (tail * scale * gain_ref[:, main:]).astype(BF)
+
+    def project(k, size):
+        summed = jnp.dot(normed_ref[k, :, :size], w_ref[pl.ds(window(k, size), size), :], preferred_element_type=F32)
+        summed = summed + bias_ref[pl.ds(k, 1), :]
+        tail = tail_ref[k].astype(F32)
+        rows = last_ref[...].astype(F32)
         for e in range(limit - main):
-            summed = summed + normed[:, e : e + 1] * rows[e : e + 1, :]
+            summed = summed + tail[:, e : e + 1] * rows[e : e + 1, :]
         out_ref[k] = summed.astype(BF)
 
-    def step(i, carry):
+    def step(work, i, carry):
         narrow = widths_ref[4 * i] * 4 <= NARROW - 124
         for j in range(1, 4):
             narrow = narrow & (widths_ref[4 * i + j] * 4 <= NARROW - 124)
@@ -100,33 +114,51 @@
         @pl.when(narrow)
         def _():
             for j in range(4):
-                band(4 * i + j, NARROW)
+                work(4 * i + j, NARROW)
 
         @pl.when(jnp.logical_not(narrow))
         def _():
             for j in range(4):
-                band(4 * i + j, WINDOW)
+                work(4 * i + j, WINDOW)
 
         return carry
 
-    lax.fori_loop(0, bands // 4, step, 0)
+    lax.fori_loop(0, bands // 4, functools.partial(step, normalise), 0)
+    for n in range(4):
+        load(n).wait()
+    lax.fori_loop(0, bands // 4, functools.partial(step, project), 0)
 
 
 def embed(spectrum, widths, bin_gain, embed_weight, embed_bias):
     frames, feature_count = spectrum.shape
     bands, width = embed_bias.shape
+    main = feature_count // 128 * 128
+
+    def full(*shape):
+        return pl.BlockSpec(shape, lambda i: (0,) * len(shape))
+
     return pl.pallas_call(
         functools.partial(embed_kernel, bands),
+        grid=(1,),
         out_shape=jax.ShapeDtypeStruct((bands, frames, width), BF),
-        in_specs=[smem()] + [whole()] * 4,
-        out_specs=whole(),
-        scratch_shapes=[pltpu.SMEM((bands,), jnp.int32)],
-        compiler_params=pltpu.CompilerParams(vmem_limit_bytes=32 * 2**20),
+        in_specs=[
+            smem(), full(frames, feature_count), full(1, feature_count), pl.BlockSpec(memory_space=pl.ANY),
+            pl.BlockSpec((16, width), lambda i: (main // 16, 0)), full(bands, width),
+        ],
+        out_specs=full(bands, frames, width),
+        scratch_shapes=[
+            pltpu.SMEM((bands,), jnp.int32),
+            VMEM((main, width), BF),
+            VMEM((bands, frames, WINDOW), BF),
+            VMEM((bands, frames, feature_count - main), BF),
+            pltpu.SemaphoreType.DMA((4,)),
+        ],
+        compiler_params=pltpu.CompilerParams(vmem_limit_bytes=60 * 2**20),
         cost_estimate=pl.CostEstimate(flops=2 * 10**9, bytes_accessed=9 * 10**6, transcendentals=0),
-    )(widths, spectrum, bin_gain[None], embed_weight, embed_bias)
-
-
-VROWS = 80
+    )(widths, spectrum, bin_gain[None], embed_weight, embed_weight, embed_bias)
+
+
+VROWS = 128
 
 
 def exchange_kernel(
@@ -204,14 +236,14 @@
         sines = sin_ref[rows, :]
         alive_row = (lax.broadcasted_iota(jnp.int32, (count, 1), 0) + base) < length
         alive_col = (lax.broadcasted_iota(jnp.int32, (1, count), 1) + base) < length
-        here = pl.ds(pl.multiple_of(row * 8 * half, 8 * half), 8 * half)
         kinds = []
         for g in range(2):
             qa, qb = rope(jnp.dot(normed, wq[g], preferred_element_type=F32), cosine, sines)
             scaled = jnp.concatenate([qa, qb], axis=1) * (LOG2E * DH**-0.5)
             parts = scaled.reshape(8, frames, GROUP)
             for n in range(2):
-                q_ref[n, g, here, :] = parts[:, n * half : (n + 1) * half].reshape(8 * half, GROUP).astype(BF)
+                later = pl.ds(pl.multiple_of(row * 8 * half + n * seq * half, 8 * half), 8 * half)
+                q_ref[g, later, :] = parts[:, n * half : (n + 1) * half].reshape(8 * half, GROUP).astype(BF)
             ka, kb = rope(jnp.dot(normed, wk[g], preferred_element_type=F32), cosine, sines)
             keys = jnp.concatenate([ka, kb], axis=1)
             keys = jnp.where(alive_row, keys, 0.0)
@@ -254,7 +286,7 @@
         functools.partial(exchange_kernel, seq),
         out_shape=(
             jax.ShapeDtypeStruct((2, seq, frames // 2, width), BF),
-            jax.ShapeDtypeStruct((2, 2, count // 2, GROUP), BF),
+            jax.ShapeDtypeStruct((2, count, GROUP), BF),
             jax.ShapeDtypeStruct((2, count, GROUP), BF),
             jax.ShapeDtypeStruct((HEADS, VROWS, count), BF),
             jax.ShapeDtypeStruct((5, 128), F32),
@@ -276,36 +308,41 @@
     bound = jnp.maximum(most_ref[0:1, :] * most_ref[1:2, :], most_ref[2:3, :] * most_ref[3:4, :])
     fits = (jnp.max(bound) * 1.05 < SAFE * SAFE) & (jnp.max(most_ref[4:5, :]) < VSAFE)
 
-    def attend(shift):
-        def head(n, carry):
-            chunk = n // HEADS
-            h = n % HEADS
-            g = h // 4
-            mine = (lane % 128) // HALF == h % 4
-            queries = jnp.where(mine, q_ref[chunk, g], jnp.zeros((), BF))
-            scores = lax.dot_general(k_ref[g], queries, NT, preferred_element_type=F32)
-            if shift:
-                alive = lax.broadcasted_iota(jnp.int32, (k_ref.shape[1], 1), 0) < length_ref[0]
-                scores = jnp.where(alive, scores, -1e30)
-                scores = scores - jnp.max(scores, axis=0, keepdims=True)
-            powers = jnp.exp2(scores).astype(BF)
-            mixed = jnp.dot(v_ref[h], powers, preferred_element_type=F32)
-            mixed = mixed[:DH] / mixed[DH : DH + 1]
-            heads_ref[chunk, pl.ds(pl.multiple_of(h * DH, DH), DH), :] = mixed.astype(BF)
-            return carry
-
-        lax.fori_loop(0, chunks * HEADS, head, 0)
+    def head(h, rows, shift):
+        g = h // 4
+        mine = (lane % 128) // HALF == h % 4
+        queries = jnp.where(mine, q_ref[g, rows, :], jnp.zeros((), BF))
+        scores = lax.dot_general(k_ref[g], queries, NT, preferred_element_type=F32)
+        if shift:
+            alive = lax.broadcasted_iota(jnp.int32, (k_ref.shape[1], 1), 0) < length_ref[0]
+            scores = jnp.where(alive, scores, -1e30)
+            scores = scores - jnp.max(scores, axis=0, keepdims=True)
+        powers = jnp.exp2(scores).astype(BF)
+        mixed = jnp.dot(v_ref[h], powers, preferred_element_type=F32)
+        mixed = mixed[:DH] * (1.0 / mixed[DH : DH + 1])
+        heads_ref[pl.ds(pl.multiple_of(h * DH, DH), DH), rows] = mixed.astype(BF)
+
+    columns = owners * half
 
     @pl.when(fits)
     def _():
-        attend(False)
+        def step(h, carry):
+            head(h, slice(0, chunks * columns), False)
+            return carry
+
+        lax.fori_loop(0, HEADS, step, 0)
 
     @pl.when(jnp.logical_not(fits))
     def _():
-        attend(True)
+        def step(n, carry):
+            head(n % HEADS, pl.ds(pl.multiple_of(n // HEADS * columns, columns), columns), True)
+            return carry
+
+        lax.fori_loop(0, chunks * HEADS, step, 0)
 
     for chunk in range(chunks):
-        projected = lax.dot_general(heads_ref[chunk], wout_ref[...], TN, preferred_element_type=F32)
+        heads = heads_ref[:, chunk * columns : (chunk + 1) * columns]
+        projected = lax.dot_general(heads, wout_ref[...], TN, preferred_element_type=F32)
         out_ref[chunk] = (x_ref[chunk].astype(F32) + projected.reshape(owners, half, width)).astype(BF)
 
 
@@ -316,8 +353,8 @@
         out_shape=jax.ShapeDtypeStruct(sequence.shape, BF),
         in_specs=[smem()] + [whole()] * 6,
         out_specs=whole(),
-        scratch_shapes=[VMEM((chunks, HEADS * DH, owners * half), BF)],
-        compiler_params=pltpu.CompilerParams(vmem_limit_bytes=TIME_LIMIT),
+        scratch_shapes=[VMEM((HEADS * DH, chunks * owners * half), BF)],
+        compiler_params=pltpu.CompilerParams(vmem_limit_bytes=44 * 2**20),
         cost_estimate=pl.CostEstimate(flops=4 * 10**10, bytes_accessed=8 * 10**6, transcendentals=0),
     )(lengths, most, sequence, wout, q, k, v)
 
@@ -368,16 +405,19 @@
     grad_ref[...] = jnp.zeros_like(grad_ref)
     pl.semaphore_wait(barrier, seq - 1 + songs - 1)
 
-    def copy(n, i):
+    pieces = [(0, slice(0, chunk)), (1, slice(0, FRAMES_EACH)), (1, slice(FRAMES_EACH, 2 * FRAMES_EACH))]
+
+    def copy(p, i):
         k = other(i)
+        n, frames = pieces[p]
         return pltpu.make_async_remote_copy(
-            src_ref=timed_ref.at[n, k], dst_ref=got.at[n, me], send_sem=send_sem.at[n, i], recv_sem=recv_sem.at[n, i],
+            src_ref=timed_ref.at[n, k, frames], dst_ref=got.at[n, me, frames], send_sem=send_sem.at[p, i], recv_sem=recv_sem.at[p, i],
             device_id=(k, song), device_id_type=MESH)
 
-    for n in range(2):
+    for p in range(3):
 
         def start(i, carry):
-            copy(n, seq - i).start()
+            copy(p, seq - i).start()
             return carry
 
         lax.fori_loop(1, seq, start, 0)
@@ -385,15 +425,16 @@
     length = length_ref[0]
     cot_copy.wait()
 
-    def attend(n):
+    def attend(p):
         def arrive(i, carry):
-            copy(n, seq - i).wait()
+            copy(p, seq - i).wait()
             return carry
 
         lax.fori_loop(1, seq, arrive, 0)
-        first = n * blocks
+        n, frames = pieces[p]
 
         def block(i, carry):
+            first = n * blocks
             piece = got[n, :, pl.ds(pl.multiple_of(i * FRAMES_EACH, FRAMES_EACH), FRAMES_EACH), :].reshape(rows, width)
             values_x = jnp.dot(order, piece, preferred_element_type=F32)
             here = pl.ds(pl.multiple_of((i + first) * rows, rows), rows)
@@ -408,7 +449,7 @@
                 queries = (jnp.concatenate([qa, qb], axis=1) * (LOG2E * DH**-0.5)).astype(BF)
                 ka, kb = rope(jnp.dot(normed, wk[g], preferred_element_type=F32), cosine, sines)
                 keys = jnp.concatenate([ka, kb], axis=1).astype(BF)
-                pieces = []
+                stacks = []
                 for s in range(rows // half):
                     part = slice(s * half, (s + 1) * half)
                     stacked = jnp.concatenate(
@@ -422,8 +463,8 @@
                     joined = mixed[:half]
                     for h in range(1, 4):
                         joined = jnp.where(lane // DH == h, mixed[h * half : (h + 1) * half], joined)
-                    pieces.append(joined.astype(BF))
-                joined_groups.append(jnp.concatenate(pieces, axis=0))
+                    stacks.append(joined.astype(BF))
+                joined_groups.append(jnp.concatenate(stacks, axis=0))
             heads = jnp.concatenate(joined_groups, axis=1)
             heads_ref[here, :] = heads
             frame = me * (2 * chunk) + (i + first) * FRAMES_EACH + lax.broadcasted_iota(jnp.int32, (rows, 1), 0) // bands
@@ -431,7 +472,7 @@
             grad_ref[...] += lax.dot_general(heads, tangent, TN, preferred_element_type=F32)
             return carry
 
-        lax.fori_loop(0, blocks, block, 0)
+        lax.fori_loop(frames.start // FRAMES_EACH, frames.stop // FRAMES_EACH, block, 0)
 
     def out_copy(i):
         here = slice(i * rows, (i + 1) * rows)
@@ -445,6 +486,7 @@
 
     attend(0)
     attend(1)
+    attend(2)
 
     def remote(src_ref, dst_ref, send, recv, device):
         return pltpu.make_async_remote_copy(
@@ -533,7 +575,7 @@
             VMEM((16, inner // 32, width), BF),
             VMEM((songs, inner // 32, width), F32),
             VMEM((2, 16, inner // 32, width), BF),
-            dma, dma((4,)), dma((2, seq)), dma((2, seq)), dma, dma, dma((16,)), dma((16,)),
+            dma, dma((4,)), dma((3, seq)), dma((3, seq)), dma, dma, dma((16,)), dma((16,)),
             dma((songs,)), dma((songs,)), dma((16,)), dma((16,)), dma, dma,
         ],
         compiler_params=pltpu.CompilerParams(collective_id=2, has_side_effects=True, vmem_limit_bytes=36 * 2**20),

time: 156 us -> 155 us (level)
    pallas_call x1, Pallas kernels: 5.99 us -> 9.42 us  [embed(): pl.pallas_call(functools.partial(embed_kernel, bands), grid=(1,), out_sha...]
    pallas_call x1, Pallas kernels: 57.8 us -> 55.6 us  [finish(): pl.pallas_call(functools.partial(finish_kernel, seq, songs), out_shape=(j...]
    unnamed x31 -> x27, local copies, waits for them, and re-layouts: 6.67 us -> 4.53 us
where the time goes in v5:
time: 155 us
  Pallas kernels  147 us (95%)
  local copies, waits for them, and re-layouts  5.94 us (4%)
    pallas_call x1, Pallas kernels, finish(): pl.pallas_call(functools.partial(finish_kernel, seq, songs), out_shape=(j...  55.6 us
    pallas_call x1, Pallas kernels, time_attention(): pl.pallas_call(time_kernel, out_shape=jax.ShapeDtypeStruct(sequence.shape...  51.5 us
    pallas_call x1, Pallas kernels, exchange(): pl.pallas_call(functools.partial(exchange_kernel, seq), out_shape=(jax.Sh...  30 us
    pallas_call x1, Pallas kernels, embed(): pl.pallas_call(functools.partial(embed_kernel, bands), grid=(1,), out_sha...  9.42 us
    unnamed x27, local copies, waits for them, and re-layouts  4.53 us

profile of v5, /device:TPU:1, one launch (start us, length us, event | category | flops | bytes accessed | tf_op | source)
XLA Modules:
  0.0 154.9 jit_solution(14539920578161496674)
XLA Ops:
  1.3 1.4 broadcast_in_dim.3.gain_ref
  2.7 0.0 copy-start.2
  2.7 0.0 copy-start.6
  2.7 0.0 copy-start.8
  2.7 0.0 copy-start.9
  2.7 9.4 %shard_map.176.bands_ref = bf16[32,64,384]{2,1,0:T(8,128)(2,1)} custom-call(s32[32]{0:T(128)} %widths_ref.1, bf16[64,8196]{1,0:T(8,128)(2,1)} %bitcast.5, f32[1,8196]{1,0:T(1,128)} %broadcast_in_dim.3.gain_ref, bf16[8196,384]{1,0:T(8,128)(2,1)} %last_ref.1, bf16[8196,384]{1,0:T(8,128)(2,1)} %last_ref.1, f32[32,384]{1,0:T(8,128)} %bias_ref.1), custom_call_target="tpu_custom_call" | custom-call | flops 2000000000 | bytes 9000000 | tf_op jit(solution)/shard_map/pallas_call | solution.py:140
  12.1 0.0 copy-done.2
  12.1 0.0 copy-done.6
  12.1 0.0 copy-done.8
  12.1 0.0 copy-done.9
  12.2 0.0 copy-start
  12.2 1.4 copy-done
  13.6 0.0 copy-start.4
  13.6 30.0 %shard_map.177 = (bf16[2,32,32,384]{3,2,1,0:T(8,128)(2,1)S(1)}, bf16[2,2048,256]{2,1,0:T(8,128)(2,1)S(1)}, bf16[2,2048,256]{2,1,0:T(8,128)(2,1)S(1)}, bf16[8,128,2048]{2,1,0:T(8,128)(2,1)S(1)}, f32[5,128]{1,0:T(8,128)S(1)}) custom-call(s32[1]{0:T(128)S(6)} %copy.20.length_ref, bf16[32,64,384]{2,1,0:T(8,128)(2,1)S(1)} %copy-done, f32[384]{0:T(512)S(1)} %copy-done.6, ...), custom_call_target="tpu_custom_call" | custom-call | flops 4000000000 | bytes 10000000 | tf_op jit(solution)/shard_map/pallas_call | solution.py:285
  43.6 0.0 copy-start.12
  43.6 1.9 %copy-done.12 = bf16[8,128,2048]{2,1,0:T(8,128)(2,1)} copy-done((bf16[8,128,2048]{2,1,0:T(8,128)(2,1)}, bf16[8,128,2048]{2,1,0:T(8,128)(2,1)S(1)}, u32[]{:S(2)}) %copy-start.12) | copy-done | bytes 4194328
  45.6 0.0 copy-done.4
  45.6 0.0 copy-start.1
  45.6 0.0 copy-start.3
  45.6 0.0 copy-start.5
  45.6 0.0 copy-start.7
  45.6 0.0 copy-start.10
  45.6 0.0 copy-start.11
  45.6 51.5 %shard_map.178.timed_ref = bf16[2,32,32,384]{3,2,1,0:T(8,128)(2,1)S(1)} custom-call(s32[1]{0:T(128)S(6)} %copy.20.length_ref, f32[5,128]{1,0:T(8,128)S(1)} %get-tuple-element.9.most_ref, bf16[2,32,32,384]{3,2,1,0:T(8,128)(2,1)S(1)} %get-tuple-element.10.x_ref, bf16[512,384]{1,0:T(8,128)(2,1)S(1)} %copy-done.4, ...), custom_call_target="tpu_custom_call" | custom-call | flops 40000000000 | bytes 8000000 | tf_op jit(solution)/shard_map/pallas_call | solution.py:351
  97.1 0.0 copy-done.1
  97.2 0.0 copy-done.3
  97.2 0.0 copy-done.5
  97.2 0.0 copy-done.7
  97.2 0.0 copy-done.10
  97.2 0.0 copy-done.11
  97.2 55.6 %shard_map.179 = (bf16[2048,384]{1,0:T(8,128)(2,1)S(1)}, bf16[512,384]{1,0:T(8,128)(2,1)S(1)}) custom-call(s32[1]{0:T(128)S(6)} %copy.20.length_ref, bf16[2,32,32,384]{3,2,1,0:T(8,128)(2,1)S(1)} %shard_map.178.timed_ref, f32[384]{0:T(512)S(1)} %copy-done.7, bf16[384,1536]{1,0:T(8,128)(2,1)S(1)} %copy-done.3, bf16[512,384]{1,0:T(8,128)(2,1)S(1)} %copy-done.5, ...), custom_call_target="tpu_custom_call" | custom-call | flops 10000000000 | bytes 7000000 | tf_op jit(solution)/shard_map/pallas_call | solution.py:560
  152.8 0.9 convert_element_type.3
  153.7 1.1 copy.21
Async XLA Ops:
  2.7 9.4 %copy-start.2 = (bf16[384,1536]{1,0:T(8,128)(2,1)S(1)}, bf16[384,1536]{1,0:T(8,128)(2,1)}, u32[]{:S(2)}) copy-start(bf16[384,1536]{1,0:T(8,128)(2,1)} %wqkv_ref.2) | copy-start | bytes 3538948
  2.7 9.4 %copy-start.6 = (f32[384]{0:T(512)S(1)}, f32[384]{0:T(512)}, u32[]{:S(2)}) copy-start(f32[384]{0:T(512)} %gain_ref.2) | copy-start | bytes 4612
  2.7 9.5 %copy-start.8 = (f32[2048,128]{1,0:T(8,128)S(1)}, f32[2048,128]{1,0:T(8,128)}, u32[]{:S(2)}) copy-start(f32[2048,128]{1,0:T(8,128)} %constant.9.clone.sin_ref) | copy-start | bytes 3145732
  2.7 9.5 %copy-start.9 = (f32[2048,128]{1,0:T(8,128)S(1)}, f32[2048,128]{1,0:T(8,128)}, u32[]{:S(2)}) copy-start(f32[2048,128]{1,0:T(8,128)} %constant.8.clone.cos_ref) | copy-start | bytes 3145732
  12.2 1.4 copy-start
  13.6 32.0 %copy-start.4 = (bf16[512,384]{1,0:T(8,128)(2,1)S(1)}, bf16[512,384]{1,0:T(8,128)(2,1)}, u32[]{:S(2)}) copy-start(bf16[512,384]{1,0:T(8,128)(2,1)} %wout_ref.2) | copy-start | bytes 1179652
  43.6 1.9 %copy-start.12 = (bf16[8,128,2048]{2,1,0:T(8,128)(2,1)}, bf16[8,128,2048]{2,1,0:T(8,128)(2,1)S(1)}, u32[]{:S(2)}) copy-start(bf16[8,128,2048]{2,1,0:T(8,128)(2,1)S(1)} %get-tuple-element.13.v_ref) | copy-start | bytes 12582916
  45.6 51.6 %copy-start.1 = (bf16[1,64,32,384]{3,2,1,0:T(8,128)(2,1)S(1)}, bf16[1,64,32,384]{3,2,1,0:T(8,128)(2,1)}, u32[]{:S(2)}) copy-start(bf16[1,64,32,384]{3,2,1,0:T(8,128)(2,1)} %param.29) | copy-start | bytes 4718596
  45.6 51.6 %copy-start.3 = (bf16[384,1536]{1,0:T(8,128)(2,1)S(1)}, bf16[384,1536]{1,0:T(8,128)(2,1)}, u32[]{:S(2)}) copy-start(bf16[384,1536]{1,0:T(8,128)(2,1)} %wqkv_ref.3) | copy-start | bytes 3538948
  45.6 51.6 %copy-start.5 = (bf16[512,384]{1,0:T(8,128)(2,1)S(1)}, bf16[512,384]{1,0:T(8,128)(2,1)}, u32[]{:S(2)}) copy-start(bf16[512,384]{1,0:T(8,128)(2,1)} %wout_ref.3) | copy-start | bytes 1179652
  45.6 51.6 %copy-start.7 = (f32[384]{0:T(512)S(1)}, f32[384]{0:T(512)}, u32[]{:S(2)}) copy-start(f32[384]{0:T(512)} %gain_ref.3) | copy-start | bytes 4612
  45.6 51.6 %copy-start.10 = (f32[512,128]{1,0:T(8,128)S(1)}, f32[512,128]{1,0:T(8,128)}, u32[]{:S(2)}) copy-start(f32[512,128]{1,0:T(8,128)} %constant.11.clone.sin_ref) | copy-start | bytes 786436
  45.6 51.6 %copy-start.11 = (f32[512,128]{1,0:T(8,128)S(1)}, f32[512,128]{1,0:T(8,128)}, u32[]{:S(2)}) copy-start(f32[512,128]{1,0:T(8,128)} %constant.10.clone.cos_ref) | copy-start | bytes 786436

commit v6 on v5

--- a/solution.py
+++ b/solution.py
@@ -62,108 +62,12 @@
     return leading * cosine - second * sines, second * cosine + leading * sines
 
 
-NARROW = 640
-
-
-def embed_kernel(bands, widths_ref, x_ref, gain_ref, w_hbm, last_ref, bias_ref, out_ref, starts_ref, w_ref, normed_ref, tail_ref, w_sem):
-    limit = x_ref.shape[1]
-    main = limit // 128 * 128
-    each = main // 4
-
-    def load(n):
-        here = pl.ds(n * each, each)
-        return pltpu.make_async_copy(w_hbm.at[here], w_ref.at[here], w_sem.at[n])
-
-    for n in range(4):
-        load(n).start()
-    total = 0
-    for k in range(bands):
-        starts_ref[k] = total
-        total = total + widths_ref[k] * 4
-
-    def window(k, size):
-        return pl.multiple_of(jnp.minimum(starts_ref[k] // 128, (main - size) // 128) * 128, 128)
-
-    def normalise(k, size):
-        first = starts_ref[k]
-        count = widths_ref[k] * 4
-        begin = window(k, size)
-        entry = lax.broadcasted_iota(jnp.int32, (1, size), 1) + begin
-        piece = x_ref[:, pl.ds(begin, size)].astype(F32)
-        piece = jnp.where((entry >= first) & (entry < first + count), piece, 0.0)
-        tail = jnp.where(k == bands - 1, x_ref[:, main:].astype(F32), 0.0)
-        square = jnp.sum(piece * piece, axis=1, keepdims=True) + jnp.sum(tail * tail, axis=1, keepdims=True)
-        scale = 1.0 / jnp.sqrt(jnp.maximum(square / count.astype(F32), FLOOR))
-        normed_ref[k, :, :size] = (piece * scale * gain_ref[:, pl.ds(begin, size)]).astype(BF)
-        tail_ref[k] = (tail * scale * gain_ref[:, main:]).astype(BF)
-
-    def project(k, size):
-        summed = jnp.dot(normed_ref[k, :, :size], w_ref[pl.ds(window(k, size), size), :], preferred_element_type=F32)
-        summed = summed + bias_ref[pl.ds(k, 1), :]
-        tail = tail_ref[k].astype(F32)
-        rows = last_ref[...].astype(F32)
-        for e in range(limit - main):
-            summed = summed + tail[:, e : e + 1] * rows[e : e + 1, :]
-        out_ref[k] = summed.astype(BF)
-
-    def step(work, i, carry):
-        narrow = widths_ref[4 * i] * 4 <= NARROW - 124
-        for j in range(1, 4):
-            narrow = narrow & (widths_ref[4 * i + j] * 4 <= NARROW - 124)
-
-        @pl.when(narrow)
-        def _():
-            for j in range(4):
-                work(4 * i + j, NARROW)
-
-        @pl.when(jnp.logical_not(narrow))
-        def _():
-            for j in range(4):
-                work(4 * i + j, WINDOW)
-
-        return carry
-
-    lax.fori_loop(0, bands // 4, functools.partial(step, normalise), 0)
-    for n in range(4):
-        load(n).wait()
-    lax.fori_loop(0, bands // 4, functools.partial(step, project), 0)
-
-
-def embed(spectrum, widths, bin_gain, embed_weight, embed_bias):
-    frames, feature_count = spectrum.shape
-    bands, width = embed_bias.shape
-    main = feature_count // 128 * 128
-
-    def full(*shape):
-        return pl.BlockSpec(shape, lambda i: (0,) * len(shape))
-
-    return pl.pallas_call(
-        functools.partial(embed_kernel, bands),
-        grid=(1,),
-        out_shape=jax.ShapeDtypeStruct((bands, frames, width), BF),
-        in_specs=[
-            smem(), full(frames, feature_count), full(1, feature_count), pl.BlockSpec(memory_space=pl.ANY),
-            pl.BlockSpec((16, width), lambda i: (main // 16, 0)), full(bands, width),
-        ],
-        out_specs=full(bands, frames, width),
-        scratch_shapes=[
-            pltpu.SMEM((bands,), jnp.int32),
-            VMEM((main, width), BF),
-            VMEM((bands, frames, WINDOW), BF),
-            VMEM((bands, frames, feature_count - main), BF),
-            pltpu.SemaphoreType.DMA((4,)),
-        ],
-        compiler_params=pltpu.CompilerParams(vmem_limit_bytes=60 * 2**20),
-        cost_estimate=pl.CostEstimate(flops=2 * 10**9, bytes_accessed=9 * 10**6, transcendentals=0),
-    )(widths, spectrum, bin_gain[None], embed_weight, embed_weight, embed_bias)
-
-
 VROWS = 128
 
 
 def exchange_kernel(
-    seq, length_ref, bands_ref, gain_ref, wqkv_ref, cos_ref, sin_ref,
-    x_ref, q_ref, k_ref, v_ref, most_ref, got, send_sem, recv_sem,
+    seq, length_ref, meta_ref, spectrum_ref, bin_gain_ref, w_hbm, last_ref, bias_ref, gain_ref, wqkv_ref, cos_ref, sin_ref,
+    x_ref, q_ref, k_ref, v_ref, most_ref, got, stage, w_ref, spec_ref, spec_gain_ref, w_sem, send_sem, recv_sem,
 ):
     frames, width = got.shape[1:]
     half = frames // 2
@@ -182,31 +86,79 @@
         return carry
 
     lax.fori_loop(1, seq, greet, 0)
+    blocks = w_ref.shape[0]
+    main = blocks * 128
+    bands = bias_ref.shape[0]
+
+    def load(n):
+        return pltpu.make_async_copy(w_hbm.at[pl.ds(pl.multiple_of(n * 128, 128), 128)], w_ref.at[n], w_sem.at[n])
+
+    def start_load(n, carry):
+        load(n).start()
+        return carry
+
+    def wait_load(n, carry):
+        load(n).wait()
+        return carry
+
+    lax.fori_loop(0, blocks, start_load, 0)
+    for n in range(blocks):
+        spec_ref[n] = spectrum_ref[:, n * 128 : (n + 1) * 128]
+        spec_gain_ref[n] = bin_gain_ref[:, n * 128 : (n + 1) * 128]
     lane = lax.broadcasted_iota(jnp.int32, (1, GROUP), 1)
     wq = [split_halves(wqkv_ref[:, g * GROUP : (g + 1) * GROUP]) for g in range(2)]
     wk = [split_halves(wqkv_ref[:, inner + g * GROUP : inner + (g + 1) * GROUP]) for g in range(2)]
     wv = wqkv_ref[:, 2 * inner :]
-    pl.semaphore_wait(barrier, seq - 1)
+    lax.fori_loop(0, blocks, wait_load, 0)
+
+    def band(k):
+        first = meta_ref[0, k]
+        count = meta_ref[1, k]
+        block = meta_ref[2, k]
+        near = range(WINDOW // 128)
+        entry = lax.broadcasted_iota(jnp.int32, (1, WINDOW), 1) + block * 128
+        piece = jnp.concatenate([spec_ref[block + n] for n in near], axis=1).astype(F32)
+        gains = jnp.concatenate([spec_gain_ref[block + n] for n in near], axis=1)
+        weights = jnp.concatenate([w_ref[block + n] for n in near], axis=0)
+        piece = jnp.where((entry >= first) & (entry < first + count), piece, 0.0)
+        tail = jnp.where(k == bands - 1, spectrum_ref[:, main:].astype(F32), 0.0)
+        square = jnp.sum(piece * piece, axis=1, keepdims=True) + jnp.sum(tail * tail, axis=1, keepdims=True)
+        scale = 1.0 / jnp.sqrt(jnp.maximum(square / count.astype(F32), FLOOR))
+        normed = (piece * scale * gains).astype(BF)
+        summed = jnp.dot(normed, weights, preferred_element_type=F32) + bias_ref[pl.ds(k, 1), :]
+        tail = (tail * scale * bin_gain_ref[:, main:]).astype(BF).astype(F32)
+        rows = last_ref[...].astype(F32)
+        for e in range(spectrum_ref.shape[1] - main):
+            summed = summed + tail[:, e : e + 1] * rows[e : e + 1, :]
+        stage[k] = summed.astype(BF)
 
     def copy(i):
         k = other(i, 1)
         return pltpu.make_async_remote_copy(
-            src_ref=bands_ref.at[k], dst_ref=got.at[me], send_sem=send_sem.at[i], recv_sem=recv_sem.at[i],
+            src_ref=stage.at[k], dst_ref=got.at[me], send_sem=send_sem.at[i], recv_sem=recv_sem.at[i],
             device_id=(k, song), device_id_type=MESH)
 
-    def start(j, carry):
-        copy(8 * (1 + 2 * (j % 2)) + j // 2).start()
-        return carry
-
-    def start_rest(j, carry):
-        copy(16 + j).start()
-        copy(j).start()
-        return carry
-
-    lax.fori_loop(0, 16, start, 0)
+    def front(j, carry):
+        for n in range(2):
+            band(other(8 + 16 * n + j, 1))
+        for n in range(2):
+            copy(8 + 16 * n + j).start()
+        return carry
+
+    def back(j, carry):
+        for n in range(2):
+            band(other(j + 16 * n, 1))
+        for n in range(2):
+            copy(j + 16 * n).start()
+        return carry
+
+    pl.semaphore_wait(barrier, seq - 1)
+    lax.fori_loop(0, 8, front, 0)
+    band(other(16, 1))
     copy(16).start()
-    lax.fori_loop(1, 8, start_rest, 0)
-    got[me] = bands_ref[me]
+    lax.fori_loop(1, 8, back, 0)
+    band(me)
+    got[me] = stage[me]
     length = length_ref[0]
 
     heads_of = lax.broadcasted_iota(jnp.int32, (GROUP, 128), 0) % 128 // HALF
@@ -276,27 +228,43 @@
     lax.fori_loop(1, seq, finish, 0)
 
 
-def exchange(computed, lengths, gain, wqkv):
+def exchange(spectrum, widths, bin_gain, embed_weight, embed_bias, lengths, gain, wqkv):
     seq = lax.axis_size("seq")
-    bands, frames, width = computed.shape
+    frames, feature_count = spectrum.shape
+    bands, width = embed_bias.shape
     count = seq * frames
+    blocks = feature_count // 128
+    main = blocks * 128
+    starts = (jnp.cumsum(widths) - widths) * 4
+    meta = jnp.stack([starts, widths * 4, jnp.minimum(starts // 128, blocks - WINDOW // 128)]).astype(jnp.int32)
     cosine, sines = rotary_tables(np.arange(count), 4)
     dma = pltpu.SemaphoreType.DMA
+
+    def full(*shape):
+        return pl.BlockSpec(shape, lambda i: (0,) * len(shape))
+
+    shapes = [(2, seq, frames // 2, width), (2, count, GROUP), (2, count, GROUP), (HEADS, VROWS, count)]
     return pl.pallas_call(
         functools.partial(exchange_kernel, seq),
-        out_shape=(
-            jax.ShapeDtypeStruct((2, seq, frames // 2, width), BF),
-            jax.ShapeDtypeStruct((2, count, GROUP), BF),
-            jax.ShapeDtypeStruct((2, count, GROUP), BF),
-            jax.ShapeDtypeStruct((HEADS, VROWS, count), BF),
-            jax.ShapeDtypeStruct((5, 128), F32),
-        ),
-        in_specs=[smem()] + [whole()] * 5,
-        out_specs=[whole()] * 5,
-        scratch_shapes=[VMEM((seq, frames, width), BF), dma((seq,)), dma((seq,))],
-        compiler_params=pltpu.CompilerParams(collective_id=1, has_side_effects=True, vmem_limit_bytes=TIME_LIMIT),
+        grid=(1,),
+        out_shape=[jax.ShapeDtypeStruct(shape, BF) for shape in shapes] + [jax.ShapeDtypeStruct((5, 128), F32)],
+        in_specs=[
+            smem(), smem(), full(frames, feature_count), full(1, feature_count), pl.BlockSpec(memory_space=pl.ANY),
+            pl.BlockSpec((16, width), lambda i: (main // 16, 0)), full(bands, width), full(width), full(*wqkv.shape),
+            full(count, 128), full(count, 128),
+        ],
+        out_specs=[full(*shape) for shape in shapes] + [full(5, 128)],
+        scratch_shapes=[
+            VMEM((seq, frames, width), BF),
+            VMEM((bands, frames, width), BF),
+            VMEM((blocks, 128, width), BF),
+            VMEM((blocks, frames, 128), BF),
+            VMEM((blocks, 1, 128), F32),
+            dma((blocks,)), dma((seq,)), dma((seq,)),
+        ],
+        compiler_params=pltpu.CompilerParams(collective_id=1, has_side_effects=True, vmem_limit_bytes=36 * 2**20),
         cost_estimate=pl.CostEstimate(flops=4 * 10**9, bytes_accessed=10 * 10**6, transcendentals=0),
-    )(lengths, computed, gain, wqkv, jnp.asarray(cosine), jnp.asarray(sines))
+    )(lengths, meta, spectrum, bin_gain[None], embed_weight, embed_weight, embed_bias, gain, wqkv, jnp.asarray(cosine), jnp.asarray(sines))
 
 
 TIME_LIMIT = 28 * 2**20
@@ -354,7 +322,7 @@
         in_specs=[smem()] + [whole()] * 6,
         out_specs=whole(),
         scratch_shapes=[VMEM((HEADS * DH, chunks * owners * half), BF)],
-        compiler_params=pltpu.CompilerParams(vmem_limit_bytes=44 * 2**20),
+        compiler_params=pltpu.CompilerParams(vmem_limit_bytes=36 * 2**20),
         cost_estimate=pl.CostEstimate(flops=4 * 10**10, bytes_accessed=8 * 10**6, transcendentals=0),
     )(lengths, most, sequence, wout, q, k, v)
 
@@ -586,9 +554,8 @@
 def per_device(spectrum, widths, lengths, bin_gain, embed_weight, embed_bias, time_gain, time_qkv, time_out, band_gain, band_qkv, band_out, cotangent):
     local_frames = spectrum.shape[1]
     bands, width = embed_bias.shape
-    computed = embed(spectrum[0], widths, bin_gain, embed_weight, embed_bias)
     tangent = cotangent.reshape(local_frames * bands, width)
-    owned, q, k, v, most = exchange(computed, lengths, time_gain, time_qkv)
+    owned, q, k, v, most = exchange(spectrum[0], widths, bin_gain, embed_weight, embed_bias, lengths, time_gain, time_qkv)
     timed = time_attention(lengths, most, owned, time_out, q, k, v)
     output, gradient = finish(lengths, timed, band_gain, band_qkv, band_out, tangent)
     return output.reshape(1, local_frames, bands, width), gradient.astype(F32)

time: 155 us -> 152 us (0.981)
  Pallas kernels: 147 us -> 139 us
  local copies, waits for them, and re-layouts: 5.94 us -> 9.14 us
    pallas_call x2 -> x1, Pallas kernels: 39.5 us -> 34.1 us  [exchange(): pl.pallas_call(functools.partial(exchange_kernel, seq), grid=(1,), out_sh...]
    unnamed x27, local copies, waits for them, and re-layouts: 4.53 us -> 7.61 us
    pallas_call x1, Pallas kernels: 51.5 us -> 49.6 us  [time_attention(): pl.pallas_call(time_kernel, out_shape=jax.ShapeDtypeStruct(sequence.shape...]
where the time goes in v6:
time: 152 us; the launch traced here: 151 us
  Pallas kernels  139 us (91%)
  local copies, waits for them, and re-layouts  9.14 us (6%)
  other arithmetic  1.79 us (1%)
    pallas_call x1, Pallas kernels, finish(): pl.pallas_call(functools.partial(finish_kernel, seq, songs), out_shape=(j...  55.2 us
    pallas_call x1, Pallas kernels, time_attention(): pl.pallas_call(time_kernel, out_shape=jax.ShapeDtypeStruct(sequence.shape...  49.6 us
    pallas_call x1, Pallas kernels, exchange(): pl.pallas_call(functools.partial(exchange_kernel, seq), grid=(1,), out_sh...  34.1 us
    unnamed x27, local copies, waits for them, and re-layouts  7.61 us

profile of v6, /device:TPU:1, one launch (start us, length us, event | category | flops | bytes accessed | tf_op | source)
XLA Modules:
  0.0 151.3 jit_solution(3233134818754872624)
XLA Ops:
  1.3 0.7 copy.20
  2.0 0.1 reduce-window.9
  2.1 0.1 reduce
  2.2 0.7 fusion
  2.9 0.8 broadcast_in_dim.3.bin_gain_ref
  3.7 0.0 copy-start
  3.7 1.3 copy-done
  4.9 0.0 copy-start.1
  4.9 1.2 copy-done.1
  6.2 0.0 copy-start.2
  6.2 1.2 copy-done.2
  7.4 0.0 copy-start.3
  7.4 1.2 copy-done.3
  8.6 0.0 copy-start.4
  8.6 0.8 copy-done.4
  9.4 0.0 copy-start.5
  9.4 0.7 copy-done.5
  10.1 0.0 copy-start.8
  10.1 34.1 %shard_map.176 = (bf16[2,32,32,384]{3,2,1,0:T(8,128)(2,1)S(1)}, bf16[2,2048,256]{2,1,0:T(8,128)(2,1)S(1)}, bf16[2,2048,256]{2,1,0:T(8,128)(2,1)S(1)}, bf16[8,128,2048]{2,1,0:T(8,128)(2,1)S(1)}, f32[5,128]{1,0:T(8,128)S(1)}) custom-call(s32[1]{0:T(128)S(6)} %copy.22.length_ref, s32[3,32]{1,0:T(4,128)S(1)} %pad_add_fusion.meta_ref, ...), custom_call_target="tpu_custom_call" | custom-call | flops 4000000000 | bytes 10000000 | tf_op jit(solution)/shard_map/pallas_call | solution.py:247
  44.2 0.0 copy-done.8
  44.3 0.0 copy-start.6
  44.3 0.0 copy-start.7
  44.3 0.0 copy-start.9
  44.3 0.0 copy-start.10
  44.3 0.0 copy-start.11
  44.3 0.0 copy-start.12
  44.3 49.6 %shard_map.177.timed_ref = bf16[2,32,32,384]{3,2,1,0:T(8,128)(2,1)S(1)} custom-call(s32[1]{0:T(128)S(6)} %copy.22.length_ref, f32[5,128]{1,0:T(8,128)S(1)} %get-tuple-element.9.most_ref, bf16[2,32,32,384]{3,2,1,0:T(8,128)(2,1)S(1)} %get-tuple-element.10.x_ref, bf16[512,384]{1,0:T(8,128)(2,1)S(1)} %copy-done.8, ...), custom_call_target="tpu_custom_call" | custom-call | flops 40000000000 | bytes 8000000 | tf_op jit(solution)/shard_map/pallas_call | solution.py:319
  93.9 0.0 copy-done.6
  94.0 0.0 copy-done.7
  94.0 0.0 copy-done.9
  94.0 0.0 copy-done.10
  94.0 0.0 copy-done.11
  94.0 0.0 copy-done.12
  94.0 55.2 %shard_map.178 = (bf16[2048,384]{1,0:T(8,128)(2,1)S(1)}, bf16[512,384]{1,0:T(8,128)(2,1)S(1)}) custom-call(s32[1]{0:T(128)S(6)} %copy.22.length_ref, bf16[2,32,32,384]{3,2,1,0:T(8,128)(2,1)S(1)} %shard_map.177.timed_ref, f32[384]{0:T(512)S(1)} %copy-done.10, bf16[384,1536]{1,0:T(8,128)(2,1)S(1)} %copy-done.7, bf16[512,384]{1,0:T(8,128)(2,1)S(1)} %copy-done.9, ...), custom_call_target="tpu_custom_call" | custom-call | flops 10000000000 | bytes 7000000 | tf_op jit(solution)/shard_map/pallas_call | solution.py:528
  149.3 0.9 convert_element_type.3
  150.2 1.1 copy.23
  (1 shorter events, 0.0 us)
Async XLA Ops:
  3.7 1.3 copy-start
  4.9 1.2 copy-start.1
  6.2 1.2 copy-start.2
  7.4 1.2 copy-start.3
  8.6 0.8 copy-start.4
  9.4 0.7 copy-start.5
  10.1 34.1 %copy-start.8 = (bf16[512,384]{1,0:T(8,128)(2,1)S(1)}, bf16[512,384]{1,0:T(8,128)(2,1)}, u32[]{:S(2)}) copy-start(bf16[512,384]{1,0:T(8,128)(2,1)} %wout_ref.2) | copy-start | bytes 1179652
  44.3 49.7 %copy-start.6 = (bf16[1,64,32,384]{3,2,1,0:T(8,128)(2,1)S(1)}, bf16[1,64,32,384]{3,2,1,0:T(8,128)(2,1)}, u32[]{:S(2)}) copy-start(bf16[1,64,32,384]{3,2,1,0:T(8,128)(2,1)} %param.29) | copy-start | bytes 4718596
  44.3 49.7 %copy-start.7 = (bf16[384,1536]{1,0:T(8,128)(2,1)S(1)}, bf16[384,1536]{1,0:T(8,128)(2,1)}, u32[]{:S(2)}) copy-start(bf16[384,1536]{1,0:T(8,128)(2,1)} %wqkv_ref.3) | copy-start | bytes 3538948
  44.3 49.7 %copy-start.9 = (bf16[512,384]{1,0:T(8,128)(2,1)S(1)}, bf16[512,384]{1,0:T(8,128)(2,1)}, u32[]{:S(2)}) copy-start(bf16[512,384]{1,0:T(8,128)(2,1)} %wout_ref.3) | copy-start | bytes 1179652
  44.3 49.7 %copy-start.10 = (f32[384]{0:T(512)S(1)}, f32[384]{0:T(512)}, u32[]{:S(2)}) copy-start(f32[384]{0:T(512)} %gain_ref.3) | copy-start | bytes 4612
  44.3 49.7 %copy-start.11 = (f32[512,128]{1,0:T(8,128)S(1)}, f32[512,128]{1,0:T(8,128)}, u32[]{:S(2)}) copy-start(f32[512,128]{1,0:T(8,128)} %constant.34.clone.sin_ref) | copy-start | bytes 786436
  44.3 49.7 %copy-start.12 = (f32[512,128]{1,0:T(8,128)S(1)}, f32[512,128]{1,0:T(8,128)}, u32[]{:S(2)}) copy-start(f32[512,128]{1,0:T(8,128)} %constant.33.clone.cos_ref) | copy-start | bytes 786436

commit v7 on v6

--- a/solution.py
+++ b/solution.py
@@ -66,7 +66,7 @@
 
 
 def exchange_kernel(
-    seq, length_ref, meta_ref, spectrum_ref, bin_gain_ref, w_hbm, last_ref, bias_ref, gain_ref, wqkv_ref, cos_ref, sin_ref,
+    seq, length_ref, meta_ref, spectrum_ref, bin_gain_ref, w_hbm, last_ref, bias_ref, gain_ref, wqkv_ref, table_ref,
     x_ref, q_ref, k_ref, v_ref, most_ref, got, stage, w_ref, spec_ref, spec_gain_ref, w_sem, send_sem, recv_sem,
 ):
     frames, width = got.shape[1:]
@@ -184,8 +184,13 @@
         x_ref[0, owners] = received[:, :half]
         x_ref[1, owners] = received[:, half:]
         normed = rms_norm(received.reshape(count, width).astype(F32), gain_ref[...].reshape(1, width))
-        cosine = cos_ref[rows, :]
-        sines = sin_ref[rows, :]
+        cosines, sine_parts = [], []
+        for o in range(8):
+            far = pl.ds(row * 8 + o, 1)
+            cosines.append(table_ref[0, far, :] * table_ref[0, seq:, :] - table_ref[1, far, :] * table_ref[1, seq:, :])
+            sine_parts.append(table_ref[1, far, :] * table_ref[0, seq:, :] + table_ref[0, far, :] * table_ref[1, seq:, :])
+        cosine = jnp.concatenate(cosines, axis=0)
+        sines = jnp.concatenate(sine_parts, axis=0)
         alive_row = (lax.broadcasted_iota(jnp.int32, (count, 1), 0) + base) < length
         alive_col = (lax.broadcasted_iota(jnp.int32, (1, count), 1) + base) < length
         kinds = []
@@ -237,21 +242,23 @@
     main = blocks * 128
     starts = (jnp.cumsum(widths) - widths) * 4
     meta = jnp.stack([starts, widths * 4, jnp.minimum(starts // 128, blocks - WINDOW // 128)]).astype(jnp.int32)
-    cosine, sines = rotary_tables(np.arange(count), 4)
+    positions = np.concatenate([np.arange(seq) * frames, np.arange(frames)])
+    table = np.stack(rotary_tables(positions, 4))
     dma = pltpu.SemaphoreType.DMA
 
     def full(*shape):
         return pl.BlockSpec(shape, lambda i: (0,) * len(shape))
 
+    anywhere = pl.BlockSpec(memory_space=pl.ANY)
     shapes = [(2, seq, frames // 2, width), (2, count, GROUP), (2, count, GROUP), (HEADS, VROWS, count)]
     return pl.pallas_call(
         functools.partial(exchange_kernel, seq),
         grid=(1,),
         out_shape=[jax.ShapeDtypeStruct(shape, BF) for shape in shapes] + [jax.ShapeDtypeStruct((5, 128), F32)],
         in_specs=[
-            smem(), smem(), full(frames, feature_count), full(1, feature_count), pl.BlockSpec(memory_space=pl.ANY),
+            smem(), smem(), full(frames, feature_count), full(1, feature_count), anywhere,
             pl.BlockSpec((16, width), lambda i: (main // 16, 0)), full(bands, width), full(width), full(*wqkv.shape),
-            full(count, 128), full(count, 128),
+            full(*table.shape),
         ],
         out_specs=[full(*shape) for shape in shapes] + [full(5, 128)],
         scratch_shapes=[
@@ -262,9 +269,9 @@
             VMEM((blocks, 1, 128), F32),
             dma((blocks,)), dma((seq,)), dma((seq,)),
         ],
-        compiler_params=pltpu.CompilerParams(collective_id=1, has_side_effects=True, vmem_limit_bytes=36 * 2**20),
+        compiler_params=pltpu.CompilerParams(collective_id=1, has_side_effects=True, vmem_limit_bytes=42 * 2**20),
         cost_estimate=pl.CostEstimate(flops=4 * 10**9, bytes_accessed=10 * 10**6, transcendentals=0),
-    )(lengths, meta, spectrum, bin_gain[None], embed_weight, embed_weight, embed_bias, gain, wqkv, jnp.asarray(cosine), jnp.asarray(sines))
+    )(lengths, meta, spectrum, bin_gain[None], embed_weight, embed_weight, embed_bias, gain, wqkv, jnp.asarray(table))
 
 
 TIME_LIMIT = 28 * 2**20

time: 152 us -> 151 us (level)
  local copies, waits for them, and re-layouts: 9.14 us -> 7.58 us
    unnamed x27 -> x25, local copies, waits for them, and re-layouts: 7.61 us -> 6.05 us
where the time goes in v7:
time: 151 us; the launch traced here: 150 us
  Pallas kernels  140 us (93%)
  local copies, waits for them, and re-layouts  7.58 us (5%)
  other arithmetic  1.79 us (1%)
    pallas_call x1, Pallas kernels, finish(): pl.pallas_call(functools.partial(finish_kernel, seq, songs), out_shape=(j...  55.3 us
    pallas_call x1, Pallas kernels, time_attention(): pl.pallas_call(time_kernel, out_shape=jax.ShapeDtypeStruct(sequence.shape...  50.1 us
    pallas_call x1, Pallas kernels, exchange(): pl.pallas_call(functools.partial(exchange_kernel, seq), grid=(1,), out_sh...  34.2 us
    unnamed x25, local copies, waits for them, and re-layouts  6.05 us

profile of v7, /device:TPU:1, one launch (start us, length us, event | category | flops | bytes accessed | tf_op | source)
XLA Modules:
  0.0 150.3 jit_solution(5473076593284577359)
XLA Ops:
  1.3 0.7 copy.19
  2.0 0.1 reduce-window.9
  2.1 0.1 reduce
  2.2 0.7 fusion
  2.9 0.8 broadcast_in_dim.3.bin_gain_ref
  3.7 0.0 copy-start
  3.7 1.3 copy-done
  4.9 0.0 copy-start.1
  4.9 1.2 copy-done.1
  6.2 0.0 copy-start.2
  6.2 0.9 copy-done.2
  7.1 0.0 copy-start.3
  7.1 0.8 copy-done.3
  7.9 0.0 copy-start.4
  7.9 0.7 copy-done.4
  8.6 0.0 copy-start.7
  8.6 34.2 %shard_map.167 = (bf16[2,32,32,384]{3,2,1,0:T(8,128)(2,1)S(1)}, bf16[2,2048,256]{2,1,0:T(8,128)(2,1)S(1)}, bf16[2,2048,256]{2,1,0:T(8,128)(2,1)S(1)}, bf16[8,128,2048]{2,1,0:T(8,128)(2,1)S(1)}, f32[5,128]{1,0:T(8,128)S(1)}) custom-call(s32[1]{0:T(128)S(6)} %copy.21.length_ref, s32[3,32]{1,0:T(4,128)S(1)} %pad_add_fusion.meta_ref, ...), custom_call_target="tpu_custom_call" | custom-call | flops 4000000000 | bytes 10000000 | tf_op jit(solution)/shard_map/pallas_call | solution.py:254
  42.7 0.0 copy-done.7
  42.7 0.0 copy-start.5
  42.7 0.0 copy-start.6
  42.8 0.0 copy-start.8
  42.8 0.0 copy-start.9
  42.8 0.0 copy-start.10
  42.8 0.0 copy-start.11
  42.8 50.1 %shard_map.168.timed_ref = bf16[2,32,32,384]{3,2,1,0:T(8,128)(2,1)S(1)} custom-call(s32[1]{0:T(128)S(6)} %copy.21.length_ref, f32[5,128]{1,0:T(8,128)S(1)} %get-tuple-element.9.most_ref, bf16[2,32,32,384]{3,2,1,0:T(8,128)(2,1)S(1)} %get-tuple-element.10.x_ref, bf16[512,384]{1,0:T(8,128)(2,1)S(1)} %copy-done.7, ...), custom_call_target="tpu_custom_call" | custom-call | flops 40000000000 | bytes 8000000 | tf_op jit(solution)/shard_map/pallas_call | solution.py:326
  92.9 0.0 copy-done.5
  93.0 0.0 copy-done.6
  93.0 0.0 copy-done.8
  93.0 0.0 copy-done.9
  93.0 0.0 copy-done.10
  93.0 0.0 copy-done.11
  93.0 55.3 %shard_map.169 = (bf16[2048,384]{1,0:T(8,128)(2,1)S(1)}, bf16[512,384]{1,0:T(8,128)(2,1)S(1)}) custom-call(s32[1]{0:T(128)S(6)} %copy.21.length_ref, bf16[2,32,32,384]{3,2,1,0:T(8,128)(2,1)S(1)} %shard_map.168.timed_ref, f32[384]{0:T(512)S(1)} %copy-done.9, bf16[384,1536]{1,0:T(8,128)(2,1)S(1)} %copy-done.6, bf16[512,384]{1,0:T(8,128)(2,1)S(1)} %copy-done.8, ...), custom_call_target="tpu_custom_call" | custom-call | flops 10000000000 | bytes 7000000 | tf_op jit(solution)/shard_map/pallas_call | solution.py:535
  148.3 0.9 convert_element_type.3
  149.2 1.1 copy.22
  (1 shorter events, 0.0 us)
Async XLA Ops:
  3.7 1.3 copy-start
  4.9 1.2 copy-start.1
  6.2 0.9 copy-start.2
  7.1 0.8 copy-start.3
  7.9 0.7 copy-start.4
  8.6 34.2 %copy-start.7 = (bf16[512,384]{1,0:T(8,128)(2,1)S(1)}, bf16[512,384]{1,0:T(8,128)(2,1)}, u32[]{:S(2)}) copy-start(bf16[512,384]{1,0:T(8,128)(2,1)} %wout_ref.2) | copy-start | bytes 1179652
  42.7 50.2 %copy-start.5 = (bf16[1,64,32,384]{3,2,1,0:T(8,128)(2,1)S(1)}, bf16[1,64,32,384]{3,2,1,0:T(8,128)(2,1)}, u32[]{:S(2)}) copy-start(bf16[1,64,32,384]{3,2,1,0:T(8,128)(2,1)} %param.28) | copy-start | bytes 4718596
  42.7 50.2 %copy-start.6 = (bf16[384,1536]{1,0:T(8,128)(2,1)S(1)}, bf16[384,1536]{1,0:T(8,128)(2,1)}, u32[]{:S(2)}) copy-start(bf16[384,1536]{1,0:T(8,128)(2,1)} %wqkv_ref.3) | copy-start | bytes 3538948
  42.8 50.2 %copy-start.8 = (bf16[512,384]{1,0:T(8,128)(2,1)S(1)}, bf16[512,384]{1,0:T(8,128)(2,1)}, u32[]{:S(2)}) copy-start(bf16[512,384]{1,0:T(8,128)(2,1)} %wout_ref.3) | copy-start | bytes 1179652
  42.8 50.2 %copy-start.9 = (f32[384]{0:T(512)S(1)}, f32[384]{0:T(512)}, u32[]{:S(2)}) copy-start(f32[384]{0:T(512)} %gain_ref.3) | copy-start | bytes 4612
  42.8 50.2 %copy-start.10 = (f32[512,128]{1,0:T(8,128)S(1)}, f32[512,128]{1,0:T(8,128)}, u32[]{:S(2)}) copy-start(f32[512,128]{1,0:T(8,128)} %constant.31.clone.sin_ref) | copy-start | bytes 786436
  42.8 50.2 %copy-start.11 = (f32[512,128]{1,0:T(8,128)S(1)}, f32[512,128]{1,0:T(8,128)}, u32[]{:S(2)}) copy-start(f32[512,128]{1,0:T(8,128)} %constant.30.clone.cos_ref) | copy-start | bytes 786436

commit v8 on v7

--- a/solution.py
+++ b/solution.py
@@ -434,7 +434,7 @@
                     powers = jnp.exp2(scores - jnp.max(scores, axis=1, keepdims=True))
                     mixed = jnp.dot(
                         powers.astype(BF), values[part, g * GROUP : (g + 1) * GROUP].astype(BF), preferred_element_type=F32)
-                    mixed = mixed / jnp.sum(powers, axis=1, keepdims=True)
+                    mixed = mixed * (1.0 / jnp.sum(powers, axis=1, keepdims=True))
                     joined = mixed[:half]
                     for h in range(1, 4):
                         joined = jnp.where(lane // DH == h, mixed[h * half : (h + 1) * half], joined)

time: 151 us -> 151 us (level)
  no operation moved by 1% of the time
where the time goes in v8:
time: 151 us; the launch traced here: 150 us
  Pallas kernels  139 us (92%)
  local copies, waits for them, and re-layouts  7.58 us (5%)
  other arithmetic  1.79 us (1%)
    pallas_call x1, Pallas kernels, finish(): pl.pallas_call(functools.partial(finish_kernel, seq, songs), out_shape=(j...  55.2 us
    pallas_call x1, Pallas kernels, time_attention(): pl.pallas_call(time_kernel, out_shape=jax.ShapeDtypeStruct(sequence.shape...  50.1 us
    pallas_call x1, Pallas kernels, exchange(): pl.pallas_call(functools.partial(exchange_kernel, seq), grid=(1,), out_sh...  34.2 us
    unnamed x25, local copies, waits for them, and re-layouts  6.05 us

profile of v8, /device:TPU:1, one launch (start us, length us, event | category | flops | bytes accessed | tf_op | source)
XLA Modules:
  0.0 150.3 jit_solution(5473076593284577359)
XLA Ops:
  1.3 0.7 copy.19
  2.0 0.1 reduce-window.9
  2.1 0.1 reduce
  2.2 0.7 fusion
  2.9 0.8 broadcast_in_dim.3.bin_gain_ref
  3.7 0.0 copy-start
  3.7 1.3 copy-done
  4.9 0.0 copy-start.1
  4.9 1.2 copy-done.1
  6.2 0.0 copy-start.2
  6.2 0.9 copy-done.2
  7.1 0.0 copy-start.3
  7.1 0.8 copy-done.3
  7.9 0.0 copy-start.4
  7.9 0.7 copy-done.4
  8.6 0.0 copy-start.7
  8.6 34.2 %shard_map.167 = (bf16[2,32,32,384]{3,2,1,0:T(8,128)(2,1)S(1)}, bf16[2,2048,256]{2,1,0:T(8,128)(2,1)S(1)}, bf16[2,2048,256]{2,1,0:T(8,128)(2,1)S(1)}, bf16[8,128,2048]{2,1,0:T(8,128)(2,1)S(1)}, f32[5,128]{1,0:T(8,128)S(1)}) custom-call(s32[1]{0:T(128)S(6)} %copy.21.length_ref, s32[3,32]{1,0:T(4,128)S(1)} %pad_add_fusion.meta_ref, ...), custom_call_target="tpu_custom_call" | custom-call | flops 4000000000 | bytes 10000000 | tf_op jit(solution)/shard_map/pallas_call | solution.py:254
  42.7 0.0 copy-done.7
  42.7 0.0 copy-start.5
  42.7 0.0 copy-start.6
  42.8 0.0 copy-start.8
  42.8 0.0 copy-start.9
  42.8 0.0 copy-start.10
  42.8 0.0 copy-start.11
  42.8 50.1 %shard_map.168.timed_ref = bf16[2,32,32,384]{3,2,1,0:T(8,128)(2,1)S(1)} custom-call(s32[1]{0:T(128)S(6)} %copy.21.length_ref, f32[5,128]{1,0:T(8,128)S(1)} %get-tuple-element.9.most_ref, bf16[2,32,32,384]{3,2,1,0:T(8,128)(2,1)S(1)} %get-tuple-element.10.x_ref, bf16[512,384]{1,0:T(8,128)(2,1)S(1)} %copy-done.7, ...), custom_call_target="tpu_custom_call" | custom-call | flops 40000000000 | bytes 8000000 | tf_op jit(solution)/shard_map/pallas_call | solution.py:326
  92.9 0.0 copy-done.5
  93.0 0.0 copy-done.6
  93.0 0.0 copy-done.8
  93.0 0.0 copy-done.9
  93.0 0.0 copy-done.10
  93.0 0.0 copy-done.11
  93.0 55.2 %shard_map.169 = (bf16[2048,384]{1,0:T(8,128)(2,1)S(1)}, bf16[512,384]{1,0:T(8,128)(2,1)S(1)}) custom-call(s32[1]{0:T(128)S(6)} %copy.21.length_ref, bf16[2,32,32,384]{3,2,1,0:T(8,128)(2,1)S(1)} %shard_map.168.timed_ref, f32[384]{0:T(512)S(1)} %copy-done.9, bf16[384,1536]{1,0:T(8,128)(2,1)S(1)} %copy-done.6, bf16[512,384]{1,0:T(8,128)(2,1)S(1)} %copy-done.8, ...), custom_call_target="tpu_custom_call" | custom-call | flops 10000000000 | bytes 7000000 | tf_op jit(solution)/shard_map/pallas_call | solution.py:535
  148.2 0.9 convert_element_type.3
  149.1 1.1 copy.22
  (1 shorter events, 0.0 us)
Async XLA Ops:
  3.7 1.3 copy-start
  4.9 1.2 copy-start.1
  6.2 0.9 copy-start.2
  7.1 0.8 copy-start.3
  7.9 0.7 copy-start.4
  8.6 34.2 %copy-start.7 = (bf16[512,384]{1,0:T(8,128)(2,1)S(1)}, bf16[512,384]{1,0:T(8,128)(2,1)}, u32[]{:S(2)}) copy-start(bf16[512,384]{1,0:T(8,128)(2,1)} %wout_ref.2) | copy-start | bytes 1179652
  42.7 50.2 %copy-start.5 = (bf16[1,64,32,384]{3,2,1,0:T(8,128)(2,1)S(1)}, bf16[1,64,32,384]{3,2,1,0:T(8,128)(2,1)}, u32[]{:S(2)}) copy-start(bf16[1,64,32,384]{3,2,1,0:T(8,128)(2,1)} %param.28) | copy-start | bytes 4718596
  42.7 50.2 %copy-start.6 = (bf16[384,1536]{1,0:T(8,128)(2,1)S(1)}, bf16[384,1536]{1,0:T(8,128)(2,1)}, u32[]{:S(2)}) copy-start(bf16[384,1536]{1,0:T(8,128)(2,1)} %wqkv_ref.3) | copy-start | bytes 3538948
  42.8 50.2 %copy-start.8 = (bf16[512,384]{1,0:T(8,128)(2,1)S(1)}, bf16[512,384]{1,0:T(8,128)(2,1)}, u32[]{:S(2)}) copy-start(bf16[512,384]{1,0:T(8,128)(2,1)} %wout_ref.3) | copy-start | bytes 1179652
  42.8 50.2 %copy-start.9 = (f32[384]{0:T(512)S(1)}, f32[384]{0:T(512)}, u32[]{:S(2)}) copy-start(f32[384]{0:T(512)} %gain_ref.3) | copy-start | bytes 4612
  42.8 50.2 %copy-start.10 = (f32[512,128]{1,0:T(8,128)S(1)}, f32[512,128]{1,0:T(8,128)}, u32[]{:S(2)}) copy-start(f32[512,128]{1,0:T(8,128)} %constant.31.clone.sin_ref) | copy-start | bytes 786436
  42.8 50.2 %copy-start.11 = (f32[512,128]{1,0:T(8,128)S(1)}, f32[512,128]{1,0:T(8,128)}, u32[]{:S(2)}) copy-start(f32[512,128]{1,0:T(8,128)} %constant.30.clone.cos_ref) | copy-start | bytes 786436
